TPU v7x, 128 devices: a whole 4x4x4 slice. The times are simulated.
128 devices in a mesh: seq: 4 (over x), fsdp: 32 (over y, z, core).
Axes of the slice: x: 4, y: 4, z: 4, core: 2. Of those that a mesh axis runs over, the one named last changes fastest.
Arguments:
- tokens: bfloat16 [32, 2048, 768], P('fsdp', 'seq'), may hold values from -6 to 6
- cotangent: bfloat16 [32, 2048, 768], P('fsdp', 'seq'), may hold values from -6 to 6
- lengths: int32 [32], P('fsdp'), may hold values from 1537 to 2048, as said below
- routes: int32 [32, 2048, 2], P('fsdp', 'seq'), may hold values from 0 to 7, all different within a row; in each aligned block of 512 rows (0 to 511, 512 to 1023, ..., all dimensions but the last counted through in order) at most 192 rows name the same one
- prior_routes: int32 [32, 2048, 2], P('fsdp', 'seq'), may hold values from 0 to 7
- gain_attend: float32 [768], P('fsdp'), may hold values from 0.5 to 1.5
- attend_in: float32 [768, 2304], P('fsdp'), may hold values from -0.3125 to 0.3125
- attend_out: float32 [768, 768], P('fsdp'), may hold values from -1.25 to 1.25
- gain_mix: float32 [768], P('fsdp'), may hold values from 0.5 to 1.5
- router: float32 [768, 8], P('fsdp'), may hold values from -0.21875 to 0.21875
- route_table: float32 [8, 8], replicated, may hold values from -2 to 2
- const_mix: float32 [768, 4], P('fsdp'), may hold values from -0.21875 to 0.21875
- const_vector: float32 [768, 2], P('fsdp'), may hold values from -6 to 6
- expert_in: float32 [4, 768, 4096], P(None, 'fsdp'), may hold values from -0.21875 to 0.21875
- expert_out: float32 [4, 2048, 768], P(None, 'fsdp'), may hold values from -0.125 to 0.125
Outputs:
- mixed_out: bfloat16 [32, 2048, 768], P('fsdp', 'seq')
- grad_tokens: bfloat16 [32, 2048, 768], P('fsdp', 'seq')
- grad_gain_attend: float32 [768], P('fsdp')
- grad_attend_in: float32 [768, 2304], P('fsdp')
- grad_attend_out: float32 [768, 768], P('fsdp')
- grad_gain_mix: float32 [768], P('fsdp')
- grad_router: float32 [768, 8], P('fsdp')
- grad_route_table: float32 [8, 8], replicated
- grad_const_mix: float32 [768, 4], P('fsdp')
- grad_const_vector: float32 [768, 2], P('fsdp')
- grad_expert_in: float32 [4, 768, 4096], P(None, 'fsdp')
- grad_expert_out: float32 [4, 2048, 768], P(None, 'fsdp')
Inputs may be any that keep to these rules, and one draw needn't show every extreme that they name: `lengths`: every length exceeds 3 * 512; in every draw some sequence has length exactly 2048. `routes`: the two numbers of a row differ; numbers below 4 name feed-forward experts, 4 the zero expert, 5 the copy expert, the rest constant experts; in the 512 rows of one device no number stands in more than 192 rows, and in every draw some number stands in exactly 192 rows of some device.
All inputs are finite; a program needn't handle non-finite values.
Results may differ from a plain program's by a relative error of at most 0.023.
The roundings to bfloat16 on the way count: a program that leaves them out, or rounds other values in their place, can miss the bound.
Values may be sent and summed in bfloat16 or wider, within the bound.
No kernel may reach another device: no remote copies, remote signals or barrier semaphores. Data moves between devices by JAX's collectives and lax.ppermute only.
A program may use at most 320 MiB of HBM per device.

v0:
```python
import functools
import math

import jax
import jax.numpy as jnp
from jax import lax
from jax.experimental import pallas as pl
from jax.experimental.pallas import tpu as pltpu
from jax.sharding import Mesh
from jax.sharding import PartitionSpec as P

HEADS = 12
HEAD_DIM = 64
HALF = HEAD_DIM // 2
NC = 2
EF = 4
NE = 8
CAP = 192
LANES = 128
SEQS = 4
SIDE = 4
YZ = ("fy", "fz")
FSDP = ("fy", "fz", "core")
ANY = pl.BlockSpec(memory_space=pl.ANY)
EPS = 1e-06
SCALE = HEAD_DIM ** (-0.5)
LOWEST = -1e30
F32 = jnp.float32
BF16 = jnp.bfloat16
VMEM = pl.BlockSpec(memory_space=pltpu.VMEM)
SMEM = pl.BlockSpec(memory_space=pltpu.SMEM)


def mm(a, b, ca=1, cb=0):
    return lax.dot_general(a, b, (((ca,), (cb,)), ((), ())), preferred_element_type=F32)


def params(mib, grid=None):
    if grid is None:
        return pltpu.CompilerParams(vmem_limit_bytes=mib << 20)
    return pltpu.CompilerParams(
        vmem_limit_bytes=mib << 20, dimension_semantics=("arbitrary",) * grid
    )


def sds(shape, dtype):
    return jax.ShapeDtypeStruct(shape, dtype)


def took(us):
    return pl.CostEstimate(flops=int(us * 1.1e9), bytes_accessed=1 << 16, transcendentals=0)


def far(x):
    return pltpu.with_memory_space_constraint(x, pltpu.HBM)


def hbm(shape, dtype):
    return pltpu.HBM(shape, dtype)


def whole(x):
    return pl.BlockSpec(x.shape, lambda i: (0,) * len(x.shape))


def come(*arrays):
    return [(x, whole(x)) for x in arrays]


def one_step(body, us, meta, inputs, results, scratch=(), before=(), mib=14, near=0):
    inputs = [x if isinstance(x, tuple) else (far(x), whole(x)) for x in inputs]
    shapes = [(sds if k < near else hbm)(*r) for k, r in enumerate(results)]
    return pl.pallas_call(
        body,
        grid=(1,),
        in_specs=[SMEM] + [spec for _, spec in inputs] + [ANY] * len(before),
        out_specs=[VMEM if k < near else whole(r) for k, r in enumerate(shapes)],
        out_shape=shapes,
        scratch_shapes=list(scratch),
        compiler_params=params(mib, 1),
        cost_estimate=took(us),
        name=getattr(body, "func", body).__name__.removesuffix("_kernel"),
    )(meta, *[x for x, _ in inputs], *map(far, before))


def shift(x, by):
    count = lax.axis_size("seq")
    return lax.ppermute(x, "seq", [(i, (i + by) % count) for i in range(count)])


def trade(x, by, axis="seq"):
    count = lax.axis_size(axis)
    return lax.ppermute(x, axis, [(i, i ^ by) for i in range(count)]) if by else x


def trades(pieces, axis="seq"):
    return [trade(piece, k, axis) for k, piece in enumerate(pieces)]


def around(meta, by):
    return lax.bitwise_xor(meta[1], by)


def swap(x, axis):
    return lax.all_to_all(x, axis, split_axis=0, concat_axis=0, tiled=True)


def two_parts(x):
    high = x.astype(BF16)
    return high, (x - high.astype(F32)).astype(BF16)


def lane_of(shape):
    return lax.broadcasted_iota(jnp.int32, shape, 1)


def pick(values, lanes, lane):
    return jnp.sum(jnp.where(lanes == lane, values, 0.0), axis=1, keepdims=True)


def tiles_moved(x, rows, columns):
    tiles = [
        x[r : r + 8, c : c + LANES]
        for r in range(0, x.shape[0], 8)
        for c in range(0, x.shape[1], LANES)
    ]
    count = columns // LANES
    lines = [jnp.concatenate(tiles[k : k + count], axis=1) for k in range(0, len(tiles), count)]
    return jnp.concatenate(lines, axis=0)


def pack_kernel(
    meta,
    attend_in,
    gain_a,
    attend_out,
    router,
    const_mix,
    const_vector,
    gain_m,
    w_in,
    w_out,
    first,
    second,
    back,
    in_mine,
    out_mine,
    sems,
):
    shard, model = attend_out.shape
    group = model // SEQS
    me = meta[1]
    in_copy = pltpu.make_async_copy(w_in.at[me], in_mine, sems.at[0])
    out_copy = pltpu.make_async_copy(w_out.at[me], out_mine, sems.at[1])
    in_copy.start()
    out_copy.start()
    used = NE + 3 * NC + 2
    rows = [router[...], const_mix[...], const_vector[...], gain_m[...], gain_a[...]]
    rows = jnp.concatenate([*rows, jnp.zeros((LANES - used, shard), F32)], axis=0)
    rows = jnp.concatenate([rows, jnp.zeros((LANES, LANES - shard), F32)], axis=1)
    small = jnp.transpose(rows)[:shard]
    lanes = lane_of(small.shape)

    pieces, own = [], []
    for k in range(3):
        parts = [
            attend_in[:, k * model + g * group : k * model + (g + 1) * group] for g in range(SEQS)
        ]
        mine = parts[0]
        for g in range(1, SEQS):
            mine = jnp.where(me == g, parts[g], mine)
        pieces.append(parts)
        own.append(mine)
    gain = pltpu.roll(small, LANES - (used - 1), 1)[:, :64]
    gain = jnp.where(lane_of(gain.shape) == 0, gain, 0.0)
    row = jnp.concatenate([*own, gain], axis=1).astype(BF16)
    first[...] = jnp.broadcast_to(row[None], first.shape)
    back[...] = jnp.concatenate(
        [pieces[k][g] for g in range(SEQS) for k in range(3)], axis=1
    ).astype(BF16)

    small = jnp.where(lanes < used - 1, small, 0.0)
    second[:, :model] = attend_out[...].astype(BF16)
    second[:, model : model + 2 * LANES] = jnp.concatenate(
        [small, jnp.zeros_like(small)], axis=1
    ).astype(BF16)
    at = model + 2 * LANES
    wide = in_mine.shape[1]
    in_copy.wait()
    second[:, at : at + wide] = in_mine[...].astype(BF16)
    out_copy.wait()
    at += wide
    second[:, at:] = tiles_moved(out_mine[...], shard, second.shape[1] - at).astype(BF16)


def pack(meta, attend_in, gain_a, attend_out, router, const_mix, const_vector, gain_m, w_in, w_out, count):
    shard, model = attend_out.shape
    wide = model + 2 * LANES + w_in.shape[2] + w_out.shape[1] * model // shard
    plain = (attend_in, gain_a, attend_out, router, const_mix, const_vector, gain_m)
    results = [
        sds((count, shard, 3 * model // SEQS + 64), BF16),
        sds((shard, wide), BF16),
        sds(attend_in.shape, BF16),
    ]
    return pl.pallas_call(
        pack_kernel,
        grid=(1,),
        in_specs=[SMEM] + [whole(x) for x in plain] + [ANY] * 2,
        out_specs=[whole(x) for x in results],
        out_shape=results,
        scratch_shapes=[
            pltpu.VMEM(w_in.shape[1:], F32),
            pltpu.VMEM(w_out.shape[1:], F32),
            pltpu.SemaphoreType.DMA((2,)),
        ],
        compiler_params=params(14, 1),
        cost_estimate=took(2),
        name="pack",
    )(meta, *map(far, (*plain, w_in, w_out)))


def plan_kernel(meta, routes, prior, table, cotangent, slots, grad, logits, counts, *sent):
    rows = routes.shape[1]
    width = cotangent.shape[1]
    ids = lax.broadcasted_iota(jnp.int32, (NE, rows), 0)
    hits = (ids == routes[0:1]) | (ids == routes[1:2])
    before = lax.broadcasted_iota(jnp.int32, (rows, rows), 0)
    before = before < lax.broadcasted_iota(jnp.int32, (rows, rows), 1)
    ranks = mm(jnp.where(hits, 1.0, 0.0).astype(BF16), jnp.where(before, 1.0, 0.0).astype(BF16))
    ranks = jnp.where(hits, ranks.astype(jnp.int32), -1)
    lines = lax.broadcasted_iota(jnp.int32, (CAP, rows), 0)
    for e in range(EF):
        slots[e] = jnp.where(lines == ranks[e : e + 1], 1.0, 0.0).astype(BF16)
    spots = lax.broadcasted_iota(jnp.int32, (rows, width), 0) + meta[1] * rows
    live = jnp.where(spots < meta[0], cotangent[...].astype(F32), 0.0).astype(BF16)
    grad[...] = live
    for s in range(SEQS):
        sent[s][...] = mm(slots[around(meta, s)], live).astype(BF16)
    count = (ids == prior[0:1]).astype(F32) + (ids == prior[1:2]).astype(F32)
    named = routes[...].astype(F32)
    flat = [count, named, jnp.zeros((LANES - NE - 2, rows), F32)]
    flat = jnp.transpose(jnp.concatenate(flat, axis=0))
    lanes = lane_of(flat.shape)
    count = jnp.where(lanes < NE, flat, 0.0).astype(BF16)
    counts[...] = count
    full = jnp.concatenate([table[...], jnp.zeros((NE, LANES - NE), F32)], axis=1)
    full = jnp.concatenate([full, jnp.zeros((LANES - NE, LANES), F32)], axis=0)
    total = jnp.zeros(flat.shape, F32)
    for _ in range(3):
        part = full.astype(BF16)
        full = full - part.astype(F32)
        total += mm(count, part)
    named = pltpu.roll(flat, NE, 1)
    logits[...] = jnp.where((lanes >= 2 * NE) & (lanes < 2 * NE + 2), named, total)


def plan(meta, routes, prior, table, cotangent):
    rows, model = cotangent.shape
    results = [
        ((EF, CAP, rows), BF16),
        ((rows, model), BF16),
        ((rows, LANES), F32),
        ((rows, LANES), BF16),
    ] + [((CAP, model), BF16)] * SEQS
    return one_step(plan_kernel, 1, meta, [routes, prior, table, cotangent], results, mib=24)


def project_kernel(meta, *refs):
    sources, (weight, gain, cosine, sine, qkv, normed) = refs[:5], refs[5:]
    width = qkv.shape[1]
    part = width // 3
    for to, which in ((0, (0,)), (3, (1,)), (1, (2,)), (2, (3, 4))):
        place = lax.rem(meta[1] + to, SEQS)
        done = 0
        for source in [sources[k] for k in which]:
            at = slice(done, done + source.shape[0])
            done = at.stop
            v = source[...].astype(F32)
            n = v * lax.rsqrt(jnp.mean(v * v, axis=-1, keepdims=True) + EPS) * gain[...]
            normed[place, at] = n.astype(BF16)
        flat = jnp.transpose(mm(normed[place], weight[:, :width]))
        c, s = cosine[place], sine[place]
        for which in range(2):
            factor = SCALE if which == 0 else 1.0
            for at in range(which * part, (which + 1) * part, HEAD_DIM):
                a, b = flat[at : at + HALF], flat[at + HALF : at + HEAD_DIM]
                qkv[place, at : at + HALF] = ((a * c - b * s) * factor).astype(BF16)
                qkv[place, at + HALF : at + HEAD_DIM] = ((b * c + a * s) * factor).astype(BF16)
        qkv[place, 2 * part :] = flat[2 * part :].astype(BF16)


def project(meta, sources, weight, gain, cosine, sine, width):
    rows, model = sources[0].shape
    results = [((SEQS, width, rows), BF16), ((SEQS, rows, model), BF16)]
    inputs = [*come(*sources, weight, gain), cosine, sine]
    return one_step(project_kernel, 100, meta, inputs, results, mib=20, near=1)


def mask_diagonal(scores, start, length):
    keys = lax.broadcasted_iota(jnp.int32, scores.shape, 0)
    queries = lax.broadcasted_iota(jnp.int32, scores.shape, 1)
    return jnp.where((keys <= queries) & (keys + start < length), scores, LOWEST)


def attend_kernel(meta, qkv, *refs):
    out, lse, top, total, acc = refs[-5:]
    rows = qkv.shape[2]
    part = qkv.shape[1] // 3
    heads = part // HEAD_DIM
    length = meta[0]
    spans = [
        [slice(k * part + h * HEAD_DIM, k * part + (h + 1) * HEAD_DIM) for k in range(3)]
        for h in range(heads)
    ]
    for block in range(SEQS):
        for h, (at, k_at, v_at) in enumerate(spans):
            scores = mm(qkv[block, k_at], qkv[block, at], 0, 0)
            scores = mask_diagonal(scores, block * rows, length)
            peak = jnp.max(scores, axis=0, keepdims=True)
            e = jnp.exp(scores - peak)
            top[h : h + 1] = peak
            total[h : h + 1] = jnp.sum(e, axis=0, keepdims=True)
            acc[at] = mm(qkv[block, v_at], e.astype(BF16))

        def step(j, carry, block=block):
            for h, (at, k_at, v_at) in enumerate(spans):
                scores = mm(qkv[j, k_at], qkv[block, at], 0, 0)
                last = top[h : h + 1]
                peak = jnp.maximum(last, jnp.max(scores, axis=0, keepdims=True))
                e = jnp.exp(scores - peak)
                fade = jnp.exp(last - peak)
                top[h : h + 1] = peak
                total[h : h + 1] = total[h : h + 1] * fade + jnp.sum(e, axis=0, keepdims=True)
                acc[at] = acc[at] * fade + mm(qkv[j, v_at], e.astype(BF16))
            return carry

        lax.fori_loop(0, block, step, 0)
        for h, (at, _, _) in enumerate(spans):
            out[block, at] = (acc[at] / total[h : h + 1]).astype(BF16)
            lse[block, h : h + 1] = top[h : h + 1] + jnp.log(total[h : h + 1])


def attend(meta, qkv):
    _, width, rows = qkv.shape
    part = width // 3
    results = [((SEQS, part, rows), BF16), ((SEQS, 8, rows), F32)]
    scratch = [
        pltpu.VMEM((8, rows), F32),
        pltpu.VMEM((8, rows), F32),
        pltpu.VMEM((part, rows), F32),
    ]
    inputs = [(qkv, VMEM)]
    return one_step(attend_kernel, 0.1, meta, inputs, results, scratch, mib=20)


def attend_back_kernel(meta, qkv, *refs):
    dout, out, lse, cosine, sine, normed = refs[:6]
    dproj = refs[-8 - SEQS : -8]
    kept, gone, dq, dk, dv, dots, normed_held, sem = refs[-8:]
    blocks, width, rows = qkv.shape
    part = width // 3
    heads = part // HEAD_DIM
    length = meta[0]

    normed_copy = pltpu.make_async_copy(normed, normed_held, sem)
    normed_copy.start()

    def pair(q, k, diagonal):
        for h in range(heads):
            at = slice(h * HEAD_DIM, (h + 1) * HEAD_DIM)
            k_at = slice(part + h * HEAD_DIM, part + (h + 1) * HEAD_DIM)
            v_at = slice(2 * part + h * HEAD_DIM, 2 * part + (h + 1) * HEAD_DIM)
            qh, kh, vh, doh = qkv[q, at], qkv[k, k_at], qkv[k, v_at], dout[q, at]
            scores = mm(kh, qh, 0, 0)
            if diagonal:
                scores = mask_diagonal(scores, k * rows, length)
            probs = jnp.exp(scores - lse[q, h : h + 1])
            dprobs = mm(vh, doh, 0, 0)
            low = probs.astype(BF16)
            dscores = (probs * (dprobs - dots[q, h : h + 1])).astype(BF16)
            if diagonal:
                dv[k, at] = mm(doh, low, 1, 1)
                dk[k, at] = mm(qh, dscores, 1, 1)
                dq[q, at] = mm(kh, dscores)
            else:
                dv[k, at] += mm(doh, low, 1, 1)
                dk[k, at] += mm(qh, dscores, 1, 1)
                dq[q, at] += mm(kh, dscores)

    for b in range(SEQS):
        for h in range(heads):
            at = slice(h * HEAD_DIM, (h + 1) * HEAD_DIM)
            both = dout[b, at].astype(F32) * out[b, at].astype(F32)
            dots[b, h : h + 1] = jnp.sum(both, axis=0, keepdims=True)

    def diagonal(b, carry):
        pair(b, b, True)
        return carry

    def below(q, carry):
        def one(k, inner):
            pair(q, k, False)
            return inner

        return lax.fori_loop(0, q, one, carry)

    lax.fori_loop(0, blocks, diagonal, 0)
    lax.fori_loop(1, blocks, below, 0)
    for to in range(SEQS):
        b = around(meta, to)
        c, s = cosine[b], sine[b]
        for which, held in ((0, dq), (1, dk)):
            factor = SCALE if which == 0 else 1.0
            for h in range(heads):
                at = h * HEAD_DIM
                rounded = (held[b, at : at + HEAD_DIM] * factor).astype(BF16).astype(F32)
                x, y = rounded[:HALF], rounded[HALF:]
                at += which * part
                dproj[to][at : at + HALF] = (x * c + y * s).astype(BF16)
                dproj[to][at + HALF : at + HEAD_DIM] = (y * c - x * s).astype(BF16)
        dproj[to][2 * part :] = dv[b].astype(BF16)

    normed_copy.wait()
    total = mm(dproj[0][...], normed_held[around(meta, 0)])
    for to in range(1, SEQS):
        total += mm(dproj[to][...], normed_held[around(meta, to)])
    pairs, shard, _ = kept.shape
    total = jnp.transpose(total).reshape(pairs, 2 * shard, width)
    even = meta[2] == 0
    kept[...] = jnp.where(even, total[:, :shard], total[:, shard:]).astype(BF16)
    gone[...] = jnp.where(even, total[:, shard:], total[:, :shard]).astype(BF16)


def attend_back(meta, before, qkv, dout, out, lse, cosine, sine, normed, count):
    blocks, width, rows = qkv.shape
    part = width // 3
    model = normed.shape[2]
    scratch = [pltpu.VMEM((blocks, part, rows), F32)] * 3
    scratch += [pltpu.VMEM((blocks, 8, rows), F32), pltpu.VMEM(normed.shape, BF16)]
    scratch += [pltpu.SemaphoreType.DMA]
    inputs = [*come(qkv, dout), out, lse, cosine, sine, (far(normed), ANY)]
    results = [((width, rows), BF16)] * SEQS
    results += [((count // 2, model // count, width), BF16)] * 2
    return one_step(attend_back_kernel, 100, meta, inputs, results, scratch, before, 48)


def route_kernel(meta, att, out_w, small_w, tok, prior, slots, *refs):
    sent = refs[-4 - SEQS : -4]
    resid, moe, stats, vectors = refs[-4:]
    res = tok[...].astype(F32) + mm(att[...], out_w[...], 0, 0)
    flipped = jnp.transpose(small_w[...].astype(F32))
    vectors[...] = flipped[NE + 2 * NC : NE + 2 * NC + 8]
    gain = flipped[NE + 3 * NC : NE + 3 * NC + 1]
    resid[...] = res
    normed = res * lax.rsqrt(jnp.mean(res * res, axis=-1, keepdims=True) + EPS) * gain
    low = normed.astype(BF16)
    moe[...] = low
    small = mm(low, small_w[...])
    small = jnp.where(lane_of(small.shape) < NE + 2 * NC, small, 0.0)
    lanes = lane_of(small.shape)
    known = prior[...]
    logits = small + jnp.where(lanes < NE, known, 0.0)
    named = lanes.astype(F32)
    hit0 = named == known[:, 2 * NE : 2 * NE + 1]
    hit1 = named == known[:, 2 * NE + 1 : 2 * NE + 2]
    chosen0 = jnp.sum(jnp.where(hit0, logits, 0.0), axis=1, keepdims=True)
    chosen1 = jnp.sum(jnp.where(hit1, logits, 0.0), axis=1, keepdims=True)
    gate0 = 1.0 / (1.0 + jnp.exp(chosen1 - chosen0))
    gate1 = 1.0 / (1.0 + jnp.exp(chosen0 - chosen1))
    share = jnp.where(hit0, gate0, 0.0) + jnp.where(hit1, gate1, 0.0)
    partner = jnp.where(lanes % 2 == 0, pltpu.roll(small, LANES - 1, 1), pltpu.roll(small, 1, 1))
    mix = 1.0 / (1.0 + jnp.exp(partner - small))
    mixing = (lanes >= NE) & (lanes < NE + 2 * NC)
    stats[...] = share + jnp.where(mixing, mix, 0.0)
    high, rest = two_parts(share)
    parts = (high.astype(F32) + pltpu.roll(rest.astype(F32), NE, 1)).astype(BF16)
    model = low.shape[1]
    for s in range(SEQS):
        chosen = slots[around(meta, s)]
        sent[s][:, :model] = mm(chosen, low).astype(BF16)
        sent[s][:, model:] = mm(chosen, parts).astype(BF16)


def weight_blocks(weights):
    model = weights.shape[0]
    return [
        (far(weights), pl.BlockSpec((model, model), lambda i: (0, 0))),
        (far(weights), pl.BlockSpec((model, LANES), lambda i: (0, model // LANES))),
    ]


def route(meta, att, weights, tok, prior, slots, *before):
    rows, model = tok.shape
    results = [((CAP, model + LANES), BF16)] * SEQS + [
        ((rows, model), F32),
        ((rows, model), BF16),
        ((rows, LANES), F32),
        ((8, model), F32),
    ]
    inputs = [*come(att), *weight_blocks(weights), tok, prior, slots]
    return one_step(route_kernel, 100, meta, inputs, results, (), before, 24)


def local_part_kernel(meta, resid, stats, grad, vectors, partial, small, grad_vec):
    gain = vectors[NC : NC + 1]
    res, g = resid[...], grad[...].astype(F32)
    normed = res * lax.rsqrt(jnp.mean(res * res, axis=-1, keepdims=True) + EPS) * gain
    held = stats[...]
    lanes = lane_of(held.shape)
    copy_dot = jnp.sum(g * normed, axis=1, keepdims=True)
    factor = pick(held, lanes, EF + 1)
    result = jnp.where(lanes == EF + 1, factor * copy_dot, 0.0)
    ways = jnp.zeros_like(held)
    added = jnp.zeros_like(res)
    for j in range(NC):
        row = vectors[j : j + 1]
        weight = pick(held, lanes, EF + 2 + j)
        first = pick(held, lanes, NE + 2 * j)
        second = pick(held, lanes, NE + 2 * j + 1)
        vec_dot = jnp.sum(g * row, axis=1, keepdims=True)
        mean = first * copy_dot + second * vec_dot
        result += jnp.where(lanes == EF + 2 + j, weight * mean, 0.0)
        result += jnp.where(lanes == NE + 2 * j, weight * first * (copy_dot - mean), 0.0)
        result += jnp.where(lanes == NE + 2 * j + 1, weight * second * (vec_dot - mean), 0.0)
        ways += jnp.where(lanes == j, weight * second, 0.0)
        added += (weight * second) * row
        factor += weight * first
    small[...] = result + jnp.where(lanes == NE + 2 * NC, factor, 0.0)
    partial[...] = res + factor * normed + added
    high, rest = two_parts(ways)
    grad_vec[...] = mm(grad[...], high, 0, 0) + mm(grad[...], rest, 0, 0)


def local_part(meta, resid, stats, grad, vectors):
    rows, model = resid.shape
    results = [((rows, model), F32), ((rows, LANES), F32), ((model, LANES), F32)]
    return one_step(local_part_kernel, 0.1, meta, [resid, stats, grad, vectors], results, mib=16)


def expert_kernel(meta, *refs):
    sent, grads = refs[:SEQS], refs[SEQS : 2 * SEQS]
    gate_w, up_w, out_w = refs[2 * SEQS + 1 : 2 * SEQS + 4]
    back = refs[2 * SEQS + 4 : 3 * SEQS + 4]
    rows, scaled, gate, hidden, dgate, dup, held, acc, dots = refs[3 * SEQS + 4 :]
    step = pl.program_id(0)
    count, model = rows.shape
    block = gate_w.shape[1]
    me = meta[1]

    @pl.when(step == 0)
    def _():
        for s in range(SEQS):
            at = slice(s * CAP, (s + 1) * CAP)
            rows[at] = sent[s][:, :model]
            held[at] = grads[s][...]
            parts = sent[s][:, model:].astype(F32)
            lanes = lane_of(parts.shape)
            own = (lanes == me) | (lanes == me + NE)
            share = jnp.sum(jnp.where(own, parts, 0.0), axis=1, keepdims=True)
            gate[at] = jnp.broadcast_to(share, (CAP, LANES))
            scaled[at] = (grads[s][...].astype(F32) * share).astype(BF16)
        acc[...] = jnp.zeros_like(acc)
        dots[...] = jnp.zeros_like(dots)

    for at in (slice(0, count // 2), slice(count // 2, count)):
        g = mm(rows[at], gate_w[...])
        u = mm(rows[at], up_w[...])
        v = mm(held[at], out_w[...], 1, 1)
        sig = 1.0 / (1.0 + jnp.exp(-g))
        silu = g * sig
        low = (silu * u).astype(BF16)
        hidden[at] = low
        both = v * low.astype(F32)
        folded = both[:, :LANES]
        for c in range(LANES, block, LANES):
            folded = folded + both[:, c : c + LANES]
        dots[at] += folded
        d = v * gate[at, 0:1]
        du = (d * silu).astype(BF16)
        dg = (d * u * (sig * (1.0 + g * (1.0 - sig)))).astype(BF16)
        dgate[at] = dg
        dup[at] = du
        acc[at] += mm(dg, gate_w[...], 1, 1) + mm(du, up_w[...], 1, 1)

    @pl.when(step == pl.num_programs(0) - 1)
    def _():
        for s in range(SEQS):
            at = slice(s * CAP, (s + 1) * CAP)
            back[s][:, :model] = acc[at].astype(BF16)
            value = jnp.sum(dots[at], axis=1, keepdims=True) * gate[at]
            lanes = lane_of(value.shape)
            high, rest = two_parts(value)
            back[s][:, model:] = (
                jnp.where(lanes == me, high.astype(F32), 0.0)
                + jnp.where(lanes == me + NE, rest.astype(F32), 0.0)
            ).astype(BF16)


def expert(meta, sent, grads, before, weights, w_out, block):
    count, model = SEQS * CAP, grads[0].shape[1]
    inner = w_out.shape[0]
    steps = inner // block
    skip = (model + 2 * LANES) // block
    results = [sds(sent[0].shape, BF16)] * SEQS + [
        sds((count, model), BF16),
        sds((count, model), BF16),
        sds((count, LANES), F32),
    ]
    return pl.pallas_call(
        expert_kernel,
        grid=(steps,),
        in_specs=[SMEM]
        + [whole(x) for x in (*sent, *grads)]
        + [
            ANY,
            pl.BlockSpec((model, block), lambda i: (0, i + skip)),
            pl.BlockSpec((model, block), lambda i: (0, i + skip + steps)),
            pl.BlockSpec((block, model), lambda i: (i, 0)),
        ],
        out_specs=[whole(x) for x in results]
        + [pl.BlockSpec((count, block), lambda i: (0, i))] * 3,
        out_shape=[hbm(r.shape, r.dtype) for r in results] + [hbm((count, inner), BF16)] * 3,
        scratch_shapes=[
            pltpu.VMEM((count, model), BF16),
            pltpu.VMEM((count, model), F32),
            pltpu.VMEM((count, LANES), F32),
        ],
        compiler_params=params(24, 1),
        cost_estimate=took(10),
        name="expert",
    )(meta, *sent, *grads, *map(far, (before, weights, weights, w_out)))


def expert_grads_kernel(
    meta, rows, scaled, gate, hidden, dgate, dup, out_w, before, *refs
):
    in_kept, in_sent, out_kept, out_sent = refs[:4]
    branch, (flipped, acc) = refs[4 : SEQS + 4], refs[SEQS + 4 :]
    step = pl.program_id(0)
    half = pl.num_programs(0) // 2
    even = meta[2] == 0

    def halves(x, kept, sent):
        pairs, shard, wide = kept.shape
        x = x.reshape(pairs, 2 * shard, wide)
        first, second = x[:, :shard], x[:, shard:]
        kept[...] = jnp.where(even, first, second).astype(BF16)
        sent[...] = jnp.where(even, second, first).astype(BF16)

    @pl.when(step == 0)
    def _():
        for s in range(SEQS):
            flipped[:, s * CAP : (s + 1) * CAP] = jnp.transpose(rows[s * CAP : (s + 1) * CAP])
        acc[...] = jnp.zeros_like(acc)

    @pl.when(step < half)
    def _():
        halves(mm(flipped[...], dgate[...]), in_kept, in_sent)
        halves(mm(hidden[...], scaled[...], 0, 0), out_kept, out_sent)

    @pl.when(step >= half)
    def _():
        halves(mm(flipped[...], dup[...]), in_kept, in_sent)
        acc[...] += mm(hidden[...], out_w[...])

    @pl.when(step == pl.num_programs(0) - 1)
    def _():
        for s in range(SEQS):
            at = slice(s * CAP, (s + 1) * CAP)
            branch[s][...] = (acc[at] * gate[at, 0:1]).astype(BF16)


def expert_grads(meta, rows, scaled, gate, hidden, dgate, dup, w_out, before, block, fsdp):
    count, model = scaled.shape
    inner = w_out.shape[0]
    half = inner // block
    pairs = fsdp // 2
    in_rows, out_rows = model // fsdp, inner // fsdp
    per = block // (2 * out_rows)

    def low(i):
        return jnp.minimum(i, half - 1)

    def high(i):
        return jnp.maximum(i - half, 0)

    in_spec = pl.BlockSpec((pairs, in_rows, block), lambda i: (0, 0, i))
    out_spec = pl.BlockSpec((per, out_rows, model), lambda i: (low(i), 0, 0))
    return pl.pallas_call(
        expert_grads_kernel,
        grid=(2 * half,),
        in_specs=[
            SMEM,
            whole(rows),
            whole(scaled),
            whole(gate),
            pl.BlockSpec((count, block), lambda i: (0, lax.rem(i, half))),
            pl.BlockSpec((count, block), lambda i: (0, low(i))),
            pl.BlockSpec((count, block), lambda i: (0, high(i))),
            pl.BlockSpec((block, model), lambda i: (high(i), 0)),
            ANY,
        ],
        out_specs=[in_spec, in_spec, out_spec, out_spec]
        + [pl.BlockSpec((CAP, model), lambda i: (0, 0))] * SEQS,
        out_shape=[hbm((pairs, in_rows, 2 * inner), BF16)] * 2
        + [hbm((pairs, out_rows, model), BF16)] * 2
        + [hbm((CAP, model), BF16)] * SEQS,
        scratch_shapes=[pltpu.VMEM((model, count), BF16), pltpu.VMEM((count, model), F32)],
        compiler_params=params(24, 1),
        cost_estimate=took(100),
        name="expert_grads",
    )(meta, *map(far, (rows, scaled, gate, hidden, dgate, dup, w_out, before)))


def split_again(small):
    lanes = lane_of(small.shape)
    table = small + pltpu.roll(small, LANES - NE, 1)
    high = table.astype(BF16).astype(F32)
    rest = pltpu.roll(table - high, NE, 1)
    at = lanes // NE
    return jnp.where(at == 2, high, jnp.where(at == 3, rest, small))


def add_cores_kernel(in_a, in_b, out_a, out_b, *refs):
    shard, wide = in_a.shape[1:]
    for k in range(in_a.shape[0]):
        both = refs[-1].at[k]
        both[:, :wide] = (in_a[k].astype(F32) + in_b[k].astype(F32)).astype(BF16)
        more = out_a[k].astype(F32) + out_b[k].astype(F32)
        both[:, wide:] = tiles_moved(more, shard, both.shape[1] - wide).astype(BF16)


def add_cores(parts, *before):
    pairs, shard, wide = parts[0].shape
    more = parts[2].shape[1] * parts[2].shape[2] // shard

    def some(shape):
        return pl.BlockSpec((SIDE, *shape), lambda i: (i, 0, 0))

    return pl.pallas_call(
        add_cores_kernel,
        grid=(pairs // SIDE,),
        in_specs=[some(x.shape[1:]) for x in parts] + [ANY] * len(before),
        out_specs=some((shard, wide + more)),
        out_shape=hbm((pairs, shard, wide + more), BF16),
        compiler_params=params(24, 1),
        cost_estimate=took(100),
        name="add_cores",
    )(*[x if k % 2 else far(x) for k, x in enumerate(parts)], *map(far, before))


def add_dense_kernel(meta, dense_a, dense_b, heads_a, heads_b, out):
    pairs, shard, wide = dense_a.shape
    width, model = heads_a.shape[2], wide - LANES
    for k in range(pairs):
        total = dense_a[k].astype(F32) + dense_b[k].astype(F32)
        out[k, :, :model] = total[:, :model].astype(BF16)
        out[k, :, model:wide] = split_again(total[:, model:]).astype(BF16)
        heads = heads_a[k].astype(F32) + heads_b[k].astype(F32)
        rest = jnp.zeros((shard, out.shape[2] - wide - width), F32)
        out[k, :, wide:] = jnp.concatenate([heads, rest], axis=1).astype(BF16)


def add_dense(meta, kept, come_dense, heads, come_heads):
    pairs, shard, wide = kept.shape
    results = [((pairs, shard, -(-(wide + heads.shape[2]) // LANES) * LANES), BF16)]
    inputs = [kept, *come(come_dense), heads, *come(come_heads)]
    return one_step(add_dense_kernel, 0.1, meta, inputs, results, mib=24)[0]


def add_pieces_kernel(meta, pieces, *refs):
    total = pieces[0].astype(F32)
    for k in range(1, pieces.shape[0]):
        total += pieces[k].astype(F32)
    model = pieces.shape[0] * pieces.shape[1] * 2
    small = split_again(total[:, model : model + LANES])
    refs[-1][:, :model] = total[:, :model].astype(BF16)
    refs[-1][:, model : model + LANES] = small.astype(BF16)
    refs[-1][:, model + LANES :] = total[:, model + LANES :].astype(BF16)


def add_pieces(meta, pieces, *before):
    results = [(pieces.shape[1:], BF16)]
    return one_step(add_pieces_kernel, 0.1, meta, come(pieces), results, (), before, 24)[0]


def mixed_kernel(meta, partial, slots, *refs):
    result = partial[...]
    for s in range(SEQS):
        result += mm(slots[around(meta, s)], refs[s][...], 0, 0)
    refs[-1][...] = result.astype(BF16)


def mixed(meta, partial, slots, branch, *before):
    results = [(partial.shape, BF16)]
    (out,) = one_step(mixed_kernel, 0.1, meta, [partial, slots, *come(*branch)], results, (), before)
    return out


def unroute_kernel(meta, *refs):
    back = refs[:SEQS]
    out_w, small_w, slots, resid, small, stats, grad, vectors = refs[SEQS : SEQS + 8]
    att, moe, grad_vec, prior_hits = refs[SEQS + 8 : SEQS + 12]
    datt = refs[-4]
    dres, kept, sent = refs[-3:]
    pairs, shard, _ = kept.shape
    even = meta[2] == 0
    gain = vectors[NC : NC + 1]
    rows, model = resid.shape
    held, local = stats[...], small[...]
    lanes = lane_of(held.shape)
    dn = jnp.zeros((rows, model), F32)
    tail = jnp.zeros((rows, LANES), F32)
    for s in range(SEQS):
        chosen = slots[around(meta, s)]
        dn += mm(chosen, back[s][:, :model], 0, 0)
        tail += mm(chosen, back[s][:, model:], 0, 0)
    ffn = tail + pltpu.roll(tail, LANES - NE, 1)
    dots = jnp.where(lanes < EF, ffn, jnp.where(lanes < NE, local, 0.0))
    total = jnp.sum(dots, axis=1, keepdims=True)
    keep = (lanes >= NE) & (lanes < NE + 2 * NC)
    dsmall = jnp.where(lanes < NE, dots - held * total, jnp.where(keep, local, 0.0))
    high, rest = two_parts(dsmall)
    dn += mm(high, small_w[...], 1, 1) + mm(rest, small_w[...], 1, 1)
    g = grad[...].astype(F32)
    dn += pick(local, lanes, NE + 2 * NC) * g
    res = resid[...]
    factor = lax.rsqrt(jnp.mean(res * res, axis=-1, keepdims=True) + EPS)
    normal = res * factor
    dgain = jnp.sum(dn * normal, axis=0, keepdims=True)
    scaled = dn * gain
    out = g + factor * (scaled - normal * jnp.mean(scaled * normal, axis=-1, keepdims=True))
    dres[...] = out
    low = out.astype(BF16)
    datt[...] = mm(out_w[...], low, 1, 1).astype(BF16)
    full = mm(att[...], low).reshape(pairs, 2 * shard, model)
    kept[:, :, :model] = jnp.where(even, full[:, :shard], full[:, shard:]).astype(BF16)
    sent[:, :, :model] = jnp.where(even, full[:, shard:], full[:, :shard]).astype(BF16)
    result = mm(moe[...], high, 0, 0) + mm(moe[...], rest, 0, 0)
    result += pltpu.roll(grad_vec[...], NE + 2 * NC, 1)
    lanes = lane_of(result.shape)
    column = jnp.transpose(jnp.broadcast_to(dgain, (LANES, model)))
    result += jnp.where(lanes == NE + 3 * NC, column, 0.0)
    table = mm(prior_hits[...], high, 0, 0) + mm(prior_hits[...], rest, 0, 0)
    table = jnp.where(lane_of((NE, LANES)) < NE, table[:NE], 0.0)
    high, rest = two_parts(table)
    block = pltpu.roll(high.astype(F32), 2 * NE, 1) + pltpu.roll(rest.astype(F32), 3 * NE, 1)
    block = jnp.concatenate([block, jnp.zeros((shard - NE, LANES), F32)], axis=0)
    full = result.reshape(pairs, 2 * shard, LANES)
    first, second = full[:, :shard] + block[None], full[:, shard:] + block[None]
    kept[:, :, model:] = jnp.where(even, first, second).astype(BF16)
    sent[:, :, model:] = jnp.where(even, second, first).astype(BF16)


def unroute(meta, before, back, weights, tokenwise, att, moe, grad_vec, prior_hits, count):
    resid = tokenwise[1]
    rows, model = resid.shape
    inputs = [*come(*back), *weight_blocks(weights), *tokenwise, att, moe, grad_vec, prior_hits]
    results = [((model, rows), BF16), ((rows, model), F32)]
    results += [((count // 2, model // count, model + LANES), BF16)] * 2
    return one_step(unroute_kernel, 100, meta, inputs, results, (), before, 32)


def finish_kernel(meta, *refs):
    dproj, (weight, tok, gain, dres) = refs[:SEQS], refs[SEQS : SEQS + 4]
    out, flat = refs[-2:]
    width = dproj[0].shape[0]
    for s in range(SEQS):
        at = pl.multiple_of(around(meta, s) * width, 64)
        flat[pl.ds(at, width)] = dproj[s][...]
    dn = jnp.transpose(mm(weight[...], flat[...]))
    v = tok[...].astype(F32)
    factor = lax.rsqrt(jnp.mean(v * v, axis=-1, keepdims=True) + EPS)
    normal = v * factor
    scaled = dn * gain[...]
    dx = factor * (scaled - normal * jnp.mean(scaled * normal, axis=-1, keepdims=True))
    out[...] = (dres[...] + dx).astype(BF16)


def finish(meta, dproj, weight, tok, gain, dres, *before):
    width, rows = dproj[0].shape
    scratch = [pltpu.VMEM((SEQS * width, rows), BF16)]
    results = [(tok.shape, BF16)]
    inputs = [*come(*dproj), weight, tok, gain, dres]
    return one_step(finish_kernel, 0.1, meta, inputs, results, scratch, before, 24)[0]


def gather_kernel(meta, *refs):
    pieces = refs[:SEQS]
    grad_in, grad_out = refs[-2:]
    wide = grad_in.shape[2]
    for s in range(SEQS):
        place = around(meta, s)
        grad_in[place] = pieces[s][:, :wide].astype(F32)
        grad_out[place] = tiles_moved(pieces[s][:, wide:].astype(F32), *grad_out.shape[1:])


def gather(meta, pieces, wide, rows, model, *before):
    shard = pieces[0].shape[0]
    results = [((SEQS, shard, wide), F32), ((SEQS, rows, model), F32)]
    return one_step(gather_kernel, 0.1, meta, come(*pieces), results, (), before, 24)


def gather_dense_kernel(meta, *refs):
    pieces, attend_in, gain_a = refs[:SEQS], refs[SEQS], refs[SEQS + 1]
    att_in, grad_gain, att_out, router, const_mix, const_vector, gain, table, held = refs[-9:]
    shard, model = att_out.shape
    group = model // SEQS
    at = model + LANES
    for s in range(SEQS):
        held[around(meta, s)] = pieces[s][...].astype(F32)
    order = [(k, g) for k in range(3) for g in range(SEQS)]
    parts = [held[g][:, at + k * group : at + (k + 1) * group] for k, g in order]
    full = jnp.concatenate(parts, axis=1)
    att_in[...] = full
    low = attend_in[...].astype(BF16).astype(F32)
    column = jnp.sum(full * low, axis=1, keepdims=True)
    column = jnp.concatenate([column, jnp.zeros((LANES - shard, 1), F32)], axis=0)
    row = jnp.transpose(jnp.broadcast_to(column, (LANES, LANES)))[:1, :shard]
    grad_gain[...] = row / gain_a[...].astype(BF16).astype(F32)

    total = held[0][:, :at]
    for s in range(1, SEQS):
        total += held[s][:, :at]
    att_out[...] = total[:, :model]
    small = jnp.concatenate([total[:, model:], jnp.zeros((LANES - shard, LANES), F32)], axis=0)
    both = small + pltpu.roll(small, LANES - NE, 1)
    table[...] = pltpu.roll(both, LANES - 2 * NE, 1)[:NE, :NE]
    small = jnp.transpose(small)[:, :shard]
    at = NE + 2 * NC
    router[...] = small[:NE]
    const_mix[...] = small[NE:at]
    const_vector[...] = small[at : at + NC]
    gain[...] = small[at + NC : at + NC + 1]


def gather_dense(meta, pieces, attend_in, gain):
    shard, wide = pieces[0].shape
    model = attend_in.shape[1] // 3
    results = [attend_in.shape, (1, shard), (shard, model), (NE, shard), (2 * NC, shard)]
    results = [(r, F32) for r in (*results, (NC, shard), (1, shard), (NE, NE))]
    scratch = [pltpu.VMEM((SEQS, shard, wide), F32)]
    inputs = [*come(*pieces), attend_in, gain]
    return one_step(gather_dense_kernel, 0.1, meta, inputs, results, scratch, mib=16)


def shards(
    tokens,
    cotangent,
    lengths,
    routes,
    prior_routes,
    gain_attend,
    attend_in,
    attend_out,
    gain_mix,
    router,
    route_table,
    const_mix,
    const_vector,
    expert_in,
    expert_out,
):
    seqs = lax.axis_size("seq")
    fsdp = lax.axis_size(FSDP)
    here = lax.axis_index("seq")
    tok = tokens[0]
    rows, model = tok.shape
    shard = attend_in.shape[0]
    group = model // seqs
    width = 3 * group
    length = lengths[0]
    meta = jnp.stack([length, here, *(lax.axis_index(a) for a in ("core", *YZ))])
    meta = meta.astype(jnp.int32)

    first, second, back_mine = pack(
        meta,
        attend_in,
        gain_attend[None],
        attend_out,
        router.T,
        const_mix.T,
        const_vector.T,
        gain_mix[None],
        expert_in,
        expert_out,
        fsdp,
    )
    first_all = swap(first, FSDP).reshape(model, width + 64)
    half = rows // 2
    left, right = shift(tok, 1), shift(tok, -1)
    far0, far1 = shift(left[:half], 1), shift(right[half:], -1)
    weights = lax.all_gather(second, FSDP, axis=0, tiled=True)
    back_w = lax.all_gather(back_mine, FSDP, axis=0, tiled=True)
    inner = expert_out.shape[1] * fsdp
    wide = expert_out.shape[1] * model // shard
    w_out = weights[:, model + 2 * LANES + 2 * inner :]
    w_out = w_out.reshape(-1, shard // 8, 8, wide // LANES, LANES).transpose(0, 1, 3, 2, 4)
    w_out = w_out.reshape(-1, model // LANES, 8, LANES).transpose(0, 2, 1, 3).reshape(inner, model)
    gain_a = first_all[:, width].astype(F32)[None]

    slots, grad, prior, prior_hits, *grad_rows = plan(
        meta, routes[0].T, prior_routes[0].T, route_table, cotangent[0]
    )
    inverse = jnp.exp(
        jnp.arange(HALF, dtype=F32) * (-2.0 * math.log(10000.0) / HEAD_DIM)
    )
    angles = jnp.arange(seqs * rows, dtype=F32).reshape(seqs, 1, rows) * inverse[None, :, None]
    cosine, sine = jnp.cos(angles), jnp.sin(angles)

    left, right, *grad_rows = lax.optimization_barrier((left, right, *grad_rows))
    grad_rows = trades(grad_rows)

    qkv, normed = project(
        meta, [tok, left, right, far0, far1], first_all, gain_a, cosine, sine, width
    )
    held, lse = attend(meta, qkv)
    held, *grad_rows = lax.optimization_barrier((held, *grad_rows))
    att = swap(held, "seq").reshape(model, rows)
    *sent, resid, moe, stats, vectors = route(meta, att, weights, tok, prior, slots)
    sent = trades(sent)
    partial, small, grad_vec = local_part(meta, resid, stats, grad, vectors)

    *back, row, scaled, gate, hidden, dgate, dup = expert(
        meta, sent, grad_rows, small, weights, w_out, 512
    )
    back = trades(back)
    in_kept, in_sent, out_kept, out_sent, *branch = expert_grads(
        meta, row, scaled, gate, hidden, dgate, dup, w_out, back_w, 512, fsdp
    )
    in_come, out_come = trade(in_sent, 1, "core"), trade(out_sent, 1, "core")
    tokenwise = (slots, resid, small, stats, grad, vectors)
    datt, dres, kept, gone = unroute(
        meta, (in_kept,), back, weights, tokenwise, att, moe, grad_vec, prior_hits, fsdp
    )
    come_dense = trade(gone, 1, "core")
    dout = swap(datt.reshape(seqs, group, rows), "seq")
    both = add_cores((in_kept, in_come, out_kept, out_come), dres)
    both, *branch = lax.optimization_barrier((both, *branch))
    branch = trades(branch)
    part = both.reshape(-1, both.shape[2])
    part = lax.psum_scatter(part, YZ, scatter_dimension=0, tiled=True)
    *dproj, heads, gone = attend_back(
        meta, (both, come_dense), qkv, dout, held, lse, cosine, sine, normed, fsdp
    )
    mixed_out = mixed(meta, partial, slots, branch, heads)
    gone, mixed_out, *dproj = lax.optimization_barrier((gone, mixed_out, *dproj))
    come_heads = trade(gone, 1, "core")
    back_all = trades(dproj)
    dense = add_dense(meta, kept, come_dense, heads, come_heads)
    dense = swap(dense, YZ)
    dense = add_pieces(meta, dense)
    grad_tokens = finish(meta, back_all, back_w, tok, gain_a, dres, dense)
    grad_attend_in, grad_gain_a, grad_att_out, *rest, table = gather_dense(
        meta, trades([dense] * seqs), attend_in, gain_attend[None]
    )
    grad_router, grad_mix, grad_vector, grad_gain_m = rest
    part, grad_tokens, grad_gain_a = lax.optimization_barrier((part, grad_tokens, grad_gain_a))
    grad_in, grad_out = gather(
        meta, trades([part] * seqs), 2 * inner, expert_out.shape[1], model
    )
    return (
        mixed_out[None],
        grad_tokens[None],
        grad_gain_a[0],
        grad_attend_in,
        grad_att_out,
        grad_gain_m[0],
        grad_router.T,
        table,
        grad_mix.T,
        grad_vector.T,
        grad_in,
        grad_out,
    )


def solution(mesh):
    fsdp = mesh.shape["fsdp"]
    finer = Mesh(
        mesh.devices.reshape(mesh.shape["seq"], fsdp // (2 * SIDE), SIDE, 2), ("seq", *FSDP)
    )
    placed = (
        P(FSDP, "seq", None),
        P(FSDP, "seq", None),
        P(FSDP),
        P(FSDP, "seq", None),
        P(FSDP, "seq", None),
        P(FSDP),
        P(FSDP, None),
        P(FSDP, None),
        P(FSDP),
        P(FSDP, None),
        P(),
        P(FSDP, None),
        P(FSDP, None),
        P(None, FSDP, None),
        P(None, FSDP, None),
    )
    return jax.shard_map(
        shards,
        mesh=finer,
        in_specs=placed,
        out_specs=(
            P(FSDP, "seq", None),
            P(FSDP, "seq", None),
            P(FSDP),
            P(FSDP, None),
            P(FSDP, None),
            P(FSDP),
            P(FSDP, None),
            P(),
            P(FSDP, None),
            P(FSDP, None),
            P(None, FSDP, None),
            P(None, FSDP, None),
        ),
        check_vma=False,
    )
```

profile of v0, /device:TPU:0, one launch (start us, length us, event | category | flops | bytes accessed | tf_op | source)
XLA Modules:
  0.0 291.6 jit_solution(13465201137348865479)
XLA Ops:
  8.0 3.3 %pack.1 = (bf16[32,24,640]{2,1,0:T(8,128)(2,1)}, bf16[24,7168]{1,0:T(8,128)(2,1)}, bf16[24,2304]{1,0:T(8,128)(2,1)}) custom-call(s32[5]{0:T(128)S(1)} %stack.19.meta, f32[24,2304]{1,0:T(8,128)} %refs_4_.1, f32[1,24]{1,0:T(1,128)} %bitcast.53, f32[24,768]{1,0:T(8,128)} %attend_out.1, f32[8,24]{1,0:T(8,128)} %bitcast.56, f32[4,24]{1,0:T(4,128)} %bitcast.60, ...), custom_call_target="tpu_custom_call" | custom-call | flops 2200000000 | bytes 65536 | tf_op jit(solution)/shard_map/pack/pallas_call | solution.py:205
  11.3 2.9 collective-permute-start.1
  14.2 8.3 %all-to-all-start = ((bf16[32,24,640]{2,1,0:T(8,128)(2,1)}), bf16[32,24,640]{2,1,0:T(8,128)(2,1)S(1)}, u32[]{:S(2)}, u32[]{:S(2)}) async-start(bf16[32,24,640]{2,1,0:T(8,128)(2,1)} %get-tuple-element.107), calls=%async_computation | async-start | bytes 1966080 | tf_op jit(solution)/shard_map/all_to_all | solution.py:105
  22.6 8.4 %collective-permute-done.1.refs_2_ = bf16[512,768]{1,0:T(8,128)(2,1)S(1)} collective-permute-done((bf16[512,768]{1,0:T(8,128)(2,1)S(1)}, bf16[512,768]{1,0:T(8,128)(2,1)S(1)}, u32[]{:S(2)}, u32[]{:S(2)}) %collective-permute-start.1) | collective-permute-done | bytes 786464 | tf_op jit(solution)/shard_map/ppermute | solution.py:88
  31.0 0.8 slice.17
  31.8 3.7 %collective-permute-start.3 = (bf16[256,768]{1,0:T(8,128)(2,1)}, bf16[256,768]{1,0:T(8,128)(2,1)}, u32[]{:S(2)}, u32[]{:S(2)}) collective-permute-start(bf16[256,768]{1,0:T(8,128)(2,1)} %slice.17), channel_id=1, source_target_pairs={{0,96},{32,0},{64,32},{96,64},{1,97},{33,1},{65,33},{97,65},{2,98}... | collective-permute-start | bytes 1179656 | tf_op jit(solution)/shard_map/ppermute | solution.py:88
  35.5 0.8 slice.16
  36.3 3.5 %plan.1 = (bf16[4,192,512]{2,1,0:T(8,128)(2,1)}, bf16[512,768]{1,0:T(8,128)(2,1)}, f32[512,128]{1,0:T(8,128)}, bf16[512,128]{1,0:T(8,128)(2,1)}, bf16[192,768]{1...) custom-call(s32[5]{0:T(128)S(1)} %stack.19.meta, ...), custom_call_target="tpu_custom_call" | custom-call | flops 1100000000 | bytes 65536 | tf_op jit(solution)/shard_map/plan/pallas_call | solution.py:73
  39.8 1.8 multiply_sine_fusion
  41.6 4.7 %collective-permute-start.5 = (bf16[192,768]{1,0:T(8,128)(2,1)}, bf16[192,768]{1,0:T(8,128)(2,1)}, u32[]{:S(2)}, u32[]{:S(2)}) collective-permute-start(bf16[192,768]{1,0:T(8,128)(2,1)} %get-tuple-element.112), channel_id=1, source_target_pairs={{0,64},{32,96},{64,0},{96,32},{1,65},{33,97},{65,1},{97,33},{2,66}... | collective-permute-start | bytes 884744 | tf_op jit(solution)/shard_map/ppermute | solution.py:93
  46.3 0.4 collective-permute-start.6
  46.8 0.2 convert_reduce_fusion
  47.0 0.6 collective-permute-done.2.refs_3_
  47.6 6.2 %project.1 = (bf16[4,576,512]{2,1,0:T(8,128)(2,1)S(1)}, bf16[4,512,768]{2,1,0:T(8,128)(2,1)}) custom-call(s32[5]{0:T(128)S(1)} %stack.19.meta, bf16[512,768]{1,0:T(8,128)(2,1)S(1)} %bitcast.44, bf16[512,768]{1,0:T(8,128)(2,1)S(1)} %collective-permute-done.refs_1_, bf16[512,768]{1,0:T(8,128)(2,1)S(1)} %collective-permute-done.1.refs_2_, ...), custom_call_target="tpu_custom_call" | custom-call | flops 109999996928 | bytes 65536 | tf_op jit(solution)/shard_map/project/pallas_call | solution.py:73
  53.8 16.2 %attend.1 = (bf16[4,192,512]{2,1,0:T(8,128)(2,1)}, f32[4,8,512]{2,1,0:T(8,128)}) custom-call(s32[5]{0:T(128)S(1)} %stack.19.meta, bf16[4,576,512]{2,1,0:T(8,128)(2,1)S(1)} %get-tuple-element.108.qkv), custom_call_target="tpu_custom_call" | custom-call | flops 110000000 | bytes 65536 | tf_op jit(solution)/shard_map/attend/pallas_call | solution.py:73
  70.0 1.4 copy-done
  71.4 3.9 %all-to-all-start.1 = ((bf16[4,192,512]{2,1,0:T(8,128)(2,1)}), bf16[4,192,512]{2,1,0:T(8,128)(2,1)S(1)}, u32[]{:S(2)}, u32[]{:S(2)}) async-start(bf16[4,192,512]{2,1,0:T(8,128)(2,1)} %get-tuple-element.114.refs_1_), calls=%async_computation.1 | async-start | bytes 1572864 | tf_op jit(solution)/shard_map/all_to_all | solution.py:105
  75.4 0.2 all-gather.5.cloned.1.call-start
  75.5 0.6 all-gather.5.cloned.1.call-update
  76.1 9.4 %all-to-all-done.1 = bf16[4,192,512]{2,1,0:T(8,128)(2,1)S(1)} async-done(((bf16[4,192,512]{2,1,0:T(8,128)(2,1)}), bf16[4,192,512]{2,1,0:T(8,128)(2,1)S(1)}, u32[]{:S(2)}, u32[]{:S(2)}) %all-to-all-start.1) | async-done | bytes 786464 | tf_op jit(solution)/shard_map/all_to_all | solution.py:105
  85.5 6.2 %route.1 = (bf16[192,896]{1,0:T(8,128)(2,1)}, bf16[192,896]{1,0:T(8,128)(2,1)}, bf16[192,896]{1,0:T(8,128)(2,1)}, bf16[192,896]{1,0:T(8,128)(2,1)}, f32[512,768]...) custom-call(s32[5]{0:T(128)S(1)} %stack.19.meta, bf16[768,512]{1,0:T(8,128)(2,1)S(1)} %bitcast.45, ...), custom_call_target="tpu_custom_call" | custom-call | flops 109999996928 | bytes 65536 | tf_op jit(solution)/shard_map/route/pallas_call | solution.py:73
  91.7 0.7 collective-permute-start.7
  92.3 2.1 collective-permute-start.8
  94.5 2.0 collective-permute-start.9
  96.5 4.1 %slice.19 = bf16[768,2048]{1,0:T(8,128)(2,1)} slice(bf16[768,7168]{1,0:T(8,128)(2,1)} %all-gather.3.cloned.1.call-done.out_w.small_w.refs_9_.refs_10_.refs_4_.refs_5_), slice={[0:768], [5120:7168]} | slice | bytes 6291456 | tf_op jit(solution)/shard_map/slice | solution.py:997
  100.6 5.0 %local_part.1 = (f32[512,768]{1,0:T(8,128)}, f32[512,128]{1,0:T(8,128)}, f32[768,128]{1,0:T(8,128)}) custom-call(s32[5]{0:T(128)S(1)} %stack.19.meta, f32[512,768]{1,0:T(8,128)} %get-tuple-element.126.resid.refs_7_, f32[512,128]{1,0:T(8,128)} %get-tuple-element.127.stats.refs_9_, bf16[512,768]{1,0:T(8,128)(2,1)} %get-tuple-element.128.grad.refs_10_, ...), custom_call_target="tpu_custom_call" | custom-call | flops 110000000 | bytes 65536 | tf_op jit(solution)/shard_map/local_part/pallas_call | solution.py:73
  105.6 0.8 collective-permute-done.8.refs_2_
  106.4 2.5 collective-permute-done.9.refs_3_
  108.9 21.0 %expert.1 = (bf16[192,896]{1,0:T(8,128)(2,1)}, bf16[192,896]{1,0:T(8,128)(2,1)}, bf16[192,896]{1,0:T(8,128)(2,1)}, bf16[192,896]{1,0:T(8,128)(2,1)}, bf16[768,76...) custom-call(s32[5]{0:T(128)S(1)} %stack.19.meta, ...), custom_call_target="tpu_custom_call" | custom-call | flops 11000000512 | bytes 65536 | tf_op jit(solution)/shard_map/expert/pallas_call | solution.py:609
  129.9 3.4 %collective-permute-start.11 = (bf16[192,896]{1,0:T(8,128)(2,1)}, bf16[192,896]{1,0:T(8,128)(2,1)S(1)}, u32[]{:S(2)}, u32[]{:S(2)}) collective-permute-start(bf16[192,896]{1,0:T(8,128)(2,1)} %get-tuple-element.133), channel_id=1, source_target_pairs={{0,64},{32,96},{64,0},{96,32},{1,65},{33,97},{65,1},{97,33},{2,66}... | collective-permute-start | bytes 1032200 | tf_op jit(solution)/shard_map/ppermute | solution.py:93
  133.3 1.4 collective-permute-start.12
  134.8 18.7 %expert_grads.1 = (bf16[16,24,4096]{2,1,0:T(8,128)(2,1)}, bf16[16,24,4096]{2,1,0:T(8,128)(2,1)}, bf16[16,64,768]{2,1,0:T(8,128)(2,1)}, bf16[16,64,768]{2,1,0:T(8...) custom-call(s32[5]{0:T(128)S(1)} %stack.19.meta, ...), custom_call_target="tpu_custom_call" | custom-call | flops 109999996928 | bytes 65536 | tf_op jit(solution)/shard_map/expert_grads/pallas_call | solution.py:689
  153.5 0.5 collective-permute-start.13
  154.0 9.3 %unroute.1 = (bf16[768,512]{1,0:T(8,128)(2,1)}, f32[512,768]{1,0:T(8,128)}, bf16[16,24,896]{2,1,0:T(8,128)(2,1)}, bf16[16,24,896]{2,1,0:T(8,128)(2,1)}) custom-call(s32[5]{0:T(128)S(1)} %stack.19.meta, bf16[192,896]{1,0:T(8,128)(2,1)S(1)} %copy-done.10, bf16[192,896]{1,0:T(8,128)(2,1)S(1)} %collective-permute-done.10.refs_1_, ...), custom_call_target="tpu_custom_call" | custom-call | flops 109999996928 | bytes 65536 | tf_op jit(solution)/shard_map/unroute/pallas_call | solution.py:73
  163.4 3.5 %all-to-all-start.2 = ((bf16[4,192,512]{2,1,0:T(8,128)(2,1)}), bf16[4,192,512]{2,1,0:T(8,128)(2,1)S(1)}, u32[]{:S(2)}, u32[]{:S(2)}) async-start(bf16[4,192,512]{2,1,0:T(8,128)(2,1)} %bitcast.52), calls=%async_computation.2 | async-start | bytes 1572864 | tf_op jit(solution)/shard_map/all_to_all | solution.py:105
  166.9 0.2 collective-permute-start.15
  167.1 6.2 %add_cores.1.refs_6_ = bf16[16,24,6144]{2,1,0:T(8,128)(2,1)} custom-call(bf16[16,24,4096]{2,1,0:T(8,128)(2,1)} %get-tuple-element.145.refs_16_.in_a, bf16[16,24,4096]{2,1,0:T(8,128)(2,1)} %collective-permute-done.13.in_b, bf16[16,64,768]{2,1,0:T(8,128)(2,1)} %get-tuple-element.150.out_a, bf16[16,64,768]{2,1,0:T(8,128)(2,1)S(1)} %collective-permute-done.14.out_b, ...), custom_call_target="tpu_custom_call" | custom-call | flops 109999996928 | bytes 65536 | tf_op jit(solution)/shard_map/add_cores/pallas_call | solution.py:740
  173.3 1.9 collective-permute-start.16
  175.2 2.7 collective-permute-start.17
  177.8 0.5 collective-permute-start.18
  178.3 1.9 all-to-all-done.2.refs_0_
  180.2 26.5 %attend_back.1 = (bf16[576,512]{1,0:T(8,128)(2,1)}, bf16[576,512]{1,0:T(8,128)(2,1)}, bf16[576,512]{1,0:T(8,128)(2,1)}, bf16[576,512]{1,0:T(8,128)(2,1)}, bf16[1...) custom-call(s32[5]{0:T(128)S(1)} %stack.19.meta, bf16[4,576,512]{2,1,0:T(8,128)(2,1)S(1)} %copy-done.1, ...), custom_call_target="tpu_custom_call" | custom-call | flops 109999996928 | bytes 65536 | tf_op jit(solution)/shard_map/attend_back/pallas_call | solution.py:73
  206.7 3.8 %mixed.1 = bf16[512,768]{1,0:T(8,128)(2,1)} custom-call(s32[5]{0:T(128)S(1)} %stack.19.meta, f32[512,768]{1,0:T(8,128)} %get-tuple-element.160.partial, bf16[4,192,512]{2,1,0:T(8,128)(2,1)} %get-tuple-element.117.slots.refs_6_, bf16[192,768]{1,0:T(8,128)(2,1)S(1)} %copy-done.6, bf16[192,768]{1,0:T(8,128)(2,1)S(1)} %collective-permute-done.16.refs_1_, ...), custom_call_target="tpu_custom_call" | custom-call | flops 110000000 | bytes 65536 | tf_op jit(solution)/shard_map/mixed/pallas_call | solution.py:73
  210.5 1.9 collective-permute-done.22.heads_b
  212.4 2.9 add_dense.1
  215.3 8.8 %all-to-all-start.3 = ((bf16[16,24,1536]{2,1,0:T(8,128)(2,1)}), bf16[16,24,1536]{2,1,0:T(8,128)(2,1)S(1)}, u32[]{:S(2)}, u32[]{:S(2)}) async-start(bf16[16,24,1536]{2,1,0:T(8,128)(2,1)} %add_dense.1), calls=%async_computation.3 | async-start | bytes 2359296 | tf_op jit(solution)/shard_map/all_to_all | solution.py:105
  224.1 1.0 collective-permute-start.19
  225.1 2.0 collective-permute-start.20
  227.2 1.7 collective-permute-start.21
  228.9 16.3 %all-to-all-done.3.pieces = bf16[16,24,1536]{2,1,0:T(8,128)(2,1)S(1)} async-done(((bf16[16,24,1536]{2,1,0:T(8,128)(2,1)}), bf16[16,24,1536]{2,1,0:T(8,128)(2,1)S(1)}, u32[]{:S(2)}, u32[]{:S(2)}) %all-to-all-start.3) | async-done | bytes 1179680 | tf_op jit(solution)/shard_map/all_to_all | solution.py:105
  245.2 1.4 add_pieces.1.refs_8_.refs_0_
  246.6 1.4 collective-permute-start.25
  248.0 1.5 collective-permute-start.24
  249.5 1.2 collective-permute-start.23
  250.7 3.6 %collective-permute-done.20.refs_2_ = bf16[576,512]{1,0:T(8,128)(2,1)S(1)} collective-permute-done((bf16[576,512]{1,0:T(8,128)(2,1)}, bf16[576,512]{1,0:T(8,128)(2,1)S(1)}, u32[]{:S(2)}, u32[]{:S(2)}) %collective-permute-start.20) | collective-permute-done | bytes 589856 | tf_op jit(solution)/shard_map/ppermute | solution.py:93
  254.2 3.9 %collective-permute-done.21.refs_3_ = bf16[576,512]{1,0:T(8,128)(2,1)S(1)} collective-permute-done((bf16[576,512]{1,0:T(8,128)(2,1)}, bf16[576,512]{1,0:T(8,128)(2,1)S(1)}, u32[]{:S(2)}, u32[]{:S(2)}) %collective-permute-start.21) | collective-permute-done | bytes 589856 | tf_op jit(solution)/shard_map/ppermute | solution.py:93
  258.1 6.5 %finish.1 = bf16[512,768]{1,0:T(8,128)(2,1)} custom-call(s32[5]{0:T(128)S(1)} %stack.19.meta, bf16[576,512]{1,0:T(8,128)(2,1)S(1)} %copy-done.5, bf16[576,512]{1,0:T(8,128)(2,1)S(1)} %collective-permute-done.19.refs_1_, bf16[576,512]{1,0:T(8,128)(2,1)S(1)} %collective-permute-done.20.refs_2_, bf16[576,512]{1,0:T(8,128)(2,1)S(1)} %collective-permute-done.21.refs_3_, ...), custom_call_target="tpu_custom_call" | custom-call | flops 110000000 | bytes 65536 | tf_op jit(solution)/shard_map/finish/pallas_call | solution.py:73
  264.6 2.0 gather_dense.1
  266.6 1.8 collective-permute-start.28
  268.4 2.4 collective-permute-start.26
  270.8 10.2 %collective-permute-done.28.refs_3_ = bf16[24,6144]{1,0:T(8,128)(2,1)S(1)} collective-permute-done((bf16[24,6144]{1,0:T(8,128)(2,1)}, bf16[24,6144]{1,0:T(8,128)(2,1)S(1)}, u32[]{:S(2)}, u32[]{:S(2)}) %collective-permute-start.28) | collective-permute-done | bytes 294944 | tf_op jit(solution)/shard_map/ppermute | solution.py:93
  281.0 0.6 collective-permute-done.26.refs_1_
  281.6 1.0 copy-done.7
  282.5 2.1 gather.1
  (63 shorter events, 0.4 us)
Async XLA Ops:
  7.2 78.3 %all-gather.3.cloned.1.call-start = ((), (), s32[]{:S(2)}) async-start(), calls=%async_computation.5 | async-start | bytes 11354112 | tf_op jit(solution)/shard_map/all_gather | solution.py:993
  8.0 3.3 %copy-start.2 = (bf16[1,512,768]{2,1,0:T(8,128)(2,1)S(1)}, bf16[1,512,768]{2,1,0:T(8,128)(2,1)}, u32[]{:S(2)}) copy-start(bf16[1,512,768]{2,1,0:T(8,128)(2,1)} %param.15) | copy-start | bytes 2359300
  11.3 19.7 %collective-permute-start.1 = (bf16[512,768]{1,0:T(8,128)(2,1)S(1)}, bf16[512,768]{1,0:T(8,128)(2,1)S(1)}, u32[]{:S(2)}, u32[]{:S(2)}) collective-permute-start(bf16[512,768]{1,0:T(8,128)(2,1)S(1)} %bitcast.42), channel_id=1, source_target_pairs={{0,96},{32,0},{64,32},{96,64},{1,97},{33,1},{65,33},{97,65},{2,98}... | collective-permute-start | bytes 2359304 | tf_op jit(solution)/shard_map/ppermute | solution.py:88
  14.2 21.3 %collective-permute-start = (bf16[512,768]{1,0:T(8,128)(2,1)S(1)}, bf16[512,768]{1,0:T(8,128)(2,1)S(1)}, u32[]{:S(2)}, u32[]{:S(2)}) collective-permute-start(bf16[512,768]{1,0:T(8,128)(2,1)S(1)} %bitcast.43), channel_id=1, source_target_pairs={{0,32},{32,64},{64,96},{96,0},{1,33},{33,65},{65,97},{97,1},{2,34}... | collective-permute-start | bytes 2359304 | tf_op jit(solution)/shard_map/ppermute | solution.py:88
  14.2 32.6 %all-to-all-start = ((bf16[32,24,640]{2,1,0:T(8,128)(2,1)}), bf16[32,24,640]{2,1,0:T(8,128)(2,1)S(1)}, u32[]{:S(2)}, u32[]{:S(2)}) async-start(bf16[32,24,640]{2,1,0:T(8,128)(2,1)} %get-tuple-element.107), calls=%async_computation | async-start | bytes 1966080 | tf_op jit(solution)/shard_map/all_to_all | solution.py:105
  31.8 15.2 %collective-permute-start.3 = (bf16[256,768]{1,0:T(8,128)(2,1)}, bf16[256,768]{1,0:T(8,128)(2,1)}, u32[]{:S(2)}, u32[]{:S(2)}) collective-permute-start(bf16[256,768]{1,0:T(8,128)(2,1)} %slice.17), channel_id=1, source_target_pairs={{0,96},{32,0},{64,32},{96,64},{1,97},{33,1},{65,33},{97,65},{2,98}... | collective-permute-start | bytes 1179656 | tf_op jit(solution)/shard_map/ppermute | solution.py:88
  36.3 11.3 %collective-permute-start.2 = (bf16[256,768]{1,0:T(8,128)(2,1)}, bf16[256,768]{1,0:T(8,128)(2,1)}, u32[]{:S(2)}, u32[]{:S(2)}) collective-permute-start(bf16[256,768]{1,0:T(8,128)(2,1)} %slice.16), channel_id=1, source_target_pairs={{0,32},{32,64},{64,96},{96,0},{1,33},{33,65},{65,97},{97,1},{2,34}... | collective-permute-start | bytes 1179656 | tf_op jit(solution)/shard_map/ppermute | solution.py:88
  41.6 29.8 %collective-permute-start.4 = (bf16[192,768]{1,0:T(8,128)(2,1)}, bf16[192,768]{1,0:T(8,128)(2,1)}, u32[]{:S(2)}, u32[]{:S(2)}) collective-permute-start(bf16[192,768]{1,0:T(8,128)(2,1)} %get-tuple-element.111), channel_id=1, source_target_pairs={{0,32},{32,0},{64,96},{96,64},{1,33},{33,1},{65,97},{97,65},{2,34}... | collective-permute-start | bytes 884744 | tf_op jit(solution)/shard_map/ppermute | solution.py:93
  41.6 29.8 %collective-permute-start.5 = (bf16[192,768]{1,0:T(8,128)(2,1)}, bf16[192,768]{1,0:T(8,128)(2,1)}, u32[]{:S(2)}, u32[]{:S(2)}) collective-permute-start(bf16[192,768]{1,0:T(8,128)(2,1)} %get-tuple-element.112), channel_id=1, source_target_pairs={{0,64},{32,96},{64,0},{96,32},{1,65},{33,97},{65,1},{97,33},{2,66}... | collective-permute-start | bytes 884744 | tf_op jit(solution)/shard_map/ppermute | solution.py:93
  46.3 25.1 %collective-permute-start.6 = (bf16[192,768]{1,0:T(8,128)(2,1)}, bf16[192,768]{1,0:T(8,128)(2,1)}, u32[]{:S(2)}, u32[]{:S(2)}) collective-permute-start(bf16[192,768]{1,0:T(8,128)(2,1)} %get-tuple-element.113), channel_id=1, source_target_pairs={{0,96},{32,64},{64,32},{96,0},{1,97},{33,65},{65,33},{97,1},{2,98}... | collective-permute-start | bytes 884744 | tf_op jit(solution)/shard_map/ppermute | solution.py:93
  47.0 6.8 %copy-start.8 = (f32[1,768]{1,0:T(1,128)}, f32[1,768]{1,0:T(1,128)S(1)}, u32[]{:S(2)}) copy-start(f32[1,768]{1,0:T(1,128)S(1)} %reshape.104.refs_6_) | copy-start | bytes 9220
  70.0 1.4 copy-start
  71.4 14.1 %all-to-all-start.1 = ((bf16[4,192,512]{2,1,0:T(8,128)(2,1)}), bf16[4,192,512]{2,1,0:T(8,128)(2,1)S(1)}, u32[]{:S(2)}, u32[]{:S(2)}) async-start(bf16[4,192,512]{2,1,0:T(8,128)(2,1)} %get-tuple-element.114.refs_1_), calls=%async_computation.1 | async-start | bytes 1572864 | tf_op jit(solution)/shard_map/all_to_all | solution.py:105
  75.4 59.4 %all-gather.5.cloned.1.call-start = ((), (), s32[]{:S(2)}) async-start(), calls=%async_computation.6 | async-start | bytes 3649536 | tf_op jit(solution)/shard_map/all_gather | solution.py:994
  85.5 6.2 %copy-start.3 = (bf16[4,192,512]{2,1,0:T(8,128)(2,1)}, bf16[4,192,512]{2,1,0:T(8,128)(2,1)S(1)}, u32[]{:S(2)}) copy-start(bf16[4,192,512]{2,1,0:T(8,128)(2,1)S(1)} %all-to-all-done.1) | copy-start | bytes 2359300
  91.7 13.9 %collective-permute-start.7 = (bf16[192,896]{1,0:T(8,128)(2,1)}, bf16[192,896]{1,0:T(8,128)(2,1)S(1)}, u32[]{:S(2)}, u32[]{:S(2)}) collective-permute-start(bf16[192,896]{1,0:T(8,128)(2,1)} %get-tuple-element.119), channel_id=1, source_target_pairs={{0,32},{32,0},{64,96},{96,64},{1,33},{33,1},{65,97},{97,65},{2,34}... | collective-permute-start | bytes 1032200 | tf_op jit(solution)/shard_map/ppermute | solution.py:93
  92.3 14.0 %collective-permute-start.8 = (bf16[192,896]{1,0:T(8,128)(2,1)}, bf16[192,896]{1,0:T(8,128)(2,1)S(1)}, u32[]{:S(2)}, u32[]{:S(2)}) collective-permute-start(bf16[192,896]{1,0:T(8,128)(2,1)} %get-tuple-element.120), channel_id=1, source_target_pairs={{0,64},{32,96},{64,0},{96,32},{1,65},{33,97},{65,1},{97,33},{2,66}... | collective-permute-start | bytes 1032200 | tf_op jit(solution)/shard_map/ppermute | solution.py:93
  94.5 14.4 %collective-permute-start.9 = (bf16[192,896]{1,0:T(8,128)(2,1)}, bf16[192,896]{1,0:T(8,128)(2,1)S(1)}, u32[]{:S(2)}, u32[]{:S(2)}) collective-permute-start(bf16[192,896]{1,0:T(8,128)(2,1)} %get-tuple-element.121), channel_id=1, source_target_pairs={{0,96},{32,64},{64,32},{96,0},{1,97},{33,65},{65,33},{97,1},{2,98}... | collective-permute-start | bytes 1032200 | tf_op jit(solution)/shard_map/ppermute | solution.py:93
  100.6 8.3 %copy-start.9 = (bf16[192,768]{1,0:T(8,128)(2,1)S(1)}, bf16[192,768]{1,0:T(8,128)(2,1)}, u32[]{:S(2)}) copy-start(bf16[192,768]{1,0:T(8,128)(2,1)} %get-tuple-element.122.refs_4_) | copy-start | bytes 884740
  100.6 8.3 %copy-start.11 = (bf16[192,896]{1,0:T(8,128)(2,1)S(1)}, bf16[192,896]{1,0:T(8,128)(2,1)}, u32[]{:S(2)}) copy-start(bf16[192,896]{1,0:T(8,128)(2,1)} %get-tuple-element.118.refs_0_) | copy-start | bytes 1032196
  129.9 24.1 %collective-permute-start.10 = (bf16[192,896]{1,0:T(8,128)(2,1)}, bf16[192,896]{1,0:T(8,128)(2,1)S(1)}, u32[]{:S(2)}, u32[]{:S(2)}) collective-permute-start(bf16[192,896]{1,0:T(8,128)(2,1)} %get-tuple-element.132), channel_id=1, source_target_pairs={{0,32},{32,0},{64,96},{96,64},{1,33},{33,1},{65,97},{97,65},{2,34}... | collective-permute-start | bytes 1032200 | tf_op jit(solution)/shard_map/ppermute | solution.py:93
  129.9 24.1 %collective-permute-start.11 = (bf16[192,896]{1,0:T(8,128)(2,1)}, bf16[192,896]{1,0:T(8,128)(2,1)S(1)}, u32[]{:S(2)}, u32[]{:S(2)}) collective-permute-start(bf16[192,896]{1,0:T(8,128)(2,1)} %get-tuple-element.133), channel_id=1, source_target_pairs={{0,64},{32,96},{64,0},{96,32},{1,65},{33,97},{65,1},{97,33},{2,66}... | collective-permute-start | bytes 1032200 | tf_op jit(solution)/shard_map/ppermute | solution.py:93
  133.3 20.7 %collective-permute-start.12 = (bf16[192,896]{1,0:T(8,128)(2,1)}, bf16[192,896]{1,0:T(8,128)(2,1)S(1)}, u32[]{:S(2)}, u32[]{:S(2)}) collective-permute-start(bf16[192,896]{1,0:T(8,128)(2,1)} %get-tuple-element.134), channel_id=1, source_target_pairs={{0,96},{32,64},{64,32},{96,0},{1,97},{33,65},{65,33},{97,1},{2,98}... | collective-permute-start | bytes 1032200 | tf_op jit(solution)/shard_map/ppermute | solution.py:93
  134.8 19.3 %copy-start.10 = (bf16[192,896]{1,0:T(8,128)(2,1)S(1)}, bf16[192,896]{1,0:T(8,128)(2,1)}, u32[]{:S(2)}) copy-start(bf16[192,896]{1,0:T(8,128)(2,1)} %get-tuple-element.131.refs_0_) | copy-start | bytes 1032196
  153.4 13.7 %collective-permute-start.14 = (bf16[16,64,768]{2,1,0:T(8,128)(2,1)}, bf16[16,64,768]{2,1,0:T(8,128)(2,1)S(1)}, u32[]{:S(2)}, u32[]{:S(2)}) collective-permute-start(bf16[16,64,768]{2,1,0:T(8,128)(2,1)} %get-tuple-element.151), channel_id=1, source_target_pairs={{0,1},{1,0},{2,3},{3,2},{4,5},{5,4},{6,7},{7,6},{8,9},{9,8},{10,11... | collective-permute-start | bytes 4718600 | tf_op jit(solution)/shard_map/ppermute | solution.py:93
  153.5 13.6 %collective-permute-start.13 = (bf16[16,24,4096]{2,1,0:T(8,128)(2,1)}, bf16[16,24,4096]{2,1,0:T(8,128)(2,1)}, u32[]{:S(2)}, u32[]{:S(2)}) collective-permute-start(bf16[16,24,4096]{2,1,0:T(8,128)(2,1)} %get-tuple-element.149), channel_id=1, source_target_pairs={{0,1},{1,0},{2,3},{3,2},{4,5},{5,4},{6,7},{7,6},{8,9},{9,8},{10,11... | collective-permute-start | bytes 9437192 | tf_op jit(solution)/shard_map/ppermute | solution.py:93
  163.4 16.8 %all-to-all-start.2 = ((bf16[4,192,512]{2,1,0:T(8,128)(2,1)}), bf16[4,192,512]{2,1,0:T(8,128)(2,1)S(1)}, u32[]{:S(2)}, u32[]{:S(2)}) async-start(bf16[4,192,512]{2,1,0:T(8,128)(2,1)} %bitcast.52), calls=%async_computation.2 | async-start | bytes 1572864 | tf_op jit(solution)/shard_map/all_to_all | solution.py:105
  166.9 99.7 %reduce-scatter.4.cloned.1.call-start = ((), (), s32[]{:S(2)}) async-start(), calls=%async_computation.7 | async-start | bytes 5013504
  166.9 13.2 %collective-permute-start.15 = (bf16[16,24,896]{2,1,0:T(8,128)(2,1)}, bf16[16,24,896]{2,1,0:T(8,128)(2,1)}, u32[]{:S(2)}, u32[]{:S(2)}) collective-permute-start(bf16[16,24,896]{2,1,0:T(8,128)(2,1)} %get-tuple-element.158), channel_id=1, source_target_pairs={{0,1},{1,0},{2,3},{3,2},{4,5},{5,4},{6,7},{7,6},{8,9},{9,8},{10,11... | collective-permute-start | bytes 2064392 | tf_op jit(solution)/shard_map/ppermute | solution.py:93
  173.3 6.9 %copy-start.1 = (bf16[4,576,512]{2,1,0:T(8,128)(2,1)S(1)}, bf16[4,576,512]{2,1,0:T(8,128)(2,1)}, u32[]{:S(2)}) copy-start(bf16[4,576,512]{2,1,0:T(8,128)(2,1)} %copy-done) | copy-start | bytes 7077892
  173.3 33.4 %collective-permute-start.16 = (bf16[192,768]{1,0:T(8,128)(2,1)}, bf16[192,768]{1,0:T(8,128)(2,1)S(1)}, u32[]{:S(2)}, u32[]{:S(2)}) collective-permute-start(bf16[192,768]{1,0:T(8,128)(2,1)} %get-tuple-element.162), channel_id=1, source_target_pairs={{0,32},{32,0},{64,96},{96,64},{1,33},{33,1},{65,97},{97,65},{2,34}... | collective-permute-start | bytes 884744 | tf_op jit(solution)/shard_map/ppermute | solution.py:93
  175.2 31.5 %collective-permute-start.17 = (bf16[192,768]{1,0:T(8,128)(2,1)}, bf16[192,768]{1,0:T(8,128)(2,1)}, u32[]{:S(2)}, u32[]{:S(2)}) collective-permute-start(bf16[192,768]{1,0:T(8,128)(2,1)} %get-tuple-element.163), channel_id=1, source_target_pairs={{0,64},{32,96},{64,0},{96,32},{1,65},{33,97},{65,1},{97,33},{2,66}... | collective-permute-start | bytes 884744 | tf_op jit(solution)/shard_map/ppermute | solution.py:93
  177.8 28.9 %collective-permute-start.18 = (bf16[192,768]{1,0:T(8,128)(2,1)}, bf16[192,768]{1,0:T(8,128)(2,1)}, u32[]{:S(2)}, u32[]{:S(2)}) collective-permute-start(bf16[192,768]{1,0:T(8,128)(2,1)} %get-tuple-element.164), channel_id=1, source_target_pairs={{0,96},{32,64},{64,32},{96,0},{1,97},{33,65},{65,33},{97,1},{2,98}... | collective-permute-start | bytes 884744 | tf_op jit(solution)/shard_map/ppermute | solution.py:93
  180.2 26.5 %copy-start.6 = (bf16[192,768]{1,0:T(8,128)(2,1)S(1)}, bf16[192,768]{1,0:T(8,128)(2,1)}, u32[]{:S(2)}) copy-start(bf16[192,768]{1,0:T(8,128)(2,1)} %get-tuple-element.161.refs_0_) | copy-start | bytes 884740
  206.7 3.8 %copy-start.12 = (bf16[16,24,576]{2,1,0:T(8,128)(2,1)S(1)}, bf16[16,24,576]{2,1,0:T(8,128)(2,1)}, u32[]{:S(2)}) copy-start(bf16[16,24,576]{2,1,0:T(8,128)(2,1)} %get-tuple-element.176) | copy-start | bytes 1327108
  210.5 1.9 collective-permute-start.22
  215.3 42.9 %copy-start.5 = (bf16[576,512]{1,0:T(8,128)(2,1)S(1)}, bf16[576,512]{1,0:T(8,128)(2,1)}, u32[]{:S(2)}) copy-start(bf16[576,512]{1,0:T(8,128)(2,1)} %get-tuple-element.171.refs_0_) | copy-start | bytes 1769476
  215.3 29.9 %all-to-all-start.3 = ((bf16[16,24,1536]{2,1,0:T(8,128)(2,1)}), bf16[16,24,1536]{2,1,0:T(8,128)(2,1)S(1)}, u32[]{:S(2)}, u32[]{:S(2)}) async-start(bf16[16,24,1536]{2,1,0:T(8,128)(2,1)} %add_dense.1), calls=%async_computation.3 | async-start | bytes 2359296 | tf_op jit(solution)/shard_map/all_to_all | solution.py:105
  224.1 25.4 %collective-permute-start.19 = (bf16[576,512]{1,0:T(8,128)(2,1)}, bf16[576,512]{1,0:T(8,128)(2,1)S(1)}, u32[]{:S(2)}, u32[]{:S(2)}) collective-permute-start(bf16[576,512]{1,0:T(8,128)(2,1)} %get-tuple-element.172), channel_id=1, source_target_pairs={{0,32},{32,0},{64,96},{96,64},{1,33},{33,1},{65,97},{97,65},{2,34}... | collective-permute-start | bytes 1769480 | tf_op jit(solution)/shard_map/ppermute | solution.py:93
  225.1 29.1 %collective-permute-start.20 = (bf16[576,512]{1,0:T(8,128)(2,1)}, bf16[576,512]{1,0:T(8,128)(2,1)S(1)}, u32[]{:S(2)}, u32[]{:S(2)}) collective-permute-start(bf16[576,512]{1,0:T(8,128)(2,1)} %get-tuple-element.173), channel_id=1, source_target_pairs={{0,64},{32,96},{64,0},{96,32},{1,65},{33,97},{65,1},{97,33},{2,66}... | collective-permute-start | bytes 1769480 | tf_op jit(solution)/shard_map/ppermute | solution.py:93
  227.2 31.0 %collective-permute-start.21 = (bf16[576,512]{1,0:T(8,128)(2,1)}, bf16[576,512]{1,0:T(8,128)(2,1)S(1)}, u32[]{:S(2)}, u32[]{:S(2)}) collective-permute-start(bf16[576,512]{1,0:T(8,128)(2,1)} %get-tuple-element.174), channel_id=1, source_target_pairs={{0,96},{32,64},{64,32},{96,0},{1,97},{33,65},{65,33},{97,1},{2,98}... | collective-permute-start | bytes 1769480 | tf_op jit(solution)/shard_map/ppermute | solution.py:93
  246.6 18.1 %copy-start.4 = (bf16[24,1536]{1,0:T(8,128)(2,1)S(1)}, bf16[24,1536]{1,0:T(8,128)(2,1)}, u32[]{:S(2)}) copy-start(bf16[24,1536]{1,0:T(8,128)(2,1)} %add_pieces.1.refs_8_.refs_0_) | copy-start | bytes 221188
  246.6 18.0 %collective-permute-start.25 = (bf16[24,1536]{1,0:T(8,128)(2,1)}, bf16[24,1536]{1,0:T(8,128)(2,1)S(1)}, u32[]{:S(2)}, u32[]{:S(2)}) collective-permute-start(bf16[24,1536]{1,0:T(8,128)(2,1)} %add_pieces.1.refs_8_.refs_0_), channel_id=1, source_target_pairs={{0,96},{32,64},{64,32},{96,0},{1,97},{33,65},{65,33},{97,1},{2,98}... | collective-permute-start | bytes 221192 | tf_op jit(solution)/shard_map/ppermute | solution.py:93
  248.0 16.7 %collective-permute-start.24 = (bf16[24,1536]{1,0:T(8,128)(2,1)}, bf16[24,1536]{1,0:T(8,128)(2,1)S(1)}, u32[]{:S(2)}, u32[]{:S(2)}) collective-permute-start(bf16[24,1536]{1,0:T(8,128)(2,1)} %add_pieces.1.refs_8_.refs_0_), channel_id=1, source_target_pairs={{0,64},{32,96},{64,0},{96,32},{1,65},{33,97},{65,1},{97,33},{2,66}... | collective-permute-start | bytes 221192 | tf_op jit(solution)/shard_map/ppermute | solution.py:93
  249.5 15.2 %collective-permute-start.23 = (bf16[24,1536]{1,0:T(8,128)(2,1)}, bf16[24,1536]{1,0:T(8,128)(2,1)S(1)}, u32[]{:S(2)}, u32[]{:S(2)}) collective-permute-start(bf16[24,1536]{1,0:T(8,128)(2,1)} %add_pieces.1.refs_8_.refs_0_), channel_id=1, source_target_pairs={{0,32},{32,0},{64,96},{96,64},{1,33},{33,1},{65,97},{97,65},{2,34}... | collective-permute-start | bytes 221192 | tf_op jit(solution)/shard_map/ppermute | solution.py:93
  266.6 14.3 %collective-permute-start.28 = (bf16[24,6144]{1,0:T(8,128)(2,1)}, bf16[24,6144]{1,0:T(8,128)(2,1)S(1)}, u32[]{:S(2)}, u32[]{:S(2)}) collective-permute-start(bf16[24,6144]{1,0:T(8,128)(2,1)} %reduce-scatter.4.cloned.1.call-done.refs_0_), channel_id=1, source_target_pairs={{0,96},{32,64},{64,32},{96,0},{1,97},{33,65},{65,33},{97,1},{2,98}... | collective-permute-start | bytes 884744 | tf_op jit(solution)/shard_map/ppermute | solution.py:93
  268.4 12.6 %collective-permute-start.27 = (bf16[24,6144]{1,0:T(8,128)(2,1)}, bf16[24,6144]{1,0:T(8,128)(2,1)S(1)}, u32[]{:S(2)}, u32[]{:S(2)}) collective-permute-start(bf16[24,6144]{1,0:T(8,128)(2,1)} %reduce-scatter.4.cloned.1.call-done.refs_0_), channel_id=1, source_target_pairs={{0,64},{32,96},{64,0},{96,32},{1,65},{33,97},{65,1},{97,33},{2,66}... | collective-permute-start | bytes 884744 | tf_op jit(solution)/shard_map/ppermute | solution.py:93
  268.4 13.2 %collective-permute-start.26 = (bf16[24,6144]{1,0:T(8,128)(2,1)}, bf16[24,6144]{1,0:T(8,128)(2,1)S(1)}, u32[]{:S(2)}, u32[]{:S(2)}) collective-permute-start(bf16[24,6144]{1,0:T(8,128)(2,1)} %reduce-scatter.4.cloned.1.call-done.refs_0_), channel_id=1, source_target_pairs={{0,32},{32,0},{64,96},{96,64},{1,33},{33,1},{65,97},{97,65},{2,34}... | collective-permute-start | bytes 884744 | tf_op jit(solution)/shard_map/ppermute | solution.py:93
  281.6 1.0 copy-start.7
Sparse Core Ops, SparseCore 0:
  11.4 68.0 all-gather.2
  81.9 45.3 all-gather.4
  173.4 90.6 reduce-scatter.3
where the time goes:
time: 297 us; the launch traced here: 292 us
  Pallas kernels  141 us (47%)
  starting transfers between devices  65 us (22%)
  waiting for transfers between devices  60.7 us (20%)
  between operations  15.1 us (5%)
  local copies, waits for them, and re-layouts  8.15 us (3%)
    pallas_call x13, Pallas kernels, one_step(): pl.pallas_call(body, grid=(1,), in_specs=[SMEM] + [spec for _, spec in in...  91.5 us
    ppermute x25, starting transfers between devices, trade(): lax.ppermute(x, axis, [(i, i ^ by) for i in range(count)])  33.6 us
    all_to_all x4, waiting for transfers between devices, swap(): return lax.all_to_all(x, axis, split_axis=0, concat_axis=0, tiled=True)  27.6 us
    all_to_all x4, starting transfers between devices, swap(): return lax.all_to_all(x, axis, split_axis=0, concat_axis=0, tiled=True)  24.5 us
    ppermute x25, waiting for transfers between devices, trade(): lax.ppermute(x, axis, [(i, i ^ by) for i in range(count)])  23.5 us
    pallas_call x1, Pallas kernels, expert(): pl.pallas_call(expert_kernel, grid=(steps,), in_specs=[SMEM] + [whole(x)...  21 us
    pallas_call x1, Pallas kernels, expert_grads(): pl.pallas_call(expert_grads_kernel, grid=(2 * half,), in_specs=[SMEM, who...  18.7 us
    ppermute x4, waiting for transfers between devices, shift(): return lax.ppermute(x, 'seq', [(i, (i + by) % count) for i in range(count)])  9.01 us
  transfers between devices with their start and end apart: 36, of which 12 were waited for; matrix products, arithmetic and copies ran while one was open for 3% of the time, Pallas kernels for 46%

commit v1 on v0

--- a/solution.py
+++ b/solution.py
@@ -302,8 +302,9 @@
     return jnp.where((keys <= queries) & (keys + start < length), scores, LOWEST)
 
 
-def attend_kernel(meta, qkv, *refs):
-    out, lse, top, total, acc = refs[-5:]
+def attend_kernel(meta, qkv, out, lse, kept, top, total, acc, sem):
+    copy = pltpu.make_async_copy(qkv, kept, sem)
+    copy.start()
     rows = qkv.shape[2]
     part = qkv.shape[1] // 3
     heads = part // HEAD_DIM
@@ -338,32 +339,47 @@
         for h, (at, _, _) in enumerate(spans):
             out[block, at] = (acc[at] / total[h : h + 1]).astype(BF16)
             lse[block, h : h + 1] = top[h : h + 1] + jnp.log(total[h : h + 1])
+    copy.wait()
 
 
 def attend(meta, qkv):
     _, width, rows = qkv.shape
     part = width // 3
-    results = [((SEQS, part, rows), BF16), ((SEQS, 8, rows), F32)]
-    scratch = [
-        pltpu.VMEM((8, rows), F32),
-        pltpu.VMEM((8, rows), F32),
-        pltpu.VMEM((part, rows), F32),
-    ]
-    inputs = [(qkv, VMEM)]
-    return one_step(attend_kernel, 0.1, meta, inputs, results, scratch, mib=20)
+    results = [sds((SEQS, part, rows), BF16), sds((SEQS, 8, rows), F32)]
+    return pl.pallas_call(
+        attend_kernel,
+        grid=(1,),
+        in_specs=[SMEM, VMEM],
+        out_specs=[whole(x) for x in results] + [ANY],
+        out_shape=[hbm(x.shape, x.dtype) for x in (*results, qkv)],
+        scratch_shapes=[
+            pltpu.VMEM((8, rows), F32),
+            pltpu.VMEM((8, rows), F32),
+            pltpu.VMEM((part, rows), F32),
+            pltpu.SemaphoreType.DMA,
+        ],
+        compiler_params=params(20, 1),
+        cost_estimate=took(0.1),
+        name="attend",
+    )(meta, qkv)
 
 
 def attend_back_kernel(meta, qkv, *refs):
-    dout, out, lse, cosine, sine, normed = refs[:6]
-    dproj = refs[-8 - SEQS : -8]
-    kept, gone, dq, dk, dv, dots, normed_held, sem = refs[-8:]
+    dout, out, lse, cosine, sine, dlogits, grad_vec, dgain, prior_hits = refs[:9]
+    later = refs[9:13]
+    dproj = refs[-11 - SEQS : -11]
+    kept, gone, dq, dk, dv, dots, *ready, sems = refs[-11:]
     blocks, width, rows = qkv.shape
     part = width // 3
     heads = part // HEAD_DIM
     length = meta[0]
 
-    normed_copy = pltpu.make_async_copy(normed, normed_held, sem)
-    normed_copy.start()
+    copies = [
+        pltpu.make_async_copy(a, b, sems.at[k]) for k, (a, b) in enumerate(zip(later, ready))
+    ]
+    for copy in copies:
+        copy.start()
+    normed_held, att, dlow, moe = ready
 
     def pair(q, k, diagonal):
         for h in range(heads):
@@ -420,28 +436,50 @@
                 dproj[to][at + HALF : at + HEAD_DIM] = (y * c - x * s).astype(BF16)
         dproj[to][2 * part :] = dv[b].astype(BF16)
 
-    normed_copy.wait()
+    for copy in copies:
+        copy.wait()
+    pairs, shard, wide = kept.shape
+    model = att.shape[0]
+    even = meta[2] == 0
+
+    def halves(x, at):
+        x = x.reshape(pairs, 2 * shard, x.shape[1])
+        first, second = x[:, :shard], x[:, shard:]
+        kept[:, :, at : at + x.shape[2]] = jnp.where(even, first, second).astype(BF16)
+        gone[:, :, at : at + x.shape[2]] = jnp.where(even, second, first).astype(BF16)
+
+    halves(mm(att[...], dlow[...]), 0)
+    high, rest = two_parts(dlogits[...])
+    result = mm(moe[...], high, 0, 0) + mm(moe[...], rest, 0, 0)
+    result += pltpu.roll(grad_vec[...], NE + 2 * NC, 1)
+    lanes = lane_of(result.shape)
+    column = jnp.transpose(jnp.broadcast_to(dgain[...], (LANES, model)))
+    result += jnp.where(lanes == NE + 3 * NC, column, 0.0)
+    table = mm(prior_hits[...], high, 0, 0) + mm(prior_hits[...], rest, 0, 0)
+    table = jnp.where(lane_of((NE, LANES)) < NE, table[:NE], 0.0)
+    high, rest = two_parts(table)
+    block = pltpu.roll(high.astype(F32), 2 * NE, 1) + pltpu.roll(rest.astype(F32), 3 * NE, 1)
+    block = jnp.concatenate([block, jnp.zeros((shard - NE, LANES), F32)], axis=0)
+    result = result.reshape(2 * pairs, shard, LANES) + block[None]
+    halves(result.reshape(model, LANES), model)
     total = mm(dproj[0][...], normed_held[around(meta, 0)])
     for to in range(1, SEQS):
         total += mm(dproj[to][...], normed_held[around(meta, to)])
-    pairs, shard, _ = kept.shape
-    total = jnp.transpose(total).reshape(pairs, 2 * shard, width)
-    even = meta[2] == 0
-    kept[...] = jnp.where(even, total[:, :shard], total[:, shard:]).astype(BF16)
-    gone[...] = jnp.where(even, total[:, shard:], total[:, :shard]).astype(BF16)
-
-
-def attend_back(meta, before, qkv, dout, out, lse, cosine, sine, normed, count):
+    total = [jnp.transpose(total), jnp.zeros((model, wide - model - LANES - width), F32)]
+    halves(jnp.concatenate(total, axis=1), model + LANES)
+
+
+def attend_back(meta, before, qkv, dout, out, lse, cosine, sine, few, later, count):
     blocks, width, rows = qkv.shape
     part = width // 3
-    model = normed.shape[2]
-    scratch = [pltpu.VMEM((blocks, part, rows), F32)] * 3
-    scratch += [pltpu.VMEM((blocks, 8, rows), F32), pltpu.VMEM(normed.shape, BF16)]
-    scratch += [pltpu.SemaphoreType.DMA]
-    inputs = [*come(qkv, dout), out, lse, cosine, sine, (far(normed), ANY)]
+    model = later[1].shape[0]
+    scratch = [pltpu.VMEM((blocks, part, rows), F32)] * 3 + [pltpu.VMEM((blocks, 8, rows), F32)]
+    scratch += [pltpu.VMEM(x.shape, BF16) for x in later] + [pltpu.SemaphoreType.DMA((4,))]
+    inputs = [qkv, *come(dout), out, lse, cosine, sine, *few, *((far(x), ANY) for x in later)]
+    wide = -(-(model + LANES + width) // LANES) * LANES
     results = [((width, rows), BF16)] * SEQS
-    results += [((count // 2, model // count, width), BF16)] * 2
-    return one_step(attend_back_kernel, 100, meta, inputs, results, scratch, before, 48)
+    results += [((count // 2, model // count, wide), BF16)] * 2
+    return one_step(attend_back_kernel, 12, meta, inputs, results, scratch, before, 48)
 
 
 def route_kernel(meta, att, out_w, small_w, tok, prior, slots, *refs):
@@ -540,18 +578,28 @@
 def expert_kernel(meta, *refs):
     sent, grads = refs[:SEQS], refs[SEQS : 2 * SEQS]
     gate_w, up_w, out_w = refs[2 * SEQS + 1 : 2 * SEQS + 4]
-    back = refs[2 * SEQS + 4 : 3 * SEQS + 4]
-    rows, scaled, gate, hidden, dgate, dup, held, acc, dots = refs[3 * SEQS + 4 :]
+    back, branch = refs[2 * SEQS + 4 : 3 * SEQS + 4], refs[3 * SEQS + 4]
+    in_kept, in_sent, out_kept, out_sent = refs[3 * SEQS + 5 : 3 * SEQS + 9]
+    rows, flipped, held, scaled, gate, hidden, dgate, dup, acc, mixed_acc, dots = refs[-11:]
     step = pl.program_id(0)
     count, model = rows.shape
     block = gate_w.shape[1]
     me = meta[1]
+    even = meta[2] == 0
+
+    def split(x, kept, gone):
+        pairs, shard, wide = kept.shape
+        x = x.reshape(pairs, 2 * shard, wide)
+        first, second = x[:, :shard], x[:, shard:]
+        kept[...] = jnp.where(even, first, second).astype(BF16)
+        gone[...] = jnp.where(even, second, first).astype(BF16)
 
     @pl.when(step == 0)
     def _():
         for s in range(SEQS):
             at = slice(s * CAP, (s + 1) * CAP)
             rows[at] = sent[s][:, :model]
+            flipped[:, at] = jnp.transpose(sent[s][:, :model])
             held[at] = grads[s][...]
             parts = sent[s][:, model:].astype(F32)
             lanes = lane_of(parts.shape)
@@ -560,6 +608,7 @@
             gate[at] = jnp.broadcast_to(share, (CAP, LANES))
             scaled[at] = (grads[s][...].astype(F32) * share).astype(BF16)
         acc[...] = jnp.zeros_like(acc)
+        mixed_acc[...] = jnp.zeros_like(mixed_acc)
         dots[...] = jnp.zeros_like(dots)
 
     for at in (slice(0, count // 2), slice(count // 2, count)):
@@ -581,6 +630,11 @@
         dgate[at] = dg
         dup[at] = du
         acc[at] += mm(dg, gate_w[...], 1, 1) + mm(du, up_w[...], 1, 1)
+        mixed_acc[at] += mm(low, out_w[...])
+
+    split(mm(flipped[...], dgate[...]), in_kept.at[0, 0], in_sent.at[0, 0])
+    split(mm(flipped[...], dup[...]), in_kept.at[0, 1], in_sent.at[0, 1])
+    split(mm(hidden[...], scaled[...], 0, 0), out_kept, out_sent)
 
     @pl.when(step == pl.num_programs(0) - 1)
     def _():
@@ -594,18 +648,19 @@
                 jnp.where(lanes == me, high.astype(F32), 0.0)
                 + jnp.where(lanes == me + NE, rest.astype(F32), 0.0)
             ).astype(BF16)
-
-
-def expert(meta, sent, grads, before, weights, w_out, block):
+            branch[around(meta, s)] = (mixed_acc[at] * gate[at, 0:1]).astype(BF16)
+
+
+def expert(meta, sent, grads, before, weights, w_out, block, fsdp):
     count, model = SEQS * CAP, grads[0].shape[1]
     inner = w_out.shape[0]
     steps = inner // block
     skip = (model + 2 * LANES) // block
-    results = [sds(sent[0].shape, BF16)] * SEQS + [
-        sds((count, model), BF16),
-        sds((count, model), BF16),
-        sds((count, LANES), F32),
-    ]
+    pairs, in_rows, out_rows = fsdp // 2, model // fsdp, inner // fsdp
+    per = block // (2 * out_rows)
+    results = [sds(sent[0].shape, BF16)] * SEQS + [sds((SEQS, CAP, model), BF16)]
+    in_spec = pl.BlockSpec((1, 2, pairs, in_rows, block), lambda i: (i, 0, 0, 0, 0))
+    out_spec = pl.BlockSpec((per, out_rows, model), lambda i: (i, 0, 0))
     return pl.pallas_call(
         expert_kernel,
         grid=(steps,),
@@ -617,99 +672,27 @@
             pl.BlockSpec((model, block), lambda i: (0, i + skip + steps)),
             pl.BlockSpec((block, model), lambda i: (i, 0)),
         ],
-        out_specs=[whole(x) for x in results]
-        + [pl.BlockSpec((count, block), lambda i: (0, i))] * 3,
-        out_shape=[hbm(r.shape, r.dtype) for r in results] + [hbm((count, inner), BF16)] * 3,
+        out_specs=[whole(x) for x in results] + [in_spec, in_spec, out_spec, out_spec],
+        out_shape=[hbm(r.shape, r.dtype) for r in results]
+        + [hbm((steps, 2, pairs, in_rows, block), BF16)] * 2
+        + [hbm((pairs, out_rows, model), BF16)] * 2,
         scratch_shapes=[
             pltpu.VMEM((count, model), BF16),
+            pltpu.VMEM((model, count), BF16),
+            pltpu.VMEM((count, model), BF16),
+            pltpu.VMEM((count, model), BF16),
+            pltpu.VMEM((count, LANES), F32),
+            pltpu.VMEM((count, block), BF16),
+            pltpu.VMEM((count, block), BF16),
+            pltpu.VMEM((count, block), BF16),
+            pltpu.VMEM((count, model), F32),
             pltpu.VMEM((count, model), F32),
             pltpu.VMEM((count, LANES), F32),
         ],
-        compiler_params=params(24, 1),
+        compiler_params=params(52, 1),
         cost_estimate=took(10),
         name="expert",
     )(meta, *sent, *grads, *map(far, (before, weights, weights, w_out)))
-
-
-def expert_grads_kernel(
-    meta, rows, scaled, gate, hidden, dgate, dup, out_w, before, *refs
-):
-    in_kept, in_sent, out_kept, out_sent = refs[:4]
-    branch, (flipped, acc) = refs[4 : SEQS + 4], refs[SEQS + 4 :]
-    step = pl.program_id(0)
-    half = pl.num_programs(0) // 2
-    even = meta[2] == 0
-
-    def halves(x, kept, sent):
-        pairs, shard, wide = kept.shape
-        x = x.reshape(pairs, 2 * shard, wide)
-        first, second = x[:, :shard], x[:, shard:]
-        kept[...] = jnp.where(even, first, second).astype(BF16)
-        sent[...] = jnp.where(even, second, first).astype(BF16)
-
-    @pl.when(step == 0)
-    def _():
-        for s in range(SEQS):
-            flipped[:, s * CAP : (s + 1) * CAP] = jnp.transpose(rows[s * CAP : (s + 1) * CAP])
-        acc[...] = jnp.zeros_like(acc)
-
-    @pl.when(step < half)
-    def _():
-        halves(mm(flipped[...], dgate[...]), in_kept, in_sent)
-        halves(mm(hidden[...], scaled[...], 0, 0), out_kept, out_sent)
-
-    @pl.when(step >= half)
-    def _():
-        halves(mm(flipped[...], dup[...]), in_kept, in_sent)
-        acc[...] += mm(hidden[...], out_w[...])
-
-    @pl.when(step == pl.num_programs(0) - 1)
-    def _():
-        for s in range(SEQS):
-            at = slice(s * CAP, (s + 1) * CAP)
-            branch[s][...] = (acc[at] * gate[at, 0:1]).astype(BF16)
-
-
-def expert_grads(meta, rows, scaled, gate, hidden, dgate, dup, w_out, before, block, fsdp):
-    count, model = scaled.shape
-    inner = w_out.shape[0]
-    half = inner // block
-    pairs = fsdp // 2
-    in_rows, out_rows = model // fsdp, inner // fsdp
-    per = block // (2 * out_rows)
-
-    def low(i):
-        return jnp.minimum(i, half - 1)
-
-    def high(i):
-        return jnp.maximum(i - half, 0)
-
-    in_spec = pl.BlockSpec((pairs, in_rows, block), lambda i: (0, 0, i))
-    out_spec = pl.BlockSpec((per, out_rows, model), lambda i: (low(i), 0, 0))
-    return pl.pallas_call(
-        expert_grads_kernel,
-        grid=(2 * half,),
-        in_specs=[
-            SMEM,
-            whole(rows),
-            whole(scaled),
-            whole(gate),
-            pl.BlockSpec((count, block), lambda i: (0, lax.rem(i, half))),
-            pl.BlockSpec((count, block), lambda i: (0, low(i))),
-            pl.BlockSpec((count, block), lambda i: (0, high(i))),
-            pl.BlockSpec((block, model), lambda i: (high(i), 0)),
-            ANY,
-        ],
-        out_specs=[in_spec, in_spec, out_spec, out_spec]
-        + [pl.BlockSpec((CAP, model), lambda i: (0, 0))] * SEQS,
-        out_shape=[hbm((pairs, in_rows, 2 * inner), BF16)] * 2
-        + [hbm((pairs, out_rows, model), BF16)] * 2
-        + [hbm((CAP, model), BF16)] * SEQS,
-        scratch_shapes=[pltpu.VMEM((model, count), BF16), pltpu.VMEM((count, model), F32)],
-        compiler_params=params(24, 1),
-        cost_estimate=took(100),
-        name="expert_grads",
-    )(meta, *map(far, (rows, scaled, gate, hidden, dgate, dup, w_out, before)))
 
 
 def split_again(small):
@@ -722,16 +705,21 @@
 
 
 def add_cores_kernel(in_a, in_b, out_a, out_b, *refs):
-    shard, wide = in_a.shape[1:]
-    for k in range(in_a.shape[0]):
+    blocks, _, _, shard, block = in_a.shape
+    wide = 2 * blocks * block
+    for k in range(in_a.shape[2]):
         both = refs[-1].at[k]
-        both[:, :wide] = (in_a[k].astype(F32) + in_b[k].astype(F32)).astype(BF16)
+        for j in range(2 * blocks):
+            at = (j % blocks, j // blocks, k)
+            total = in_a[at].astype(F32) + in_b[at].astype(F32)
+            both[:, j * block : (j + 1) * block] = total.astype(BF16)
         more = out_a[k].astype(F32) + out_b[k].astype(F32)
         both[:, wide:] = tiles_moved(more, shard, both.shape[1] - wide).astype(BF16)
 
 
 def add_cores(parts, *before):
-    pairs, shard, wide = parts[0].shape
+    blocks, _, pairs, shard, block = parts[0].shape
+    wide = 2 * blocks * block
     more = parts[2].shape[1] * parts[2].shape[2] // shard
 
     def some(shape):
@@ -740,32 +728,29 @@
     return pl.pallas_call(
         add_cores_kernel,
         grid=(pairs // SIDE,),
-        in_specs=[some(x.shape[1:]) for x in parts] + [ANY] * len(before),
+        in_specs=[pl.BlockSpec((blocks, 2, SIDE, shard, block), lambda i: (0, 0, i, 0, 0))] * 2
+        + [some(x.shape[1:]) for x in parts[2:]]
+        + [ANY] * len(before),
         out_specs=some((shard, wide + more)),
         out_shape=hbm((pairs, shard, wide + more), BF16),
         compiler_params=params(24, 1),
-        cost_estimate=took(100),
+        cost_estimate=took(0.1),
         name="add_cores",
     )(*[x if k % 2 else far(x) for k, x in enumerate(parts)], *map(far, before))
 
 
-def add_dense_kernel(meta, dense_a, dense_b, heads_a, heads_b, out):
-    pairs, shard, wide = dense_a.shape
-    width, model = heads_a.shape[2], wide - LANES
+def add_dense_kernel(meta, kept, other, out):
+    pairs, shard, wide = kept.shape
+    model = 2 * pairs * shard
     for k in range(pairs):
-        total = dense_a[k].astype(F32) + dense_b[k].astype(F32)
-        out[k, :, :model] = total[:, :model].astype(BF16)
-        out[k, :, model:wide] = split_again(total[:, model:]).astype(BF16)
-        heads = heads_a[k].astype(F32) + heads_b[k].astype(F32)
-        rest = jnp.zeros((shard, out.shape[2] - wide - width), F32)
-        out[k, :, wide:] = jnp.concatenate([heads, rest], axis=1).astype(BF16)
-
-
-def add_dense(meta, kept, come_dense, heads, come_heads):
-    pairs, shard, wide = kept.shape
-    results = [((pairs, shard, -(-(wide + heads.shape[2]) // LANES) * LANES), BF16)]
-    inputs = [kept, *come(come_dense), heads, *come(come_heads)]
-    return one_step(add_dense_kernel, 0.1, meta, inputs, results, mib=24)[0]
+        total = kept[k].astype(F32) + other[k].astype(F32)
+        out[k] = total.astype(BF16)
+        out[k, :, model : model + LANES] = split_again(total[:, model : model + LANES]).astype(BF16)
+
+
+def add_dense(meta, kept, other):
+    inputs = [kept, *come(other)]
+    return one_step(add_dense_kernel, 0.1, meta, inputs, [(kept.shape, BF16)], mib=24)[0]
 
 
 def add_pieces_kernel(meta, pieces, *refs):
@@ -774,9 +759,9 @@
         total += pieces[k].astype(F32)
     model = pieces.shape[0] * pieces.shape[1] * 2
     small = split_again(total[:, model : model + LANES])
-    refs[-1][:, :model] = total[:, :model].astype(BF16)
-    refs[-1][:, model : model + LANES] = small.astype(BF16)
-    refs[-1][:, model + LANES :] = total[:, model + LANES :].astype(BF16)
+    parts = [total[:, :model], small, total[:, model + LANES :]]
+    total = jnp.concatenate(parts, axis=1).astype(BF16)
+    refs[-1][...] = total
 
 
 def add_pieces(meta, pieces, *before):
@@ -786,25 +771,21 @@
 
 def mixed_kernel(meta, partial, slots, *refs):
     result = partial[...]
-    for s in range(SEQS):
-        result += mm(slots[around(meta, s)], refs[s][...], 0, 0)
+    for e in range(EF):
+        result += mm(slots[e], refs[0][e], 0, 0)
     refs[-1][...] = result.astype(BF16)
 
 
 def mixed(meta, partial, slots, branch, *before):
     results = [(partial.shape, BF16)]
-    (out,) = one_step(mixed_kernel, 0.1, meta, [partial, slots, *come(*branch)], results, (), before)
+    (out,) = one_step(mixed_kernel, 0.1, meta, [partial, slots, *come(branch)], results, (), before)
     return out
 
 
 def unroute_kernel(meta, *refs):
     back = refs[:SEQS]
     out_w, small_w, slots, resid, small, stats, grad, vectors = refs[SEQS : SEQS + 8]
-    att, moe, grad_vec, prior_hits = refs[SEQS + 8 : SEQS + 12]
-    datt = refs[-4]
-    dres, kept, sent = refs[-3:]
-    pairs, shard, _ = kept.shape
-    even = meta[2] == 0
+    datt, dres, dlow, dlogits, dgain = refs[-5:]
     gain = vectors[NC : NC + 1]
     rows, model = resid.shape
     held, local = stats[...], small[...]
@@ -827,37 +808,26 @@
     res = resid[...]
     factor = lax.rsqrt(jnp.mean(res * res, axis=-1, keepdims=True) + EPS)
     normal = res * factor
-    dgain = jnp.sum(dn * normal, axis=0, keepdims=True)
+    dgain[...] = jnp.sum(dn * normal, axis=0, keepdims=True)
+    dlogits[...] = dsmall
     scaled = dn * gain
     out = g + factor * (scaled - normal * jnp.mean(scaled * normal, axis=-1, keepdims=True))
     dres[...] = out
     low = out.astype(BF16)
+    dlow[...] = low
     datt[...] = mm(out_w[...], low, 1, 1).astype(BF16)
-    full = mm(att[...], low).reshape(pairs, 2 * shard, model)
-    kept[:, :, :model] = jnp.where(even, full[:, :shard], full[:, shard:]).astype(BF16)
-    sent[:, :, :model] = jnp.where(even, full[:, shard:], full[:, :shard]).astype(BF16)
-    result = mm(moe[...], high, 0, 0) + mm(moe[...], rest, 0, 0)
-    result += pltpu.roll(grad_vec[...], NE + 2 * NC, 1)
-    lanes = lane_of(result.shape)
-    column = jnp.transpose(jnp.broadcast_to(dgain, (LANES, model)))
-    result += jnp.where(lanes == NE + 3 * NC, column, 0.0)
-    table = mm(prior_hits[...], high, 0, 0) + mm(prior_hits[...], rest, 0, 0)
-    table = jnp.where(lane_of((NE, LANES)) < NE, table[:NE], 0.0)
-    high, rest = two_parts(table)
-    block = pltpu.roll(high.astype(F32), 2 * NE, 1) + pltpu.roll(rest.astype(F32), 3 * NE, 1)
-    block = jnp.concatenate([block, jnp.zeros((shard - NE, LANES), F32)], axis=0)
-    full = result.reshape(pairs, 2 * shard, LANES)
-    first, second = full[:, :shard] + block[None], full[:, shard:] + block[None]
-    kept[:, :, model:] = jnp.where(even, first, second).astype(BF16)
-    sent[:, :, model:] = jnp.where(even, second, first).astype(BF16)
-
-
-def unroute(meta, before, back, weights, tokenwise, att, moe, grad_vec, prior_hits, count):
-    resid = tokenwise[1]
-    rows, model = resid.shape
-    inputs = [*come(*back), *weight_blocks(weights), *tokenwise, att, moe, grad_vec, prior_hits]
-    results = [((model, rows), BF16), ((rows, model), F32)]
-    results += [((count // 2, model // count, model + LANES), BF16)] * 2
+
+
+def unroute(meta, before, back, weights, tokenwise):
+    rows, model = tokenwise[1].shape
+    inputs = [*come(*back), *weight_blocks(weights), *tokenwise]
+    results = [
+        ((model, rows), BF16),
+        ((rows, model), F32),
+        ((rows, model), BF16),
+        ((rows, LANES), F32),
+        ((1, model), F32),
+    ]
     return one_step(unroute_kernel, 100, meta, inputs, results, (), before, 32)
 
 
@@ -882,7 +852,7 @@
     scratch = [pltpu.VMEM((SEQS * width, rows), BF16)]
     results = [(tok.shape, BF16)]
     inputs = [*come(*dproj), weight, tok, gain, dres]
-    return one_step(finish_kernel, 0.1, meta, inputs, results, scratch, before, 24)[0]
+    return one_step(finish_kernel, 10, meta, inputs, results, scratch, before, 24)[0]
 
 
 def gather_kernel(meta, *refs):
@@ -1014,50 +984,45 @@
     qkv, normed = project(
         meta, [tok, left, right, far0, far1], first_all, gain_a, cosine, sine, width
     )
-    held, lse = attend(meta, qkv)
+    held, lse, qkv = attend(meta, qkv)
     held, *grad_rows = lax.optimization_barrier((held, *grad_rows))
     att = swap(held, "seq").reshape(model, rows)
     *sent, resid, moe, stats, vectors = route(meta, att, weights, tok, prior, slots)
     sent = trades(sent)
     partial, small, grad_vec = local_part(meta, resid, stats, grad, vectors)
 
-    *back, row, scaled, gate, hidden, dgate, dup = expert(
-        meta, sent, grad_rows, small, weights, w_out, 512
-    )
-    back = trades(back)
-    in_kept, in_sent, out_kept, out_sent, *branch = expert_grads(
-        meta, row, scaled, gate, hidden, dgate, dup, w_out, back_w, 512, fsdp
-    )
+    *results, in_kept, in_sent, out_kept, out_sent = expert(
+        meta, sent, grad_rows, small, weights, w_out, 512, fsdp
+    )
+    back, branch = trades(results[:seqs]), swap(results[seqs], "seq")
     in_come, out_come = trade(in_sent, 1, "core"), trade(out_sent, 1, "core")
-    tokenwise = (slots, resid, small, stats, grad, vectors)
-    datt, dres, kept, gone = unroute(
-        meta, (in_kept,), back, weights, tokenwise, att, moe, grad_vec, prior_hits, fsdp
-    )
-    come_dense = trade(gone, 1, "core")
-    dout = swap(datt.reshape(seqs, group, rows), "seq")
-    both = add_cores((in_kept, in_come, out_kept, out_come), dres)
-    both, *branch = lax.optimization_barrier((both, *branch))
-    branch = trades(branch)
+    both = add_cores((in_kept, in_come, out_kept, out_come), back_w)
     part = both.reshape(-1, both.shape[2])
     part = lax.psum_scatter(part, YZ, scatter_dimension=0, tiled=True)
-    *dproj, heads, gone = attend_back(
-        meta, (both, come_dense), qkv, dout, held, lse, cosine, sine, normed, fsdp
-    )
-    mixed_out = mixed(meta, partial, slots, branch, heads)
-    gone, mixed_out, *dproj = lax.optimization_barrier((gone, mixed_out, *dproj))
-    come_heads = trade(gone, 1, "core")
+    tokenwise = (slots, resid, small, stats, grad, vectors)
+    datt, dres, dlow, dlogits, dgain_m = unroute(meta, (both,), back, weights, tokenwise)
+    dout = swap(datt.reshape(seqs, group, rows), "seq")
+    mixed_out = mixed(meta, partial, slots, branch, dres)
+    few = (dlogits, grad_vec, dgain_m, prior_hits)
+    *dproj, kept, gone = attend_back(
+        meta, (mixed_out,), qkv, dout, held, lse, cosine, sine, few, (normed, att, dlow, moe), fsdp
+    )
+    other = trade(gone, 1, "core")
     back_all = trades(dproj)
-    dense = add_dense(meta, kept, come_dense, heads, come_heads)
+    dense = add_dense(meta, kept, other)
     dense = swap(dense, YZ)
-    dense = add_pieces(meta, dense)
-    grad_tokens = finish(meta, back_all, back_w, tok, gain_a, dres, dense)
+    part, back_all[2] = lax.optimization_barrier((part, back_all[2]))
+    pieces = trades([part] * seqs)
+    grad_tokens = finish(meta, back_all, back_w, tok, gain_a, dres)
+    dense = add_pieces(meta, dense, grad_tokens)
+    dense, *pieces = lax.optimization_barrier((dense, *pieces))
+    dense = trades([dense] * seqs)
     grad_attend_in, grad_gain_a, grad_att_out, *rest, table = gather_dense(
-        meta, trades([dense] * seqs), attend_in, gain_attend[None]
+        meta, dense, attend_in, gain_attend[None]
     )
     grad_router, grad_mix, grad_vector, grad_gain_m = rest
-    part, grad_tokens, grad_gain_a = lax.optimization_barrier((part, grad_tokens, grad_gain_a))
     grad_in, grad_out = gather(
-        meta, trades([part] * seqs), 2 * inner, expert_out.shape[1], model
+        meta, pieces, 2 * inner, expert_out.shape[1], model
     )
     return (
         mixed_out[None],

time: 297 us -> 285 us (0.960)
  the two profiles are of different devices: /device:TPU:0 before, /device:TPU:64 now
where the time goes in v1:
time: 285 us; the launch traced here: 279 us
  Pallas kernels  133 us (47%)
  starting transfers between devices  61.6 us (22%)
  waiting for transfers between devices  59.7 us (21%)
  between operations  14.9 us (5%)
  local copies, waits for them, and re-layouts  8.41 us (3%)
    pallas_call x12, Pallas kernels, one_step(): pl.pallas_call(body, grid=(1,), in_specs=[SMEM] + [spec for _, spec in in...  76.1 us
    pallas_call x1, Pallas kernels, expert(): pl.pallas_call(expert_kernel, grid=(steps,), in_specs=[SMEM] + [whole(x)...  31.1 us
    ppermute x21, starting transfers between devices, trade(): lax.ppermute(x, axis, [(i, i ^ by) for i in range(count)])  28.9 us
    ppermute x21, waiting for transfers between devices, trade(): lax.ppermute(x, axis, [(i, i ^ by) for i in range(count)])  28.6 us
    all_to_all x5, starting transfers between devices, swap(): return lax.all_to_all(x, axis, split_axis=0, concat_axis=0, tiled=True)  25.4 us
    all_to_all x5, waiting for transfers between devices, swap(): return lax.all_to_all(x, axis, split_axis=0, concat_axis=0, tiled=True)  21.3 us
    pallas_call x1, Pallas kernels, attend(): pl.pallas_call(attend_kernel, grid=(1,), in_specs=[SMEM, VMEM], out_specs...  16.2 us
    ppermute x4, waiting for transfers between devices, shift(): return lax.ppermute(x, 'seq', [(i, (i + by) % count) for i in range(count)])  9.47 us
  transfers between devices with their start and end apart: 33, of which 13 were waited for; matrix products, arithmetic and copies ran while one was open for 3% of the time, Pallas kernels for 46%

profile of v1, /device:TPU:64, one launch (start us, length us, event | category | flops | bytes accessed | tf_op | source)
XLA Modules:
  0.0 279.5 jit_solution(14580289379482657852)
XLA Ops:
  8.0 3.3 %pack.1 = (bf16[32,24,640]{2,1,0:T(8,128)(2,1)}, bf16[24,7168]{1,0:T(8,128)(2,1)}, bf16[24,2304]{1,0:T(8,128)(2,1)}) custom-call(s32[5]{0:T(128)S(1)} %stack.19.meta, f32[24,2304]{1,0:T(8,128)} %refs_4_.1, f32[1,24]{1,0:T(1,128)} %bitcast.52, f32[24,768]{1,0:T(8,128)} %attend_out.1, f32[8,24]{1,0:T(8,128)} %bitcast.55, f32[4,24]{1,0:T(4,128)} %bitcast.59, ...), custom_call_target="tpu_custom_call" | custom-call | flops 2200000000 | bytes 65536 | tf_op jit(solution)/shard_map/pack/pallas_call | solution.py:205
  11.3 1.6 collective-permute-start
  12.8 1.7 collective-permute-start.1
  14.6 7.8 %all-to-all-start = ((bf16[32,24,640]{2,1,0:T(8,128)(2,1)}), bf16[32,24,640]{2,1,0:T(8,128)(2,1)S(1)}, u32[]{:S(2)}, u32[]{:S(2)}) async-start(bf16[32,24,640]{2,1,0:T(8,128)(2,1)} %get-tuple-element.93), calls=%async_computation | async-start | bytes 1966080 | tf_op jit(solution)/shard_map/all_to_all | solution.py:105
  22.4 9.5 %collective-permute-done.refs_1_ = bf16[512,768]{1,0:T(8,128)(2,1)S(1)} collective-permute-done((bf16[512,768]{1,0:T(8,128)(2,1)S(1)}, bf16[512,768]{1,0:T(8,128)(2,1)S(1)}, u32[]{:S(2)}, u32[]{:S(2)}) %collective-permute-start) | collective-permute-done | bytes 786464 | tf_op jit(solution)/shard_map/ppermute | solution.py:88
  31.8 0.8 slice.16
  32.6 0.3 collective-permute-start.2
  32.9 0.8 slice.17
  33.7 3.0 %collective-permute-start.3 = (bf16[256,768]{1,0:T(8,128)(2,1)}, bf16[256,768]{1,0:T(8,128)(2,1)}, u32[]{:S(2)}, u32[]{:S(2)}) collective-permute-start(bf16[256,768]{1,0:T(8,128)(2,1)} %slice.17), channel_id=1, source_target_pairs={{0,96},{32,0},{64,32},{96,64},{1,97},{33,1},{65,33},{97,65},{2,98}... | collective-permute-start | bytes 1179656 | tf_op jit(solution)/shard_map/ppermute | solution.py:88
  36.7 3.5 %plan.1 = (bf16[4,192,512]{2,1,0:T(8,128)(2,1)}, bf16[512,768]{1,0:T(8,128)(2,1)}, f32[512,128]{1,0:T(8,128)}, bf16[512,128]{1,0:T(8,128)(2,1)}, bf16[192,768]{1...) custom-call(s32[5]{0:T(128)S(1)} %stack.19.meta, ...), custom_call_target="tpu_custom_call" | custom-call | flops 1100000000 | bytes 65536 | tf_op jit(solution)/shard_map/plan/pallas_call | solution.py:73
  40.2 1.8 multiply_sine_fusion
  42.0 1.8 collective-permute-start.5
  43.8 3.1 %collective-permute-start.6 = (bf16[192,768]{1,0:T(8,128)(2,1)}, bf16[192,768]{1,0:T(8,128)(2,1)}, u32[]{:S(2)}, u32[]{:S(2)}) collective-permute-start(bf16[192,768]{1,0:T(8,128)(2,1)} %get-tuple-element.99), channel_id=1, source_target_pairs={{0,96},{32,64},{64,32},{96,0},{1,97},{33,65},{65,33},{97,1},{2,98}... | collective-permute-start | bytes 884744 | tf_op jit(solution)/shard_map/ppermute | solution.py:93
  47.2 6.3 %project.1 = (bf16[4,576,512]{2,1,0:T(8,128)(2,1)S(1)}, bf16[4,512,768]{2,1,0:T(8,128)(2,1)}) custom-call(s32[5]{0:T(128)S(1)} %stack.19.meta, bf16[512,768]{1,0:T(8,128)(2,1)S(1)} %bitcast.46, bf16[512,768]{1,0:T(8,128)(2,1)S(1)} %collective-permute-done.refs_1_, bf16[512,768]{1,0:T(8,128)(2,1)S(1)} %collective-permute-done.1.refs_2_, ...), custom_call_target="tpu_custom_call" | custom-call | flops 109999996928 | bytes 65536 | tf_op jit(solution)/shard_map/project/pallas_call | solution.py:73
  53.5 16.2 %attend.1 = (bf16[4,192,512]{2,1,0:T(8,128)(2,1)}, f32[4,8,512]{2,1,0:T(8,128)}, bf16[4,576,512]{2,1,0:T(8,128)(2,1)}) custom-call(s32[5]{0:T(128)S(1)} %stack.19.meta, bf16[4,576,512]{2,1,0:T(8,128)(2,1)S(1)} %get-tuple-element.94.qkv), custom_call_target="tpu_custom_call" | custom-call | flops 110000000 | bytes 65536 | tf_op jit(solution)/shard_map/attend/pallas_call | solution.py:349
  69.7 3.5 %all-to-all-start.1 = ((bf16[4,192,512]{2,1,0:T(8,128)(2,1)}), bf16[4,192,512]{2,1,0:T(8,128)(2,1)S(1)}, u32[]{:S(2)}, u32[]{:S(2)}) async-start(bf16[4,192,512]{2,1,0:T(8,128)(2,1)} %get-tuple-element.100.refs_1_), calls=%async_computation.1 | async-start | bytes 1572864 | tf_op jit(solution)/shard_map/all_to_all | solution.py:105
  73.2 0.5 all-gather.5.cloned.1.call-start
  73.7 0.2 all-gather.5.cloned.1.call-update
  74.0 9.8 %all-to-all-done.1 = bf16[4,192,512]{2,1,0:T(8,128)(2,1)S(1)} async-done(((bf16[4,192,512]{2,1,0:T(8,128)(2,1)}), bf16[4,192,512]{2,1,0:T(8,128)(2,1)S(1)}, u32[]{:S(2)}, u32[]{:S(2)}) %all-to-all-start.1) | async-done | bytes 786464 | tf_op jit(solution)/shard_map/all_to_all | solution.py:105
  83.8 6.2 %route.1 = (bf16[192,896]{1,0:T(8,128)(2,1)}, bf16[192,896]{1,0:T(8,128)(2,1)}, bf16[192,896]{1,0:T(8,128)(2,1)}, bf16[192,896]{1,0:T(8,128)(2,1)}, f32[512,768]...) custom-call(s32[5]{0:T(128)S(1)} %stack.19.meta, bf16[768,512]{1,0:T(8,128)(2,1)S(1)} %bitcast.40, ...), custom_call_target="tpu_custom_call" | custom-call | flops 109999996928 | bytes 65536 | tf_op jit(solution)/shard_map/route/pallas_call | solution.py:73
  90.0 0.6 collective-permute-start.7
  90.6 2.1 collective-permute-start.8
  92.7 2.0 collective-permute-start.9
  94.7 4.0 %slice.19 = bf16[768,2048]{1,0:T(8,128)(2,1)} slice(bf16[768,7168]{1,0:T(8,128)(2,1)} %all-gather.3.cloned.1.call-done.out_w.small_w.refs_9_.refs_10_.refs_4_.refs_5_), slice={[0:768], [5120:7168]} | slice | bytes 6291456 | tf_op jit(solution)/shard_map/slice | solution.py:967
  98.8 5.0 %local_part.1 = (f32[512,768]{1,0:T(8,128)}, f32[512,128]{1,0:T(8,128)}, f32[768,128]{1,0:T(8,128)}) custom-call(s32[5]{0:T(128)S(1)} %stack.19.meta, f32[512,768]{1,0:T(8,128)} %get-tuple-element.104.resid.refs_7_, f32[512,128]{1,0:T(8,128)} %get-tuple-element.105.stats.refs_9_, bf16[512,768]{1,0:T(8,128)(2,1)} %get-tuple-element.106.grad.refs_10_, ...), custom_call_target="tpu_custom_call" | custom-call | flops 110000000 | bytes 65536 | tf_op jit(solution)/shard_map/local_part/pallas_call | solution.py:73
  103.7 1.3 collective-permute-done.8.refs_2_
  105.0 2.6 collective-permute-done.9.refs_3_
  107.6 0.8 copy-done.10
  108.4 31.1 %expert.1 = (bf16[192,896]{1,0:T(8,128)(2,1)}, bf16[192,896]{1,0:T(8,128)(2,1)}, bf16[192,896]{1,0:T(8,128)(2,1)}, bf16[192,896]{1,0:T(8,128)(2,1)}, bf16[4,192,...) custom-call(s32[5]{0:T(128)S(1)} %stack.19.meta, ...), custom_call_target="tpu_custom_call" | custom-call | flops 11000000512 | bytes 65536 | tf_op jit(solution)/shard_map/expert/pallas_call | solution.py:664
  139.6 0.5 collective-permute-start.14
  140.1 3.5 %collective-permute-start.11 = (bf16[192,896]{1,0:T(8,128)(2,1)}, bf16[192,896]{1,0:T(8,128)(2,1)S(1)}, u32[]{:S(2)}, u32[]{:S(2)}) collective-permute-start(bf16[192,896]{1,0:T(8,128)(2,1)} %get-tuple-element.121), channel_id=1, source_target_pairs={{0,64},{32,96},{64,0},{96,32},{1,65},{33,97},{65,1},{97,33},{2,66}... | collective-permute-start | bytes 1032200 | tf_op jit(solution)/shard_map/ppermute | solution.py:93
  143.6 1.2 collective-permute-start.12
  144.8 3.5 %all-to-all-start.2 = ((bf16[4,192,768]{2,1,0:T(8,128)(2,1)}), bf16[4,192,768]{2,1,0:T(8,128)(2,1)S(1)}, u32[]{:S(2)}, u32[]{:S(2)}) async-start(bf16[4,192,768]{2,1,0:T(8,128)(2,1)} %get-tuple-element.118), calls=%async_computation.2 | async-start | bytes 2359296 | tf_op jit(solution)/shard_map/all_to_all | solution.py:105
  148.6 6.1 %add_cores.1.refs_12_ = bf16[16,24,6144]{2,1,0:T(8,128)(2,1)} custom-call(bf16[4,2,16,24,512]{4,3,2,1,0:T(8,128)(2,1)} %get-tuple-element.123.in_a, bf16[4,2,16,24,512]{4,3,2,1,0:T(8,128)(2,1)} %collective-permute-done.13.in_b, bf16[16,64,768]{2,1,0:T(8,128)(2,1)} %get-tuple-element.125.out_a, bf16[16,64,768]{2,1,0:T(8,128)(2,1)S(1)} %collective-permute-done.14.out_b, ...), custom_call_target="tpu_custom_call" | custom-call | flops 110000000 | bytes 65536 | tf_op jit(solution)/shard_map/add_cores/pallas_call | solution.py:728
  154.8 5.3 %collective-permute-done.11.refs_2_ = bf16[192,896]{1,0:T(8,128)(2,1)S(1)} collective-permute-done((bf16[192,896]{1,0:T(8,128)(2,1)}, bf16[192,896]{1,0:T(8,128)(2,1)S(1)}, u32[]{:S(2)}, u32[]{:S(2)}) %collective-permute-start.11) | collective-permute-done | bytes 344096 | tf_op jit(solution)/shard_map/ppermute | solution.py:93
  160.1 3.4 %collective-permute-done.12.refs_3_ = bf16[192,896]{1,0:T(8,128)(2,1)} collective-permute-done((bf16[192,896]{1,0:T(8,128)(2,1)}, bf16[192,896]{1,0:T(8,128)(2,1)}, u32[]{:S(2)}, u32[]{:S(2)}) %collective-permute-start.12) | collective-permute-done | bytes 344096 | tf_op jit(solution)/shard_map/ppermute | solution.py:93
  163.5 7.3 %unroute.1 = (bf16[768,512]{1,0:T(8,128)(2,1)}, f32[512,768]{1,0:T(8,128)}, bf16[512,768]{1,0:T(8,128)(2,1)}, f32[512,128]{1,0:T(8,128)}, f32[1,768]{1,0:T(1,128)}) custom-call(s32[5]{0:T(128)S(1)} %stack.19.meta, bf16[192,896]{1,0:T(8,128)(2,1)S(1)} %copy-done.6, bf16[192,896]{1,0:T(8,128)(2,1)S(1)} %collective-permute-done.10.refs_1_, ...), custom_call_target="tpu_custom_call" | custom-call | flops 109999996928 | bytes 65536 | tf_op jit(solution)/shard_map/unroute/pallas_call | solution.py:73
  170.8 3.7 %all-to-all-done.2.refs_0_ = bf16[4,192,768]{2,1,0:T(8,128)(2,1)S(1)} async-done(((bf16[4,192,768]{2,1,0:T(8,128)(2,1)}), bf16[4,192,768]{2,1,0:T(8,128)(2,1)S(1)}, u32[]{:S(2)}, u32[]{:S(2)}) %all-to-all-start.2) | async-done | bytes 1179680 | tf_op jit(solution)/shard_map/all_to_all | solution.py:105
  174.5 3.5 %all-to-all-start.3 = ((bf16[4,192,512]{2,1,0:T(8,128)(2,1)}), bf16[4,192,512]{2,1,0:T(8,128)(2,1)S(1)}, u32[]{:S(2)}, u32[]{:S(2)}) async-start(bf16[4,192,512]{2,1,0:T(8,128)(2,1)} %bitcast.51), calls=%async_computation.3 | async-start | bytes 1572864 | tf_op jit(solution)/shard_map/all_to_all | solution.py:105
  178.0 3.7 %mixed.1.refs_13_ = bf16[512,768]{1,0:T(8,128)(2,1)} custom-call(s32[5]{0:T(128)S(1)} %stack.19.meta, f32[512,768]{1,0:T(8,128)} %get-tuple-element.108.partial, bf16[4,192,512]{2,1,0:T(8,128)(2,1)} %get-tuple-element.103.slots.refs_6_, bf16[4,192,768]{2,1,0:T(8,128)(2,1)S(1)} %all-to-all-done.2.refs_0_, f32[512,768]{1,0:T(8,128)} %get-tuple-element.128.refs_1_.refs_7_), custom_call_target="tpu_custom_call" | custom-call | flops 110000000 | bytes 65536 | tf_op jit(solution)/shard_map/mixed/pallas_call | solution.py:73
  181.7 7.7 %all-to-all-done.3.refs_0_ = bf16[4,192,512]{2,1,0:T(8,128)(2,1)S(1)} async-done(((bf16[4,192,512]{2,1,0:T(8,128)(2,1)}), bf16[4,192,512]{2,1,0:T(8,128)(2,1)S(1)}, u32[]{:S(2)}, u32[]{:S(2)}) %all-to-all-start.3) | async-done | bytes 786464 | tf_op jit(solution)/shard_map/all_to_all | solution.py:105
  189.4 29.2 %attend_back.1 = (bf16[576,512]{1,0:T(8,128)(2,1)}, bf16[576,512]{1,0:T(8,128)(2,1)}, bf16[576,512]{1,0:T(8,128)(2,1)}, bf16[576,512]{1,0:T(8,128)(2,1)}, bf16[1...) custom-call(s32[5]{0:T(128)S(1)} %stack.19.meta, bf16[4,576,512]{2,1,0:T(8,128)(2,1)} %get-tuple-element.129.qkv, ...), custom_call_target="tpu_custom_call" | custom-call | flops 13200000000 | bytes 65536 | tf_op jit(solution)/shard_map/attend_back/pallas_call | solution.py:73
  218.7 0.4 collective-permute-start.16
  219.2 1.6 collective-permute-start.15
  220.8 2.4 collective-permute-start.17
  223.2 2.7 add_dense.1
  225.9 7.1 %all-to-all-start.4 = ((bf16[16,24,1536]{2,1,0:T(8,128)(2,1)}), bf16[16,24,1536]{2,1,0:T(8,128)(2,1)S(1)}, u32[]{:S(2)}, u32[]{:S(2)}) async-start(bf16[16,24,1536]{2,1,0:T(8,128)(2,1)} %add_dense.1), calls=%async_computation.4 | async-start | bytes 2359296 | tf_op jit(solution)/shard_map/all_to_all | solution.py:105
  233.0 3.7 %collective-permute-done.16.refs_2_ = bf16[576,512]{1,0:T(8,128)(2,1)S(1)} collective-permute-done((bf16[576,512]{1,0:T(8,128)(2,1)}, bf16[576,512]{1,0:T(8,128)(2,1)S(1)}, u32[]{:S(2)}, u32[]{:S(2)}) %collective-permute-start.16) | collective-permute-done | bytes 589856 | tf_op jit(solution)/shard_map/ppermute | solution.py:93
  236.7 0.6 collective-permute-start.19
  237.3 2.0 collective-permute-start.20
  239.3 2.1 collective-permute-start.21
  241.4 6.5 %collective-permute-done.15.refs_1_ = bf16[576,512]{1,0:T(8,128)(2,1)} collective-permute-done((bf16[576,512]{1,0:T(8,128)(2,1)}, bf16[576,512]{1,0:T(8,128)(2,1)}, u32[]{:S(2)}, u32[]{:S(2)}) %collective-permute-start.15) | collective-permute-done | bytes 589856 | tf_op jit(solution)/shard_map/ppermute | solution.py:93
  247.9 1.1 collective-permute-done.17.refs_3_
  249.0 1.1 copy-done.8
  250.1 6.8 %finish.1.refs_0_ = bf16[512,768]{1,0:T(8,128)(2,1)} custom-call(s32[5]{0:T(128)S(1)} %stack.19.meta, bf16[576,512]{1,0:T(8,128)(2,1)S(1)} %copy-done.8, bf16[576,512]{1,0:T(8,128)(2,1)} %collective-permute-done.15.refs_1_, bf16[576,512]{1,0:T(8,128)(2,1)S(1)} %collective-permute-done.16.refs_2_, bf16[576,512]{1,0:T(8,128)(2,1)} %collective-permute-done.17.refs_3_, ...), custom_call_target="tpu_custom_call" | custom-call | flops 11000000512 | bytes 65536 | tf_op jit(solution)/shard_map/finish/pallas_call | solution.py:73
  256.9 1.4 add_pieces.1.refs_0_
  258.3 3.2 %collective-permute-done.20.refs_2_ = bf16[24,6144]{1,0:T(8,128)(2,1)S(1)} collective-permute-done((bf16[24,6144]{1,0:T(8,128)(2,1)}, bf16[24,6144]{1,0:T(8,128)(2,1)S(1)}, u32[]{:S(2)}, u32[]{:S(2)}) %collective-permute-start.20) | collective-permute-done | bytes 294944 | tf_op jit(solution)/shard_map/ppermute | solution.py:93
  261.5 0.6 collective-permute-start.22
  262.1 2.0 collective-permute-start.23
  264.1 2.1 collective-permute-start.24
  266.2 2.1 gather.1
  268.3 1.5 collective-permute-done.24.refs_3_
  269.9 0.9 copy-done.1
  270.7 1.9 gather_dense.1
  (52 shorter events, 0.9 us)
Async XLA Ops:
  7.2 76.6 %all-gather.3.cloned.1.call-start = ((), (), s32[]{:S(2)}) async-start(), calls=%async_computation.6 | async-start | bytes 11354112 | tf_op jit(solution)/shard_map/all_gather | solution.py:963
  8.0 3.3 %copy-start.4 = (bf16[1,512,768]{2,1,0:T(8,128)(2,1)S(1)}, bf16[1,512,768]{2,1,0:T(8,128)(2,1)}, u32[]{:S(2)}) copy-start(bf16[1,512,768]{2,1,0:T(8,128)(2,1)} %param.15) | copy-start | bytes 2359300
  11.3 20.6 %collective-permute-start = (bf16[512,768]{1,0:T(8,128)(2,1)S(1)}, bf16[512,768]{1,0:T(8,128)(2,1)S(1)}, u32[]{:S(2)}, u32[]{:S(2)}) collective-permute-start(bf16[512,768]{1,0:T(8,128)(2,1)S(1)} %bitcast.44), channel_id=1, source_target_pairs={{0,32},{32,64},{64,96},{96,0},{1,33},{33,65},{65,97},{97,1},{2,34}... | collective-permute-start | bytes 2359304 | tf_op jit(solution)/shard_map/ppermute | solution.py:88
  12.8 20.1 %collective-permute-start.1 = (bf16[512,768]{1,0:T(8,128)(2,1)S(1)}, bf16[512,768]{1,0:T(8,128)(2,1)S(1)}, u32[]{:S(2)}, u32[]{:S(2)}) collective-permute-start(bf16[512,768]{1,0:T(8,128)(2,1)S(1)} %bitcast.45), channel_id=1, source_target_pairs={{0,96},{32,0},{64,32},{96,64},{1,97},{33,1},{65,33},{97,65},{2,98}... | collective-permute-start | bytes 2359304 | tf_op jit(solution)/shard_map/ppermute | solution.py:88
  14.6 32.3 %all-to-all-start = ((bf16[32,24,640]{2,1,0:T(8,128)(2,1)}), bf16[32,24,640]{2,1,0:T(8,128)(2,1)S(1)}, u32[]{:S(2)}, u32[]{:S(2)}) async-start(bf16[32,24,640]{2,1,0:T(8,128)(2,1)} %get-tuple-element.93), calls=%async_computation | async-start | bytes 1966080 | tf_op jit(solution)/shard_map/all_to_all | solution.py:105
  32.6 14.6 %collective-permute-start.2 = (bf16[256,768]{1,0:T(8,128)(2,1)}, bf16[256,768]{1,0:T(8,128)(2,1)}, u32[]{:S(2)}, u32[]{:S(2)}) collective-permute-start(bf16[256,768]{1,0:T(8,128)(2,1)} %slice.16), channel_id=1, source_target_pairs={{0,32},{32,64},{64,96},{96,0},{1,33},{33,65},{65,97},{97,1},{2,34}... | collective-permute-start | bytes 1179656 | tf_op jit(solution)/shard_map/ppermute | solution.py:88
  33.7 13.5 %collective-permute-start.3 = (bf16[256,768]{1,0:T(8,128)(2,1)}, bf16[256,768]{1,0:T(8,128)(2,1)}, u32[]{:S(2)}, u32[]{:S(2)}) collective-permute-start(bf16[256,768]{1,0:T(8,128)(2,1)} %slice.17), channel_id=1, source_target_pairs={{0,96},{32,0},{64,32},{96,64},{1,97},{33,1},{65,33},{97,65},{2,98}... | collective-permute-start | bytes 1179656 | tf_op jit(solution)/shard_map/ppermute | solution.py:88
  42.0 27.6 %collective-permute-start.4 = (bf16[192,768]{1,0:T(8,128)(2,1)}, bf16[192,768]{1,0:T(8,128)(2,1)}, u32[]{:S(2)}, u32[]{:S(2)}) collective-permute-start(bf16[192,768]{1,0:T(8,128)(2,1)} %get-tuple-element.97), channel_id=1, source_target_pairs={{0,32},{32,0},{64,96},{96,64},{1,33},{33,1},{65,97},{97,65},{2,34}... | collective-permute-start | bytes 884744 | tf_op jit(solution)/shard_map/ppermute | solution.py:93
  42.0 27.6 %collective-permute-start.5 = (bf16[192,768]{1,0:T(8,128)(2,1)}, bf16[192,768]{1,0:T(8,128)(2,1)}, u32[]{:S(2)}, u32[]{:S(2)}) collective-permute-start(bf16[192,768]{1,0:T(8,128)(2,1)} %get-tuple-element.98), channel_id=1, source_target_pairs={{0,64},{32,96},{64,0},{96,32},{1,65},{33,97},{65,1},{97,33},{2,66}... | collective-permute-start | bytes 884744 | tf_op jit(solution)/shard_map/ppermute | solution.py:93
  43.8 25.9 %collective-permute-start.6 = (bf16[192,768]{1,0:T(8,128)(2,1)}, bf16[192,768]{1,0:T(8,128)(2,1)}, u32[]{:S(2)}, u32[]{:S(2)}) collective-permute-start(bf16[192,768]{1,0:T(8,128)(2,1)} %get-tuple-element.99), channel_id=1, source_target_pairs={{0,96},{32,64},{64,32},{96,0},{1,97},{33,65},{65,33},{97,1},{2,98}... | collective-permute-start | bytes 884744 | tf_op jit(solution)/shard_map/ppermute | solution.py:93
  47.2 6.3 %copy-start.3 = (f32[1,768]{1,0:T(1,128)}, f32[1,768]{1,0:T(1,128)S(1)}, u32[]{:S(2)}) copy-start(f32[1,768]{1,0:T(1,128)S(1)} %reshape.104.refs_6_) | copy-start | bytes 9220
  69.7 14.1 %all-to-all-start.1 = ((bf16[4,192,512]{2,1,0:T(8,128)(2,1)}), bf16[4,192,512]{2,1,0:T(8,128)(2,1)S(1)}, u32[]{:S(2)}, u32[]{:S(2)}) async-start(bf16[4,192,512]{2,1,0:T(8,128)(2,1)} %get-tuple-element.100.refs_1_), calls=%async_computation.1 | async-start | bytes 1572864 | tf_op jit(solution)/shard_map/all_to_all | solution.py:105
  73.2 75.4 %all-gather.5.cloned.1.call-start = ((), (), s32[]{:S(2)}) async-start(), calls=%async_computation.7 | async-start | bytes 3649536 | tf_op jit(solution)/shard_map/all_gather | solution.py:964
  83.8 6.2 %copy-start = (bf16[4,192,512]{2,1,0:T(8,128)(2,1)}, bf16[4,192,512]{2,1,0:T(8,128)(2,1)S(1)}, u32[]{:S(2)}) copy-start(bf16[4,192,512]{2,1,0:T(8,128)(2,1)S(1)} %all-to-all-done.1) | copy-start | bytes 2359300
  90.0 13.8 %collective-permute-start.7 = (bf16[192,896]{1,0:T(8,128)(2,1)}, bf16[192,896]{1,0:T(8,128)(2,1)S(1)}, u32[]{:S(2)}, u32[]{:S(2)}) collective-permute-start(bf16[192,896]{1,0:T(8,128)(2,1)} %get-tuple-element.110), channel_id=1, source_target_pairs={{0,32},{32,0},{64,96},{96,64},{1,33},{33,1},{65,97},{97,65},{2,34}... | collective-permute-start | bytes 1032200 | tf_op jit(solution)/shard_map/ppermute | solution.py:93
  90.6 14.4 %collective-permute-start.8 = (bf16[192,896]{1,0:T(8,128)(2,1)}, bf16[192,896]{1,0:T(8,128)(2,1)S(1)}, u32[]{:S(2)}, u32[]{:S(2)}) collective-permute-start(bf16[192,896]{1,0:T(8,128)(2,1)} %get-tuple-element.111), channel_id=1, source_target_pairs={{0,64},{32,96},{64,0},{96,32},{1,65},{33,97},{65,1},{97,33},{2,66}... | collective-permute-start | bytes 1032200 | tf_op jit(solution)/shard_map/ppermute | solution.py:93
  92.7 14.9 %collective-permute-start.9 = (bf16[192,896]{1,0:T(8,128)(2,1)}, bf16[192,896]{1,0:T(8,128)(2,1)S(1)}, u32[]{:S(2)}, u32[]{:S(2)}) collective-permute-start(bf16[192,896]{1,0:T(8,128)(2,1)} %get-tuple-element.112), channel_id=1, source_target_pairs={{0,96},{32,64},{64,32},{96,0},{1,97},{33,65},{65,33},{97,1},{2,98}... | collective-permute-start | bytes 1032200 | tf_op jit(solution)/shard_map/ppermute | solution.py:93
  98.8 9.6 %copy-start.5 = (bf16[192,768]{1,0:T(8,128)(2,1)S(1)}, bf16[192,768]{1,0:T(8,128)(2,1)}, u32[]{:S(2)}) copy-start(bf16[192,768]{1,0:T(8,128)(2,1)} %get-tuple-element.113.refs_4_) | copy-start | bytes 884740
  98.8 9.6 %copy-start.7 = (bf16[192,896]{1,0:T(8,128)(2,1)S(1)}, bf16[192,896]{1,0:T(8,128)(2,1)}, u32[]{:S(2)}) copy-start(bf16[192,896]{1,0:T(8,128)(2,1)} %get-tuple-element.109.refs_0_) | copy-start | bytes 1032196
  105.0 2.6 copy-start.9
  107.6 0.8 copy-start.10
  139.5 9.1 %collective-permute-start.13 = (bf16[4,2,16,24,512]{4,3,2,1,0:T(8,128)(2,1)}, bf16[4,2,16,24,512]{4,3,2,1,0:T(8,128)(2,1)}, u32[]{:S(2)}, u32[]{:S(2)}) collective-permute-start(bf16[4,2,16,24,512]{4,3,2,1,0:T(8,128)(2,1)} %get-tuple-element.124), channel_id=1, source_target_pairs={{0,1},{1,0},{2,3},{3,2},{4,5},{5,4},{6,7},{7,6},{8,9},{9,8},{10,11... | collective-permute-start | bytes 9437192 | tf_op jit(solution)/shard_map/ppermute | solution.py:93
  139.6 9.0 %collective-permute-start.14 = (bf16[16,64,768]{2,1,0:T(8,128)(2,1)}, bf16[16,64,768]{2,1,0:T(8,128)(2,1)S(1)}, u32[]{:S(2)}, u32[]{:S(2)}) collective-permute-start(bf16[16,64,768]{2,1,0:T(8,128)(2,1)} %get-tuple-element.126), channel_id=1, source_target_pairs={{0,1},{1,0},{2,3},{3,2},{4,5},{5,4},{6,7},{7,6},{8,9},{9,8},{10,11... | collective-permute-start | bytes 4718600 | tf_op jit(solution)/shard_map/ppermute | solution.py:93
  140.1 14.7 %collective-permute-start.10 = (bf16[192,896]{1,0:T(8,128)(2,1)}, bf16[192,896]{1,0:T(8,128)(2,1)S(1)}, u32[]{:S(2)}, u32[]{:S(2)}) collective-permute-start(bf16[192,896]{1,0:T(8,128)(2,1)} %get-tuple-element.120), channel_id=1, source_target_pairs={{0,32},{32,0},{64,96},{96,64},{1,33},{33,1},{65,97},{97,65},{2,34}... | collective-permute-start | bytes 1032200 | tf_op jit(solution)/shard_map/ppermute | solution.py:93
  140.1 20.0 %collective-permute-start.11 = (bf16[192,896]{1,0:T(8,128)(2,1)}, bf16[192,896]{1,0:T(8,128)(2,1)S(1)}, u32[]{:S(2)}, u32[]{:S(2)}) collective-permute-start(bf16[192,896]{1,0:T(8,128)(2,1)} %get-tuple-element.121), channel_id=1, source_target_pairs={{0,64},{32,96},{64,0},{96,32},{1,65},{33,97},{65,1},{97,33},{2,66}... | collective-permute-start | bytes 1032200 | tf_op jit(solution)/shard_map/ppermute | solution.py:93
  143.6 19.9 %collective-permute-start.12 = (bf16[192,896]{1,0:T(8,128)(2,1)}, bf16[192,896]{1,0:T(8,128)(2,1)}, u32[]{:S(2)}, u32[]{:S(2)}) collective-permute-start(bf16[192,896]{1,0:T(8,128)(2,1)} %get-tuple-element.122), channel_id=1, source_target_pairs={{0,96},{32,64},{64,32},{96,0},{1,97},{33,65},{65,33},{97,1},{2,98}... | collective-permute-start | bytes 1032200 | tf_op jit(solution)/shard_map/ppermute | solution.py:93
  144.8 29.7 %all-to-all-start.2 = ((bf16[4,192,768]{2,1,0:T(8,128)(2,1)}), bf16[4,192,768]{2,1,0:T(8,128)(2,1)S(1)}, u32[]{:S(2)}, u32[]{:S(2)}) async-start(bf16[4,192,768]{2,1,0:T(8,128)(2,1)} %get-tuple-element.118), calls=%async_computation.2 | async-start | bytes 2359296 | tf_op jit(solution)/shard_map/all_to_all | solution.py:105
  148.3 88.4 %reduce-scatter.4.cloned.1.call-start = ((), (), s32[]{:S(2)}) async-start(), calls=%async_computation.8 | async-start | bytes 5013504
  154.8 8.7 %copy-start.6 = (bf16[192,896]{1,0:T(8,128)(2,1)S(1)}, bf16[192,896]{1,0:T(8,128)(2,1)}, u32[]{:S(2)}) copy-start(bf16[192,896]{1,0:T(8,128)(2,1)} %get-tuple-element.119.refs_0_) | copy-start | bytes 1032196
  174.5 14.9 %all-to-all-start.3 = ((bf16[4,192,512]{2,1,0:T(8,128)(2,1)}), bf16[4,192,512]{2,1,0:T(8,128)(2,1)S(1)}, u32[]{:S(2)}, u32[]{:S(2)}) async-start(bf16[4,192,512]{2,1,0:T(8,128)(2,1)} %bitcast.51), calls=%async_computation.3 | async-start | bytes 1572864 | tf_op jit(solution)/shard_map/all_to_all | solution.py:105
  218.6 4.5 %collective-permute-start.18 = (bf16[16,24,1536]{2,1,0:T(8,128)(2,1)}, bf16[16,24,1536]{2,1,0:T(8,128)(2,1)S(1)}, u32[]{:S(2)}, u32[]{:S(2)}) collective-permute-start(bf16[16,24,1536]{2,1,0:T(8,128)(2,1)} %get-tuple-element.145), channel_id=1, source_target_pairs={{0,1},{1,0},{2,3},{3,2},{4,5},{5,4},{6,7},{7,6},{8,9},{9,8},{10,11... | collective-permute-start | bytes 3538952 | tf_op jit(solution)/shard_map/ppermute | solution.py:93
  218.7 18.0 %collective-permute-start.16 = (bf16[576,512]{1,0:T(8,128)(2,1)}, bf16[576,512]{1,0:T(8,128)(2,1)S(1)}, u32[]{:S(2)}, u32[]{:S(2)}) collective-permute-start(bf16[576,512]{1,0:T(8,128)(2,1)} %get-tuple-element.141), channel_id=1, source_target_pairs={{0,64},{32,96},{64,0},{96,32},{1,65},{33,97},{65,1},{97,33},{2,66}... | collective-permute-start | bytes 1769480 | tf_op jit(solution)/shard_map/ppermute | solution.py:93
  219.2 28.7 %collective-permute-start.15 = (bf16[576,512]{1,0:T(8,128)(2,1)}, bf16[576,512]{1,0:T(8,128)(2,1)}, u32[]{:S(2)}, u32[]{:S(2)}) collective-permute-start(bf16[576,512]{1,0:T(8,128)(2,1)} %get-tuple-element.140), channel_id=1, source_target_pairs={{0,32},{32,0},{64,96},{96,64},{1,33},{33,1},{65,97},{97,65},{2,34}... | collective-permute-start | bytes 1769480 | tf_op jit(solution)/shard_map/ppermute | solution.py:93
  220.8 28.3 %collective-permute-start.17 = (bf16[576,512]{1,0:T(8,128)(2,1)}, bf16[576,512]{1,0:T(8,128)(2,1)}, u32[]{:S(2)}, u32[]{:S(2)}) collective-permute-start(bf16[576,512]{1,0:T(8,128)(2,1)} %get-tuple-element.143), channel_id=1, source_target_pairs={{0,96},{32,64},{64,32},{96,0},{1,97},{33,65},{65,33},{97,1},{2,98}... | collective-permute-start | bytes 1769480 | tf_op jit(solution)/shard_map/ppermute | solution.py:93
  225.9 31.0 %all-to-all-start.4 = ((bf16[16,24,1536]{2,1,0:T(8,128)(2,1)}), bf16[16,24,1536]{2,1,0:T(8,128)(2,1)S(1)}, u32[]{:S(2)}, u32[]{:S(2)}) async-start(bf16[16,24,1536]{2,1,0:T(8,128)(2,1)} %add_dense.1), calls=%async_computation.4 | async-start | bytes 2359296 | tf_op jit(solution)/shard_map/all_to_all | solution.py:105
  236.7 21.6 %collective-permute-start.19 = (bf16[24,6144]{1,0:T(8,128)(2,1)}, bf16[24,6144]{1,0:T(8,128)(2,1)S(1)}, u32[]{:S(2)}, u32[]{:S(2)}) collective-permute-start(bf16[24,6144]{1,0:T(8,128)(2,1)} %reduce-scatter.4.cloned.1.call-done.refs_0_), channel_id=1, source_target_pairs={{0,32},{32,0},{64,96},{96,64},{1,33},{33,1},{65,97},{97,65},{2,34}... | collective-permute-start | bytes 884744 | tf_op jit(solution)/shard_map/ppermute | solution.py:93
  237.3 24.2 %collective-permute-start.20 = (bf16[24,6144]{1,0:T(8,128)(2,1)}, bf16[24,6144]{1,0:T(8,128)(2,1)S(1)}, u32[]{:S(2)}, u32[]{:S(2)}) collective-permute-start(bf16[24,6144]{1,0:T(8,128)(2,1)} %reduce-scatter.4.cloned.1.call-done.refs_0_), channel_id=1, source_target_pairs={{0,64},{32,96},{64,0},{96,32},{1,65},{33,97},{65,1},{97,33},{2,66}... | collective-permute-start | bytes 884744 | tf_op jit(solution)/shard_map/ppermute | solution.py:93
  239.3 22.2 %collective-permute-start.21 = (bf16[24,6144]{1,0:T(8,128)(2,1)}, bf16[24,6144]{1,0:T(8,128)(2,1)S(1)}, u32[]{:S(2)}, u32[]{:S(2)}) collective-permute-start(bf16[24,6144]{1,0:T(8,128)(2,1)} %reduce-scatter.4.cloned.1.call-done.refs_0_), channel_id=1, source_target_pairs={{0,96},{32,64},{64,32},{96,0},{1,97},{33,65},{65,33},{97,1},{2,98}... | collective-permute-start | bytes 884744 | tf_op jit(solution)/shard_map/ppermute | solution.py:93
  249.0 1.1 copy-start.8
  256.9 9.3 %copy-start.2 = (bf16[24,6144]{1,0:T(8,128)(2,1)S(1)}, bf16[24,6144]{1,0:T(8,128)(2,1)}, u32[]{:S(2)}) copy-start(bf16[24,6144]{1,0:T(8,128)(2,1)} %reduce-scatter.4.cloned.1.call-done.refs_0_) | copy-start | bytes 884740
  261.5 6.8 %collective-permute-start.22 = (bf16[24,1536]{1,0:T(8,128)(2,1)}, bf16[24,1536]{1,0:T(8,128)(2,1)S(1)}, u32[]{:S(2)}, u32[]{:S(2)}) collective-permute-start(bf16[24,1536]{1,0:T(8,128)(2,1)} %add_pieces.1.refs_0_), channel_id=1, source_target_pairs={{0,32},{32,0},{64,96},{96,64},{1,33},{33,1},{65,97},{97,65},{2,34}... | collective-permute-start | bytes 221192 | tf_op jit(solution)/shard_map/ppermute | solution.py:93
  262.1 6.2 %collective-permute-start.23 = (bf16[24,1536]{1,0:T(8,128)(2,1)}, bf16[24,1536]{1,0:T(8,128)(2,1)S(1)}, u32[]{:S(2)}, u32[]{:S(2)}) collective-permute-start(bf16[24,1536]{1,0:T(8,128)(2,1)} %add_pieces.1.refs_0_), channel_id=1, source_target_pairs={{0,64},{32,96},{64,0},{96,32},{1,65},{33,97},{65,1},{97,33},{2,66}... | collective-permute-start | bytes 221192 | tf_op jit(solution)/shard_map/ppermute | solution.py:93
  264.1 5.8 %collective-permute-start.24 = (bf16[24,1536]{1,0:T(8,128)(2,1)}, bf16[24,1536]{1,0:T(8,128)(2,1)S(1)}, u32[]{:S(2)}, u32[]{:S(2)}) collective-permute-start(bf16[24,1536]{1,0:T(8,128)(2,1)} %add_pieces.1.refs_0_), channel_id=1, source_target_pairs={{0,96},{32,64},{64,32},{96,0},{1,97},{33,65},{65,33},{97,1},{2,98}... | collective-permute-start | bytes 221192 | tf_op jit(solution)/shard_map/ppermute | solution.py:93
  269.9 0.9 copy-start.1
Sparse Core Ops, SparseCore 0:
  11.4 65.6 all-gather.2
  79.4 44.3 all-gather.4
  154.9 79.6 reduce-scatter.3

commit v2 on v1

--- a/solution.py
+++ b/solution.py
@@ -365,21 +365,16 @@
 
 
 def attend_back_kernel(meta, qkv, *refs):
-    dout, out, lse, cosine, sine, dlogits, grad_vec, dgain, prior_hits = refs[:9]
-    later = refs[9:13]
-    dproj = refs[-11 - SEQS : -11]
-    kept, gone, dq, dk, dv, dots, *ready, sems = refs[-11:]
+    dout, out, lse, cosine, sine, normed = refs[:6]
+    dproj = refs[-8 - SEQS : -8]
+    kept, gone, dq, dk, dv, dots, normed_held, sem = refs[-8:]
     blocks, width, rows = qkv.shape
     part = width // 3
     heads = part // HEAD_DIM
     length = meta[0]
 
-    copies = [
-        pltpu.make_async_copy(a, b, sems.at[k]) for k, (a, b) in enumerate(zip(later, ready))
-    ]
-    for copy in copies:
-        copy.start()
-    normed_held, att, dlow, moe = ready
+    copy = pltpu.make_async_copy(normed, normed_held, sem)
+    copy.start()
 
     def pair(q, k, diagonal):
         for h in range(heads):
@@ -436,9 +431,37 @@
                 dproj[to][at + HALF : at + HEAD_DIM] = (y * c - x * s).astype(BF16)
         dproj[to][2 * part :] = dv[b].astype(BF16)
 
-    for copy in copies:
-        copy.wait()
-    pairs, shard, wide = kept.shape
+    copy.wait()
+    pairs, shard, _ = kept.shape
+    even = meta[2] == 0
+
+    def halves(x, at):
+        x = x.reshape(pairs, 2 * shard, x.shape[1])
+        first, second = x[:, :shard], x[:, shard:]
+        kept[:, :, at : at + x.shape[2]] = jnp.where(even, first, second).astype(BF16)
+        gone[:, :, at : at + x.shape[2]] = jnp.where(even, second, first).astype(BF16)
+
+    total = mm(dproj[0][...], normed_held[around(meta, 0)])
+    for to in range(1, SEQS):
+        total += mm(dproj[to][...], normed_held[around(meta, to)])
+    halves(jnp.transpose(total), 0)
+
+
+def attend_back(meta, before, qkv, dout, out, lse, cosine, sine, normed, count):
+    blocks, width, rows = qkv.shape
+    part = width // 3
+    model = normed.shape[2]
+    scratch = [pltpu.VMEM((blocks, part, rows), F32)] * 3 + [pltpu.VMEM((blocks, 8, rows), F32)]
+    scratch += [pltpu.VMEM(normed.shape, BF16), pltpu.SemaphoreType.DMA]
+    inputs = [qkv, *come(dout), out, lse, cosine, sine, (far(normed), ANY)]
+    results = [((width, rows), BF16)] * SEQS
+    results += [((count // 2, model // count, width), BF16)] * 2
+    return one_step(attend_back_kernel, 12, meta, inputs, results, scratch, before, 48)
+
+
+def dense_kernel(meta, att, dlow, moe, dlogits, grad_vec, dgain, prior_hits, *refs):
+    kept, gone = refs[-2:]
+    pairs, shard, _ = kept.shape
     model = att.shape[0]
     even = meta[2] == 0
 
@@ -462,24 +485,13 @@
     block = jnp.concatenate([block, jnp.zeros((shard - NE, LANES), F32)], axis=0)
     result = result.reshape(2 * pairs, shard, LANES) + block[None]
     halves(result.reshape(model, LANES), model)
-    total = mm(dproj[0][...], normed_held[around(meta, 0)])
-    for to in range(1, SEQS):
-        total += mm(dproj[to][...], normed_held[around(meta, to)])
-    total = [jnp.transpose(total), jnp.zeros((model, wide - model - LANES - width), F32)]
-    halves(jnp.concatenate(total, axis=1), model + LANES)
-
-
-def attend_back(meta, before, qkv, dout, out, lse, cosine, sine, few, later, count):
-    blocks, width, rows = qkv.shape
-    part = width // 3
-    model = later[1].shape[0]
-    scratch = [pltpu.VMEM((blocks, part, rows), F32)] * 3 + [pltpu.VMEM((blocks, 8, rows), F32)]
-    scratch += [pltpu.VMEM(x.shape, BF16) for x in later] + [pltpu.SemaphoreType.DMA((4,))]
-    inputs = [qkv, *come(dout), out, lse, cosine, sine, *few, *((far(x), ANY) for x in later)]
-    wide = -(-(model + LANES + width) // LANES) * LANES
-    results = [((width, rows), BF16)] * SEQS
-    results += [((count // 2, model // count, wide), BF16)] * 2
-    return one_step(attend_back_kernel, 12, meta, inputs, results, scratch, before, 48)
+
+
+def dense(meta, att, dlow, moe, dlogits, grad_vec, dgain, prior_hits, count, *before):
+    model = dlow.shape[1]
+    inputs = [*come(att), dlow, moe, dlogits, grad_vec, dgain, prior_hits]
+    results = [((count // 2, model // count, model + LANES), BF16)] * 2
+    return one_step(dense_kernel, 0.1, meta, inputs, results, (), before, 24)
 
 
 def route_kernel(meta, att, out_w, small_w, tok, prior, slots, *refs):
@@ -739,18 +751,24 @@
     )(*[x if k % 2 else far(x) for k, x in enumerate(parts)], *map(far, before))
 
 
-def add_dense_kernel(meta, kept, other, out):
+def add_dense_kernel(meta, dense_a, dense_b, heads_a, heads_b, *refs):
+    out = refs[-1]
+    pairs, shard, wide = dense_a.shape
+    width, model = heads_a.shape[2], wide - LANES
+    for k in range(pairs):
+        total = dense_a[k].astype(F32) + dense_b[k].astype(F32)
+        out[k, :, :model] = total[:, :model].astype(BF16)
+        out[k, :, model:wide] = split_again(total[:, model:]).astype(BF16)
+        heads = heads_a[k].astype(F32) + heads_b[k].astype(F32)
+        rest = jnp.zeros((shard, out.shape[2] - wide - width), F32)
+        out[k, :, wide:] = jnp.concatenate([heads, rest], axis=1).astype(BF16)
+
+
+def add_dense(meta, kept, come_dense, heads, come_heads, *before):
     pairs, shard, wide = kept.shape
-    model = 2 * pairs * shard
-    for k in range(pairs):
-        total = kept[k].astype(F32) + other[k].astype(F32)
-        out[k] = total.astype(BF16)
-        out[k, :, model : model + LANES] = split_again(total[:, model : model + LANES]).astype(BF16)
-
-
-def add_dense(meta, kept, other):
-    inputs = [kept, *come(other)]
-    return one_step(add_dense_kernel, 0.1, meta, inputs, [(kept.shape, BF16)], mib=24)[0]
+    results = [((pairs, shard, -(-(wide + heads.shape[2]) // LANES) * LANES), BF16)]
+    inputs = [kept, *come(come_dense), heads, *come(come_heads)]
+    return one_step(add_dense_kernel, 0.1, meta, inputs, results, (), before, 24)[0]
 
 
 def add_pieces_kernel(meta, pieces, *refs):
@@ -994,7 +1012,7 @@
     *results, in_kept, in_sent, out_kept, out_sent = expert(
         meta, sent, grad_rows, small, weights, w_out, 512, fsdp
     )
-    back, branch = trades(results[:seqs]), swap(results[seqs], "seq")
+    back, branch = trades(results[:seqs]), results[seqs]
     in_come, out_come = trade(in_sent, 1, "core"), trade(out_sent, 1, "core")
     both = add_cores((in_kept, in_come, out_kept, out_come), back_w)
     part = both.reshape(-1, both.shape[2])
@@ -1002,23 +1020,28 @@
     tokenwise = (slots, resid, small, stats, grad, vectors)
     datt, dres, dlow, dlogits, dgain_m = unroute(meta, (both,), back, weights, tokenwise)
     dout = swap(datt.reshape(seqs, group, rows), "seq")
-    mixed_out = mixed(meta, partial, slots, branch, dres)
-    few = (dlogits, grad_vec, dgain_m, prior_hits)
-    *dproj, kept, gone = attend_back(
-        meta, (mixed_out,), qkv, dout, held, lse, cosine, sine, few, (normed, att, dlow, moe), fsdp
-    )
-    other = trade(gone, 1, "core")
+    dout, branch = lax.optimization_barrier((dout, branch))
+    branch = swap(branch, "seq")
+    kept, gone = dense(
+        meta, att, dlow, moe, dlogits, grad_vec, dgain_m, prior_hits, fsdp
+    )
+    come_dense = trade(gone, 1, "core")
+    *dproj, heads, gone = attend_back(
+        meta, (kept,), qkv, dout, held, lse, cosine, sine, normed, fsdp
+    )
+    come_heads = trade(gone, 1, "core")
     back_all = trades(dproj)
-    dense = add_dense(meta, kept, other)
-    dense = swap(dense, YZ)
+    sums = add_dense(meta, kept, come_dense, heads, come_heads, branch)
+    sums = swap(sums, YZ)
     part, back_all[2] = lax.optimization_barrier((part, back_all[2]))
     pieces = trades([part] * seqs)
     grad_tokens = finish(meta, back_all, back_w, tok, gain_a, dres)
-    dense = add_pieces(meta, dense, grad_tokens)
-    dense, *pieces = lax.optimization_barrier((dense, *pieces))
-    dense = trades([dense] * seqs)
+    sums = add_pieces(meta, sums, grad_tokens)
+    sums, *pieces = lax.optimization_barrier((sums, *pieces))
+    mixed_out = mixed(meta, partial, slots, branch, sums)
+    sums = trades([sums] * seqs)
     grad_attend_in, grad_gain_a, grad_att_out, *rest, table = gather_dense(
-        meta, dense, attend_in, gain_attend[None]
+        meta, sums, attend_in, gain_attend[None]
     )
     grad_router, grad_mix, grad_vector, grad_gain_m = rest
     grad_in, grad_out = gather(

time: 285 us -> 279 us (0.979)
  the two profiles are of different devices: /device:TPU:64 before, /device:TPU:88 now
where the time goes in v2:
time: 279 us; the launch traced here: 274 us
  Pallas kernels  134 us (48%)
  starting transfers between devices  61.7 us (22%)
  waiting for transfers between devices  51.9 us (19%)
  between operations  14.9 us (5%)
  local copies, waits for them, and re-layouts  9.3 us (3%)
    pallas_call x13, Pallas kernels, one_step(): pl.pallas_call(body, grid=(1,), in_specs=[SMEM] + [spec for _, spec in in...  77.6 us
    pallas_call x1, Pallas kernels, expert(): pl.pallas_call(expert_kernel, grid=(steps,), in_specs=[SMEM] + [whole(x)...  31.1 us
    ppermute x22, starting transfers between devices, trade(): lax.ppermute(x, axis, [(i, i ^ by) for i in range(count)])  29.4 us
    all_to_all x5, starting transfers between devices, swap(): return lax.all_to_all(x, axis, split_axis=0, concat_axis=0, tiled=True)  25.1 us
    ppermute x22, waiting for transfers between devices, trade(): lax.ppermute(x, axis, [(i, i ^ by) for i in range(count)])  25.1 us
    all_to_all x5, waiting for transfers between devices, swap(): return lax.all_to_all(x, axis, split_axis=0, concat_axis=0, tiled=True)  16.4 us
    pallas_call x1, Pallas kernels, attend(): pl.pallas_call(attend_kernel, grid=(1,), in_specs=[SMEM, VMEM], out_specs...  16.2 us
    ppermute x4, waiting for transfers between devices, shift(): return lax.ppermute(x, 'seq', [(i, (i + by) % count) for i in range(count)])  9.74 us
  transfers between devices with their start and end apart: 34, of which 12 were waited for; matrix products, arithmetic and copies ran while one was open for 3% of the time, Pallas kernels for 47%

profile of v2, /device:TPU:88, one launch (start us, length us, event | category | flops | bytes accessed | tf_op | source)
XLA Modules:
  0.0 274.0 jit_solution(17383060895463538911)
XLA Ops:
  8.0 3.3 %pack.1 = (bf16[32,24,640]{2,1,0:T(8,128)(2,1)}, bf16[24,7168]{1,0:T(8,128)(2,1)}, bf16[24,2304]{1,0:T(8,128)(2,1)}) custom-call(s32[5]{0:T(128)S(1)} %stack.19.meta, f32[24,2304]{1,0:T(8,128)} %refs_4_.1, f32[1,24]{1,0:T(1,128)} %bitcast.52, f32[24,768]{1,0:T(8,128)} %attend_out.1, f32[8,24]{1,0:T(8,128)} %bitcast.55, f32[4,24]{1,0:T(4,128)} %bitcast.59, ...), custom_call_target="tpu_custom_call" | custom-call | flops 2200000000 | bytes 65536 | tf_op jit(solution)/shard_map/pack/pallas_call | solution.py:205
  11.3 1.6 collective-permute-start
  12.8 1.7 collective-permute-start.1
  14.6 7.5 %all-to-all-start = ((bf16[32,24,640]{2,1,0:T(8,128)(2,1)}), bf16[32,24,640]{2,1,0:T(8,128)(2,1)S(1)}, u32[]{:S(2)}, u32[]{:S(2)}) async-start(bf16[32,24,640]{2,1,0:T(8,128)(2,1)} %get-tuple-element.97), calls=%async_computation | async-start | bytes 1966080 | tf_op jit(solution)/shard_map/all_to_all | solution.py:105
  22.1 9.7 %collective-permute-done.refs_1_ = bf16[512,768]{1,0:T(8,128)(2,1)S(1)} collective-permute-done((bf16[512,768]{1,0:T(8,128)(2,1)S(1)}, bf16[512,768]{1,0:T(8,128)(2,1)S(1)}, u32[]{:S(2)}, u32[]{:S(2)}) %collective-permute-start) | collective-permute-done | bytes 786464 | tf_op jit(solution)/shard_map/ppermute | solution.py:88
  31.8 0.8 slice.16
  32.6 0.3 collective-permute-start.2
  32.9 0.8 slice.17
  33.7 3.0 %collective-permute-start.3 = (bf16[256,768]{1,0:T(8,128)(2,1)}, bf16[256,768]{1,0:T(8,128)(2,1)}, u32[]{:S(2)}, u32[]{:S(2)}) collective-permute-start(bf16[256,768]{1,0:T(8,128)(2,1)} %slice.17), channel_id=1, source_target_pairs={{0,96},{32,0},{64,32},{96,64},{1,97},{33,1},{65,33},{97,65},{2,98}... | collective-permute-start | bytes 1179656 | tf_op jit(solution)/shard_map/ppermute | solution.py:88
  36.6 3.5 %plan.1 = (bf16[4,192,512]{2,1,0:T(8,128)(2,1)}, bf16[512,768]{1,0:T(8,128)(2,1)}, f32[512,128]{1,0:T(8,128)}, bf16[512,128]{1,0:T(8,128)(2,1)}, bf16[192,768]{1...) custom-call(s32[5]{0:T(128)S(1)} %stack.19.meta, ...), custom_call_target="tpu_custom_call" | custom-call | flops 1100000000 | bytes 65536 | tf_op jit(solution)/shard_map/plan/pallas_call | solution.py:73
  40.2 1.8 multiply_sine_fusion
  42.0 1.8 collective-permute-start.5
  43.8 3.1 %collective-permute-start.6 = (bf16[192,768]{1,0:T(8,128)(2,1)}, bf16[192,768]{1,0:T(8,128)(2,1)}, u32[]{:S(2)}, u32[]{:S(2)}) collective-permute-start(bf16[192,768]{1,0:T(8,128)(2,1)} %get-tuple-element.103), channel_id=1, source_target_pairs={{0,96},{32,64},{64,32},{96,0},{1,97},{33,65},{65,33},{97,1},{2,98}... | collective-permute-start | bytes 884744 | tf_op jit(solution)/shard_map/ppermute | solution.py:93
  47.2 6.1 %project.1 = (bf16[4,576,512]{2,1,0:T(8,128)(2,1)S(1)}, bf16[4,512,768]{2,1,0:T(8,128)(2,1)}) custom-call(s32[5]{0:T(128)S(1)} %stack.19.meta, bf16[512,768]{1,0:T(8,128)(2,1)S(1)} %bitcast.46, bf16[512,768]{1,0:T(8,128)(2,1)S(1)} %collective-permute-done.refs_1_, bf16[512,768]{1,0:T(8,128)(2,1)S(1)} %collective-permute-done.1.refs_2_, ...), custom_call_target="tpu_custom_call" | custom-call | flops 109999996928 | bytes 65536 | tf_op jit(solution)/shard_map/project/pallas_call | solution.py:73
  53.3 16.2 %attend.1 = (bf16[4,192,512]{2,1,0:T(8,128)(2,1)}, f32[4,8,512]{2,1,0:T(8,128)}, bf16[4,576,512]{2,1,0:T(8,128)(2,1)}) custom-call(s32[5]{0:T(128)S(1)} %stack.19.meta, bf16[4,576,512]{2,1,0:T(8,128)(2,1)S(1)} %get-tuple-element.98.qkv), custom_call_target="tpu_custom_call" | custom-call | flops 110000000 | bytes 65536 | tf_op jit(solution)/shard_map/attend/pallas_call | solution.py:349
  69.5 3.5 %all-to-all-start.1 = ((bf16[4,192,512]{2,1,0:T(8,128)(2,1)}), bf16[4,192,512]{2,1,0:T(8,128)(2,1)S(1)}, u32[]{:S(2)}, u32[]{:S(2)}) async-start(bf16[4,192,512]{2,1,0:T(8,128)(2,1)} %get-tuple-element.104.refs_1_), calls=%async_computation.1 | async-start | bytes 1572864 | tf_op jit(solution)/shard_map/all_to_all | solution.py:105
  73.1 0.7 all-gather.5.cloned.1.call-update
  73.8 0.5 reduce-scatter.4.cloned.1.call-start
  74.3 9.4 %all-to-all-done.1 = bf16[4,192,512]{2,1,0:T(8,128)(2,1)S(1)} async-done(((bf16[4,192,512]{2,1,0:T(8,128)(2,1)}), bf16[4,192,512]{2,1,0:T(8,128)(2,1)S(1)}, u32[]{:S(2)}, u32[]{:S(2)}) %all-to-all-start.1) | async-done | bytes 786464 | tf_op jit(solution)/shard_map/all_to_all | solution.py:105
  83.7 5.8 %route.1 = (bf16[192,896]{1,0:T(8,128)(2,1)}, bf16[192,896]{1,0:T(8,128)(2,1)}, bf16[192,896]{1,0:T(8,128)(2,1)}, bf16[192,896]{1,0:T(8,128)(2,1)}, f32[512,768]...) custom-call(s32[5]{0:T(128)S(1)} %stack.19.meta, bf16[768,512]{1,0:T(8,128)(2,1)S(1)} %bitcast.38, ...), custom_call_target="tpu_custom_call" | custom-call | flops 109999996928 | bytes 65536 | tf_op jit(solution)/shard_map/route/pallas_call | solution.py:73
  89.5 0.6 collective-permute-start.7
  90.1 2.1 collective-permute-start.8
  92.2 2.1 collective-permute-start.9
  94.2 4.0 %slice.19 = bf16[768,2048]{1,0:T(8,128)(2,1)} slice(bf16[768,7168]{1,0:T(8,128)(2,1)} %all-gather.3.cloned.1.call-done.out_w.small_w.refs_9_.refs_10_.refs_4_.refs_5_), slice={[0:768], [5120:7168]} | slice | bytes 6291456 | tf_op jit(solution)/shard_map/slice | solution.py:985
  98.2 5.0 %local_part.1 = (f32[512,768]{1,0:T(8,128)}, f32[512,128]{1,0:T(8,128)}, f32[768,128]{1,0:T(8,128)}) custom-call(s32[5]{0:T(128)S(1)} %stack.19.meta, f32[512,768]{1,0:T(8,128)} %get-tuple-element.108.resid.refs_7_, f32[512,128]{1,0:T(8,128)} %get-tuple-element.109.stats.refs_9_, bf16[512,768]{1,0:T(8,128)(2,1)} %get-tuple-element.110.grad.refs_10_, ...), custom_call_target="tpu_custom_call" | custom-call | flops 110000000 | bytes 65536 | tf_op jit(solution)/shard_map/local_part/pallas_call | solution.py:73
  103.2 1.3 collective-permute-done.8.refs_2_
  104.5 2.6 collective-permute-done.9.refs_3_
  107.2 0.7 copy-done.13
  107.9 31.1 %expert.1 = (bf16[192,896]{1,0:T(8,128)(2,1)}, bf16[192,896]{1,0:T(8,128)(2,1)}, bf16[192,896]{1,0:T(8,128)(2,1)}, bf16[192,896]{1,0:T(8,128)(2,1)}, bf16[4,192,...) custom-call(s32[5]{0:T(128)S(1)} %stack.19.meta, ...), custom_call_target="tpu_custom_call" | custom-call | flops 11000000512 | bytes 65536 | tf_op jit(solution)/shard_map/expert/pallas_call | solution.py:676
  139.1 0.5 collective-permute-start.14
  139.6 3.4 %collective-permute-start.11 = (bf16[192,896]{1,0:T(8,128)(2,1)}, bf16[192,896]{1,0:T(8,128)(2,1)S(1)}, u32[]{:S(2)}, u32[]{:S(2)}) collective-permute-start(bf16[192,896]{1,0:T(8,128)(2,1)} %get-tuple-element.124), channel_id=1, source_target_pairs={{0,64},{32,96},{64,0},{96,32},{1,65},{33,97},{65,1},{97,33},{2,66}... | collective-permute-start | bytes 1032200 | tf_op jit(solution)/shard_map/ppermute | solution.py:93
  143.0 1.4 collective-permute-start.12
  144.4 2.4 collective-permute-done.14.out_b
  146.8 0.5 collective-permute-done.13.in_b
  147.3 6.0 %add_cores.1.refs_12_ = bf16[16,24,6144]{2,1,0:T(8,128)(2,1)} custom-call(bf16[4,2,16,24,512]{4,3,2,1,0:T(8,128)(2,1)} %get-tuple-element.126.in_a, bf16[4,2,16,24,512]{4,3,2,1,0:T(8,128)(2,1)} %collective-permute-done.13.in_b, bf16[16,64,768]{2,1,0:T(8,128)(2,1)} %get-tuple-element.128.out_a, bf16[16,64,768]{2,1,0:T(8,128)(2,1)S(1)} %collective-permute-done.14.out_b, ...), custom_call_target="tpu_custom_call" | custom-call | flops 110000000 | bytes 65536 | tf_op jit(solution)/shard_map/add_cores/pallas_call | solution.py:740
  153.4 5.4 %collective-permute-done.11.refs_2_ = bf16[192,896]{1,0:T(8,128)(2,1)S(1)} collective-permute-done((bf16[192,896]{1,0:T(8,128)(2,1)}, bf16[192,896]{1,0:T(8,128)(2,1)S(1)}, u32[]{:S(2)}, u32[]{:S(2)}) %collective-permute-start.11) | collective-permute-done | bytes 344096 | tf_op jit(solution)/shard_map/ppermute | solution.py:93
  158.8 2.7 collective-permute-done.12.refs_3_
  161.5 7.6 %unroute.1 = (bf16[768,512]{1,0:T(8,128)(2,1)}, f32[512,768]{1,0:T(8,128)}, bf16[512,768]{1,0:T(8,128)(2,1)}, f32[512,128]{1,0:T(8,128)}, f32[1,768]{1,0:T(1,128)}) custom-call(s32[5]{0:T(128)S(1)} %stack.19.meta, bf16[192,896]{1,0:T(8,128)(2,1)S(1)} %copy-done.9, bf16[192,896]{1,0:T(8,128)(2,1)S(1)} %collective-permute-done.10.refs_1_, ...), custom_call_target="tpu_custom_call" | custom-call | flops 109999996928 | bytes 65536 | tf_op jit(solution)/shard_map/unroute/pallas_call | solution.py:73
  169.1 3.5 %all-to-all-start.2 = ((bf16[4,192,512]{2,1,0:T(8,128)(2,1)}), bf16[4,192,512]{2,1,0:T(8,128)(2,1)S(1)}, u32[]{:S(2)}, u32[]{:S(2)}) async-start(bf16[4,192,512]{2,1,0:T(8,128)(2,1)} %bitcast.51), calls=%async_computation.2 | async-start | bytes 1572864 | tf_op jit(solution)/shard_map/all_to_all | solution.py:105
  172.6 4.2 %dense.1 = (bf16[16,24,896]{2,1,0:T(8,128)(2,1)}, bf16[16,24,896]{2,1,0:T(8,128)(2,1)}) custom-call(s32[5]{0:T(128)S(1)} %stack.19.meta, bf16[768,512]{1,0:T(8,128)(2,1)S(1)} %bitcast.39, bf16[512,768]{1,0:T(8,128)(2,1)} %get-tuple-element.134.dlow, bf16[512,768]{1,0:T(8,128)(2,1)} %get-tuple-element.135.moe, f32[512,128]{1,0:T(8,128)} %get-tuple-element.136.dlogits, ...), custom_call_target="tpu_custom_call" | custom-call | flops 110000000 | bytes 65536 | tf_op jit(solution)/shard_map/dense/pallas_call | solution.py:73
  176.8 6.9 %all-to-all-done.2.refs_0_ = bf16[4,192,512]{2,1,0:T(8,128)(2,1)S(1)} async-done(((bf16[4,192,512]{2,1,0:T(8,128)(2,1)}), bf16[4,192,512]{2,1,0:T(8,128)(2,1)S(1)}, u32[]{:S(2)}, u32[]{:S(2)}) %all-to-all-start.2) | async-done | bytes 786464 | tf_op jit(solution)/shard_map/all_to_all | solution.py:105
  183.7 3.5 %all-to-all-start.3 = ((bf16[4,192,768]{2,1,0:T(8,128)(2,1)}), bf16[4,192,768]{2,1,0:T(8,128)(2,1)S(1)}, u32[]{:S(2)}, u32[]{:S(2)}) async-start(bf16[4,192,768]{2,1,0:T(8,128)(2,1)} %get-tuple-element.133), calls=%async_computation.3 | async-start | bytes 2359296 | tf_op jit(solution)/shard_map/all_to_all | solution.py:105
  187.2 26.9 %attend_back.1 = (bf16[576,512]{1,0:T(8,128)(2,1)}, bf16[576,512]{1,0:T(8,128)(2,1)}, bf16[576,512]{1,0:T(8,128)(2,1)}, bf16[576,512]{1,0:T(8,128)(2,1)}, bf16[1...) custom-call(s32[5]{0:T(128)S(1)} %stack.19.meta, bf16[4,576,512]{2,1,0:T(8,128)(2,1)} %get-tuple-element.142.qkv, ...), custom_call_target="tpu_custom_call" | custom-call | flops 13200000000 | bytes 65536 | tf_op jit(solution)/shard_map/attend_back/pallas_call | solution.py:73
  214.1 3.6 %collective-permute-start.18 = (bf16[576,512]{1,0:T(8,128)(2,1)}, bf16[576,512]{1,0:T(8,128)(2,1)S(1)}, u32[]{:S(2)}, u32[]{:S(2)}) collective-permute-start(bf16[576,512]{1,0:T(8,128)(2,1)} %get-tuple-element.150), channel_id=1, source_target_pairs={{0,64},{32,96},{64,0},{96,32},{1,65},{33,97},{65,1},{97,33},{2,66}... | collective-permute-start | bytes 1769480 | tf_op jit(solution)/shard_map/ppermute | solution.py:93
  217.7 0.6 collective-permute-start.17
  218.3 0.6 collective-permute-start.19
  219.1 2.1 collective-permute-done.16.heads_b
  221.1 1.0 copy-done
  222.2 2.7 add_dense.1
  224.9 7.1 %all-to-all-start.4 = ((bf16[16,24,1536]{2,1,0:T(8,128)(2,1)}), bf16[16,24,1536]{2,1,0:T(8,128)(2,1)S(1)}, u32[]{:S(2)}, u32[]{:S(2)}) async-start(bf16[16,24,1536]{2,1,0:T(8,128)(2,1)} %add_dense.1), calls=%async_computation.4 | async-start | bytes 2359296 | tf_op jit(solution)/shard_map/all_to_all | solution.py:105
  231.9 0.3 collective-permute-done.18.refs_2_
  232.3 0.8 copy-done.6
  233.1 1.9 collective-permute-start.20
  235.0 2.7 collective-permute-start.21
  237.8 7.7 %collective-permute-done.17.refs_1_ = bf16[576,512]{1,0:T(8,128)(2,1)} collective-permute-done((bf16[576,512]{1,0:T(8,128)(2,1)}, bf16[576,512]{1,0:T(8,128)(2,1)}, u32[]{:S(2)}, u32[]{:S(2)}) %collective-permute-start.17) | collective-permute-done | bytes 589856 | tf_op jit(solution)/shard_map/ppermute | solution.py:93
  245.5 1.1 copy-done.7
  246.6 6.8 %finish.1.refs_0_ = bf16[512,768]{1,0:T(8,128)(2,1)} custom-call(s32[5]{0:T(128)S(1)} %stack.19.meta, bf16[576,512]{1,0:T(8,128)(2,1)S(1)} %copy-done.11, bf16[576,512]{1,0:T(8,128)(2,1)} %collective-permute-done.17.refs_1_, bf16[576,512]{1,0:T(8,128)(2,1)S(1)} %copy-done.7, bf16[576,512]{1,0:T(8,128)(2,1)} %collective-permute-done.19.refs_3_, ...), custom_call_target="tpu_custom_call" | custom-call | flops 11000000512 | bytes 65536 | tf_op jit(solution)/shard_map/finish/pallas_call | solution.py:73
  253.4 1.4 add_pieces.1.refs_1_.refs_0_
  254.8 1.5 collective-permute-start.23
  256.3 2.3 collective-permute-start.24
  258.7 0.9 collective-permute-start.25
  259.6 2.1 gather.1
  261.7 3.6 %mixed.1 = bf16[512,768]{1,0:T(8,128)(2,1)} custom-call(s32[5]{0:T(128)S(1)} %stack.19.meta, f32[512,768]{1,0:T(8,128)} %get-tuple-element.112.partial, bf16[4,192,512]{2,1,0:T(8,128)(2,1)} %get-tuple-element.107.slots.refs_6_, bf16[4,192,768]{2,1,0:T(8,128)(2,1)S(1)} %copy-done.1, bf16[24,1536]{1,0:T(8,128)(2,1)} %add_pieces.1.refs_1_.refs_0_), custom_call_target="tpu_custom_call" | custom-call | flops 110000000 | bytes 65536 | tf_op jit(solution)/shard_map/mixed/pallas_call | solution.py:73
  265.2 2.0 gather_dense.1
  (61 shorter events, 0.9 us)
Async XLA Ops:
  7.2 76.5 %all-gather.3.cloned.1.call-start = ((), (), s32[]{:S(2)}) async-start(), calls=%async_computation.6 | async-start | bytes 11354112 | tf_op jit(solution)/shard_map/all_gather | solution.py:981
  8.0 3.3 %copy-start.5 = (bf16[1,512,768]{2,1,0:T(8,128)(2,1)S(1)}, bf16[1,512,768]{2,1,0:T(8,128)(2,1)}, u32[]{:S(2)}) copy-start(bf16[1,512,768]{2,1,0:T(8,128)(2,1)} %param.15) | copy-start | bytes 2359300
  11.3 20.6 %collective-permute-start = (bf16[512,768]{1,0:T(8,128)(2,1)S(1)}, bf16[512,768]{1,0:T(8,128)(2,1)S(1)}, u32[]{:S(2)}, u32[]{:S(2)}) collective-permute-start(bf16[512,768]{1,0:T(8,128)(2,1)S(1)} %bitcast.44), channel_id=1, source_target_pairs={{0,32},{32,64},{64,96},{96,0},{1,33},{33,65},{65,97},{97,1},{2,34}... | collective-permute-start | bytes 2359304 | tf_op jit(solution)/shard_map/ppermute | solution.py:88
  12.8 20.1 %collective-permute-start.1 = (bf16[512,768]{1,0:T(8,128)(2,1)S(1)}, bf16[512,768]{1,0:T(8,128)(2,1)S(1)}, u32[]{:S(2)}, u32[]{:S(2)}) collective-permute-start(bf16[512,768]{1,0:T(8,128)(2,1)S(1)} %bitcast.45), channel_id=1, source_target_pairs={{0,96},{32,0},{64,32},{96,64},{1,97},{33,1},{65,33},{97,65},{2,98}... | collective-permute-start | bytes 2359304 | tf_op jit(solution)/shard_map/ppermute | solution.py:88
  14.6 32.3 %all-to-all-start = ((bf16[32,24,640]{2,1,0:T(8,128)(2,1)}), bf16[32,24,640]{2,1,0:T(8,128)(2,1)S(1)}, u32[]{:S(2)}, u32[]{:S(2)}) async-start(bf16[32,24,640]{2,1,0:T(8,128)(2,1)} %get-tuple-element.97), calls=%async_computation | async-start | bytes 1966080 | tf_op jit(solution)/shard_map/all_to_all | solution.py:105
  32.6 14.5 %collective-permute-start.2 = (bf16[256,768]{1,0:T(8,128)(2,1)}, bf16[256,768]{1,0:T(8,128)(2,1)}, u32[]{:S(2)}, u32[]{:S(2)}) collective-permute-start(bf16[256,768]{1,0:T(8,128)(2,1)} %slice.16), channel_id=1, source_target_pairs={{0,32},{32,64},{64,96},{96,0},{1,33},{33,65},{65,97},{97,1},{2,34}... | collective-permute-start | bytes 1179656 | tf_op jit(solution)/shard_map/ppermute | solution.py:88
  33.7 13.5 %collective-permute-start.3 = (bf16[256,768]{1,0:T(8,128)(2,1)}, bf16[256,768]{1,0:T(8,128)(2,1)}, u32[]{:S(2)}, u32[]{:S(2)}) collective-permute-start(bf16[256,768]{1,0:T(8,128)(2,1)} %slice.17), channel_id=1, source_target_pairs={{0,96},{32,0},{64,32},{96,64},{1,97},{33,1},{65,33},{97,65},{2,98}... | collective-permute-start | bytes 1179656 | tf_op jit(solution)/shard_map/ppermute | solution.py:88
  42.0 27.5 %collective-permute-start.4 = (bf16[192,768]{1,0:T(8,128)(2,1)}, bf16[192,768]{1,0:T(8,128)(2,1)}, u32[]{:S(2)}, u32[]{:S(2)}) collective-permute-start(bf16[192,768]{1,0:T(8,128)(2,1)} %get-tuple-element.101), channel_id=1, source_target_pairs={{0,32},{32,0},{64,96},{96,64},{1,33},{33,1},{65,97},{97,65},{2,34}... | collective-permute-start | bytes 884744 | tf_op jit(solution)/shard_map/ppermute | solution.py:93
  42.0 27.5 %collective-permute-start.5 = (bf16[192,768]{1,0:T(8,128)(2,1)}, bf16[192,768]{1,0:T(8,128)(2,1)}, u32[]{:S(2)}, u32[]{:S(2)}) collective-permute-start(bf16[192,768]{1,0:T(8,128)(2,1)} %get-tuple-element.102), channel_id=1, source_target_pairs={{0,64},{32,96},{64,0},{96,32},{1,65},{33,97},{65,1},{97,33},{2,66}... | collective-permute-start | bytes 884744 | tf_op jit(solution)/shard_map/ppermute | solution.py:93
  43.8 25.7 %collective-permute-start.6 = (bf16[192,768]{1,0:T(8,128)(2,1)}, bf16[192,768]{1,0:T(8,128)(2,1)}, u32[]{:S(2)}, u32[]{:S(2)}) collective-permute-start(bf16[192,768]{1,0:T(8,128)(2,1)} %get-tuple-element.103), channel_id=1, source_target_pairs={{0,96},{32,64},{64,32},{96,0},{1,97},{33,65},{65,33},{97,1},{2,98}... | collective-permute-start | bytes 884744 | tf_op jit(solution)/shard_map/ppermute | solution.py:93
  47.2 6.1 %copy-start.4 = (f32[1,768]{1,0:T(1,128)}, f32[1,768]{1,0:T(1,128)S(1)}, u32[]{:S(2)}) copy-start(f32[1,768]{1,0:T(1,128)S(1)} %reshape.104.refs_6_) | copy-start | bytes 9220
  69.5 14.2 %all-to-all-start.1 = ((bf16[4,192,512]{2,1,0:T(8,128)(2,1)}), bf16[4,192,512]{2,1,0:T(8,128)(2,1)S(1)}, u32[]{:S(2)}, u32[]{:S(2)}) async-start(bf16[4,192,512]{2,1,0:T(8,128)(2,1)} %get-tuple-element.104.refs_1_), calls=%async_computation.1 | async-start | bytes 1572864 | tf_op jit(solution)/shard_map/all_to_all | solution.py:105
  73.0 71.4 %all-gather.5.cloned.1.call-start = ((), (), s32[]{:S(2)}) async-start(), calls=%async_computation.7 | async-start | bytes 3649536 | tf_op jit(solution)/shard_map/all_gather | solution.py:982
  73.8 159.3 %reduce-scatter.4.cloned.1.call-start = ((), (), s32[]{:S(2)}) async-start(), calls=%async_computation.8 | async-start | bytes 5013504
  89.5 13.7 %collective-permute-start.7 = (bf16[192,896]{1,0:T(8,128)(2,1)}, bf16[192,896]{1,0:T(8,128)(2,1)S(1)}, u32[]{:S(2)}, u32[]{:S(2)}) collective-permute-start(bf16[192,896]{1,0:T(8,128)(2,1)} %get-tuple-element.114), channel_id=1, source_target_pairs={{0,32},{32,0},{64,96},{96,64},{1,33},{33,1},{65,97},{97,65},{2,34}... | collective-permute-start | bytes 1032200 | tf_op jit(solution)/shard_map/ppermute | solution.py:93
  90.1 14.4 %collective-permute-start.8 = (bf16[192,896]{1,0:T(8,128)(2,1)}, bf16[192,896]{1,0:T(8,128)(2,1)S(1)}, u32[]{:S(2)}, u32[]{:S(2)}) collective-permute-start(bf16[192,896]{1,0:T(8,128)(2,1)} %get-tuple-element.115), channel_id=1, source_target_pairs={{0,64},{32,96},{64,0},{96,32},{1,65},{33,97},{65,1},{97,33},{2,66}... | collective-permute-start | bytes 1032200 | tf_op jit(solution)/shard_map/ppermute | solution.py:93
  92.2 15.0 %collective-permute-start.9 = (bf16[192,896]{1,0:T(8,128)(2,1)}, bf16[192,896]{1,0:T(8,128)(2,1)S(1)}, u32[]{:S(2)}, u32[]{:S(2)}) collective-permute-start(bf16[192,896]{1,0:T(8,128)(2,1)} %get-tuple-element.116), channel_id=1, source_target_pairs={{0,96},{32,64},{64,32},{96,0},{1,97},{33,65},{65,33},{97,1},{2,98}... | collective-permute-start | bytes 1032200 | tf_op jit(solution)/shard_map/ppermute | solution.py:93
  98.2 9.7 %copy-start.8 = (bf16[192,768]{1,0:T(8,128)(2,1)S(1)}, bf16[192,768]{1,0:T(8,128)(2,1)}, u32[]{:S(2)}) copy-start(bf16[192,768]{1,0:T(8,128)(2,1)} %get-tuple-element.117.refs_4_) | copy-start | bytes 884740
  98.2 9.7 %copy-start.10 = (bf16[192,896]{1,0:T(8,128)(2,1)S(1)}, bf16[192,896]{1,0:T(8,128)(2,1)}, u32[]{:S(2)}) copy-start(bf16[192,896]{1,0:T(8,128)(2,1)} %get-tuple-element.113.refs_0_) | copy-start | bytes 1032196
  104.5 2.6 copy-start.12
  107.2 0.7 copy-start.13
  139.0 8.3 %collective-permute-start.13 = (bf16[4,2,16,24,512]{4,3,2,1,0:T(8,128)(2,1)}, bf16[4,2,16,24,512]{4,3,2,1,0:T(8,128)(2,1)}, u32[]{:S(2)}, u32[]{:S(2)}) collective-permute-start(bf16[4,2,16,24,512]{4,3,2,1,0:T(8,128)(2,1)} %get-tuple-element.127), channel_id=1, source_target_pairs={{0,1},{1,0},{2,3},{3,2},{4,5},{5,4},{6,7},{7,6},{8,9},{9,8},{10,11... | collective-permute-start | bytes 9437192 | tf_op jit(solution)/shard_map/ppermute | solution.py:93
  139.1 7.7 %collective-permute-start.14 = (bf16[16,64,768]{2,1,0:T(8,128)(2,1)}, bf16[16,64,768]{2,1,0:T(8,128)(2,1)S(1)}, u32[]{:S(2)}, u32[]{:S(2)}) collective-permute-start(bf16[16,64,768]{2,1,0:T(8,128)(2,1)} %get-tuple-element.129), channel_id=1, source_target_pairs={{0,1},{1,0},{2,3},{3,2},{4,5},{5,4},{6,7},{7,6},{8,9},{9,8},{10,11... | collective-permute-start | bytes 4718600 | tf_op jit(solution)/shard_map/ppermute | solution.py:93
  139.6 13.8 %collective-permute-start.10 = (bf16[192,896]{1,0:T(8,128)(2,1)}, bf16[192,896]{1,0:T(8,128)(2,1)S(1)}, u32[]{:S(2)}, u32[]{:S(2)}) collective-permute-start(bf16[192,896]{1,0:T(8,128)(2,1)} %get-tuple-element.123), channel_id=1, source_target_pairs={{0,32},{32,0},{64,96},{96,64},{1,33},{33,1},{65,97},{97,65},{2,34}... | collective-permute-start | bytes 1032200 | tf_op jit(solution)/shard_map/ppermute | solution.py:93
  139.6 19.2 %collective-permute-start.11 = (bf16[192,896]{1,0:T(8,128)(2,1)}, bf16[192,896]{1,0:T(8,128)(2,1)S(1)}, u32[]{:S(2)}, u32[]{:S(2)}) collective-permute-start(bf16[192,896]{1,0:T(8,128)(2,1)} %get-tuple-element.124), channel_id=1, source_target_pairs={{0,64},{32,96},{64,0},{96,32},{1,65},{33,97},{65,1},{97,33},{2,66}... | collective-permute-start | bytes 1032200 | tf_op jit(solution)/shard_map/ppermute | solution.py:93
  143.0 18.4 %collective-permute-start.12 = (bf16[192,896]{1,0:T(8,128)(2,1)}, bf16[192,896]{1,0:T(8,128)(2,1)S(1)}, u32[]{:S(2)}, u32[]{:S(2)}) collective-permute-start(bf16[192,896]{1,0:T(8,128)(2,1)} %get-tuple-element.125), channel_id=1, source_target_pairs={{0,96},{32,64},{64,32},{96,0},{1,97},{33,65},{65,33},{97,1},{2,98}... | collective-permute-start | bytes 1032200 | tf_op jit(solution)/shard_map/ppermute | solution.py:93
  153.4 8.1 %copy-start.9 = (bf16[192,896]{1,0:T(8,128)(2,1)S(1)}, bf16[192,896]{1,0:T(8,128)(2,1)}, u32[]{:S(2)}) copy-start(bf16[192,896]{1,0:T(8,128)(2,1)} %get-tuple-element.122.refs_0_) | copy-start | bytes 1032196
  169.1 14.6 %all-to-all-start.2 = ((bf16[4,192,512]{2,1,0:T(8,128)(2,1)}), bf16[4,192,512]{2,1,0:T(8,128)(2,1)S(1)}, u32[]{:S(2)}, u32[]{:S(2)}) async-start(bf16[4,192,512]{2,1,0:T(8,128)(2,1)} %bitcast.51), calls=%async_computation.2 | async-start | bytes 1572864 | tf_op jit(solution)/shard_map/all_to_all | solution.py:105
  176.7 42.3 %collective-permute-start.15 = (bf16[16,24,896]{2,1,0:T(8,128)(2,1)}, bf16[16,24,896]{2,1,0:T(8,128)(2,1)S(1)}, u32[]{:S(2)}, u32[]{:S(2)}) collective-permute-start(bf16[16,24,896]{2,1,0:T(8,128)(2,1)} %get-tuple-element.141), channel_id=1, source_target_pairs={{0,1},{1,0},{2,3},{3,2},{4,5},{5,4},{6,7},{7,6},{8,9},{9,8},{10,11... | collective-permute-start | bytes 2064392 | tf_op jit(solution)/shard_map/ppermute | solution.py:93
  183.7 37.5 %all-to-all-start.3 = ((bf16[4,192,768]{2,1,0:T(8,128)(2,1)}), bf16[4,192,768]{2,1,0:T(8,128)(2,1)S(1)}, u32[]{:S(2)}, u32[]{:S(2)}) async-start(bf16[4,192,768]{2,1,0:T(8,128)(2,1)} %get-tuple-element.133), calls=%async_computation.3 | async-start | bytes 2359296 | tf_op jit(solution)/shard_map/all_to_all | solution.py:105
  214.1 18.1 %collective-permute-start.18 = (bf16[576,512]{1,0:T(8,128)(2,1)}, bf16[576,512]{1,0:T(8,128)(2,1)S(1)}, u32[]{:S(2)}, u32[]{:S(2)}) collective-permute-start(bf16[576,512]{1,0:T(8,128)(2,1)} %get-tuple-element.150), channel_id=1, source_target_pairs={{0,64},{32,96},{64,0},{96,32},{1,65},{33,97},{65,1},{97,33},{2,66}... | collective-permute-start | bytes 1769480 | tf_op jit(solution)/shard_map/ppermute | solution.py:93
  217.7 27.8 %collective-permute-start.17 = (bf16[576,512]{1,0:T(8,128)(2,1)}, bf16[576,512]{1,0:T(8,128)(2,1)}, u32[]{:S(2)}, u32[]{:S(2)}) collective-permute-start(bf16[576,512]{1,0:T(8,128)(2,1)} %get-tuple-element.149), channel_id=1, source_target_pairs={{0,32},{32,0},{64,96},{96,64},{1,33},{33,1},{65,97},{97,65},{2,34}... | collective-permute-start | bytes 1769480 | tf_op jit(solution)/shard_map/ppermute | solution.py:93
  218.3 27.2 %collective-permute-start.19 = (bf16[576,512]{1,0:T(8,128)(2,1)}, bf16[576,512]{1,0:T(8,128)(2,1)}, u32[]{:S(2)}, u32[]{:S(2)}) collective-permute-start(bf16[576,512]{1,0:T(8,128)(2,1)} %get-tuple-element.152), channel_id=1, source_target_pairs={{0,96},{32,64},{64,32},{96,0},{1,97},{33,65},{65,33},{97,1},{2,98}... | collective-permute-start | bytes 1769480 | tf_op jit(solution)/shard_map/ppermute | solution.py:93
  218.9 2.3 collective-permute-start.16
  221.1 1.0 copy-start
  224.9 20.7 %copy-start.11 = (bf16[576,512]{1,0:T(8,128)(2,1)S(1)}, bf16[576,512]{1,0:T(8,128)(2,1)}, u32[]{:S(2)}) copy-start(bf16[576,512]{1,0:T(8,128)(2,1)} %get-tuple-element.148.refs_0_) | copy-start | bytes 1769476
  224.9 28.5 %all-to-all-start.4 = ((bf16[16,24,1536]{2,1,0:T(8,128)(2,1)}), bf16[16,24,1536]{2,1,0:T(8,128)(2,1)S(1)}, u32[]{:S(2)}, u32[]{:S(2)}) async-start(bf16[16,24,1536]{2,1,0:T(8,128)(2,1)} %add_dense.1), calls=%async_computation.4 | async-start | bytes 2359296 | tf_op jit(solution)/shard_map/all_to_all | solution.py:105
  232.2 0.8 copy-start.6
  233.1 21.7 %collective-permute-start.20 = (bf16[24,6144]{1,0:T(8,128)(2,1)}, bf16[24,6144]{1,0:T(8,128)(2,1)S(1)}, u32[]{:S(2)}, u32[]{:S(2)}) collective-permute-start(bf16[24,6144]{1,0:T(8,128)(2,1)} %reduce-scatter.4.cloned.1.call-done.refs_0_), channel_id=1, source_target_pairs={{0,32},{32,0},{64,96},{96,64},{1,33},{33,1},{65,97},{97,65},{2,34}... | collective-permute-start | bytes 884744 | tf_op jit(solution)/shard_map/ppermute | solution.py:93
  235.0 19.8 %collective-permute-start.21 = (bf16[24,6144]{1,0:T(8,128)(2,1)}, bf16[24,6144]{1,0:T(8,128)(2,1)S(1)}, u32[]{:S(2)}, u32[]{:S(2)}) collective-permute-start(bf16[24,6144]{1,0:T(8,128)(2,1)} %reduce-scatter.4.cloned.1.call-done.refs_0_), channel_id=1, source_target_pairs={{0,64},{32,96},{64,0},{96,32},{1,65},{33,97},{65,1},{97,33},{2,66}... | collective-permute-start | bytes 884744 | tf_op jit(solution)/shard_map/ppermute | solution.py:93
  237.7 17.1 %collective-permute-start.22 = (bf16[24,6144]{1,0:T(8,128)(2,1)}, bf16[24,6144]{1,0:T(8,128)(2,1)S(1)}, u32[]{:S(2)}, u32[]{:S(2)}) collective-permute-start(bf16[24,6144]{1,0:T(8,128)(2,1)} %reduce-scatter.4.cloned.1.call-done.refs_0_), channel_id=1, source_target_pairs={{0,96},{32,64},{64,32},{96,0},{1,97},{33,65},{65,33},{97,1},{2,98}... | collective-permute-start | bytes 884744 | tf_op jit(solution)/shard_map/ppermute | solution.py:93
  245.5 1.1 copy-start.7
  253.4 6.2 %copy-start.3 = (bf16[24,6144]{1,0:T(8,128)(2,1)S(1)}, bf16[24,6144]{1,0:T(8,128)(2,1)}, u32[]{:S(2)}) copy-start(bf16[24,6144]{1,0:T(8,128)(2,1)} %reduce-scatter.4.cloned.1.call-done.refs_0_) | copy-start | bytes 884740
  253.4 8.3 %copy-start.1 = (bf16[4,192,768]{2,1,0:T(8,128)(2,1)S(1)}, bf16[4,192,768]{2,1,0:T(8,128)(2,1)}, u32[]{:S(2)}) copy-start(bf16[4,192,768]{2,1,0:T(8,128)(2,1)} %copy-done) | copy-start | bytes 3538948
  254.8 10.4 %collective-permute-start.23 = (bf16[24,1536]{1,0:T(8,128)(2,1)}, bf16[24,1536]{1,0:T(8,128)(2,1)S(1)}, u32[]{:S(2)}, u32[]{:S(2)}) collective-permute-start(bf16[24,1536]{1,0:T(8,128)(2,1)} %add_pieces.1.refs_1_.refs_0_), channel_id=1, source_target_pairs={{0,32},{32,0},{64,96},{96,64},{1,33},{33,1},{65,97},{97,65},{2,34}... | collective-permute-start | bytes 221192 | tf_op jit(solution)/shard_map/ppermute | solution.py:93
  256.3 8.9 %collective-permute-start.24 = (bf16[24,1536]{1,0:T(8,128)(2,1)}, bf16[24,1536]{1,0:T(8,128)(2,1)S(1)}, u32[]{:S(2)}, u32[]{:S(2)}) collective-permute-start(bf16[24,1536]{1,0:T(8,128)(2,1)} %add_pieces.1.refs_1_.refs_0_), channel_id=1, source_target_pairs={{0,64},{32,96},{64,0},{96,32},{1,65},{33,97},{65,1},{97,33},{2,66}... | collective-permute-start | bytes 221192 | tf_op jit(solution)/shard_map/ppermute | solution.py:93
  258.7 6.6 %collective-permute-start.25 = (bf16[24,1536]{1,0:T(8,128)(2,1)}, bf16[24,1536]{1,0:T(8,128)(2,1)S(1)}, u32[]{:S(2)}, u32[]{:S(2)}) collective-permute-start(bf16[24,1536]{1,0:T(8,128)(2,1)} %add_pieces.1.refs_1_.refs_0_), channel_id=1, source_target_pairs={{0,96},{32,64},{64,32},{96,0},{1,97},{33,65},{65,33},{97,1},{2,98}... | collective-permute-start | bytes 221192 | tf_op jit(solution)/shard_map/ppermute | solution.py:93
  261.7 3.6 %copy-start.2 = (bf16[24,1536]{1,0:T(8,128)(2,1)S(1)}, bf16[24,1536]{1,0:T(8,128)(2,1)}, u32[]{:S(2)}) copy-start(bf16[24,1536]{1,0:T(8,128)(2,1)} %add_pieces.1.refs_1_.refs_0_) | copy-start | bytes 221188
Sparse Core Ops, SparseCore 0:
  11.4 64.0 all-gather.2
  77.8 44.8 all-gather.4
  153.5 76.5 reduce-scatter.3

commit v3 on v2

--- a/solution.py
+++ b/solution.py
@@ -94,7 +94,8 @@
 
 
 def trades(pieces, axis="seq"):
-    return [trade(piece, k, axis) for k, piece in enumerate(pieces)]
+    done = {k: trade(pieces[k], k, axis) for k in (2, 1, 3)}
+    return [pieces[0]] + [done[k] for k in (1, 2, 3)]
 
 
 def around(meta, by):
@@ -1032,13 +1033,13 @@
     come_heads = trade(gone, 1, "core")
     back_all = trades(dproj)
     sums = add_dense(meta, kept, come_dense, heads, come_heads, branch)
+    mixed_out = mixed(meta, partial, slots, branch, sums)
     sums = swap(sums, YZ)
     part, back_all[2] = lax.optimization_barrier((part, back_all[2]))
     pieces = trades([part] * seqs)
-    grad_tokens = finish(meta, back_all, back_w, tok, gain_a, dres)
+    grad_tokens = finish(meta, back_all, back_w, tok, gain_a, dres, mixed_out)
     sums = add_pieces(meta, sums, grad_tokens)
     sums, *pieces = lax.optimization_barrier((sums, *pieces))
-    mixed_out = mixed(meta, partial, slots, branch, sums)
     sums = trades([sums] * seqs)
     grad_attend_in, grad_gain_a, grad_att_out, *rest, table = gather_dense(
         meta, sums, attend_in, gain_attend[None]

time: 279 us -> 279 us (level)
  the two profiles are of different devices: /device:TPU:88 before, /device:TPU:0 now
where the time goes in v3:
time: 279 us; the launch traced here: 274 us
  Pallas kernels  134 us (48%)
  starting transfers between devices  64.5 us (23%)
  waiting for transfers between devices  49.4 us (18%)
  between operations  14.9 us (5%)
  local copies, waits for them, and re-layouts  9.38 us (3%)
    pallas_call x13, Pallas kernels, one_step(): pl.pallas_call(body, grid=(1,), in_specs=[SMEM] + [spec for _, spec in in...  77.6 us
    pallas_call x1, Pallas kernels, expert(): pl.pallas_call(expert_kernel, grid=(steps,), in_specs=[SMEM] + [whole(x)...  30.8 us
    ppermute x22, starting transfers between devices, trade(): lax.ppermute(x, axis, [(i, i ^ by) for i in range(count)])  29.4 us
    all_to_all x5, starting transfers between devices, swap(): return lax.all_to_all(x, axis, split_axis=0, concat_axis=0, tiled=True)  28 us
    ppermute x22, waiting for transfers between devices, trade(): lax.ppermute(x, axis, [(i, i ^ by) for i in range(count)])  21.5 us
    all_to_all x5, waiting for transfers between devices, swap(): return lax.all_to_all(x, axis, split_axis=0, concat_axis=0, tiled=True)  18.5 us
    pallas_call x1, Pallas kernels, attend(): pl.pallas_call(attend_kernel, grid=(1,), in_specs=[SMEM, VMEM], out_specs...  16.2 us
    ppermute x4, waiting for transfers between devices, shift(): return lax.ppermute(x, 'seq', [(i, (i + by) % count) for i in range(count)])  8.7 us
  transfers between devices with their start and end apart: 34, of which 14 were waited for; matrix products, arithmetic and copies ran while one was open for 3% of the time, Pallas kernels for 47%

profile of v3, /device:TPU:0, one launch (start us, length us, event | category | flops | bytes accessed | tf_op | source)
XLA Modules:
  0.0 274.2 jit_solution(10536616325900568063)
XLA Ops:
  8.0 3.3 %pack.1 = (bf16[32,24,640]{2,1,0:T(8,128)(2,1)}, bf16[24,7168]{1,0:T(8,128)(2,1)}, bf16[24,2304]{1,0:T(8,128)(2,1)}) custom-call(s32[5]{0:T(128)S(1)} %stack.19.meta, f32[24,2304]{1,0:T(8,128)} %refs_4_.1, f32[1,24]{1,0:T(1,128)} %bitcast.52, f32[24,768]{1,0:T(8,128)} %attend_out.1, f32[8,24]{1,0:T(8,128)} %bitcast.55, f32[4,24]{1,0:T(4,128)} %bitcast.59, ...), custom_call_target="tpu_custom_call" | custom-call | flops 2200000000 | bytes 65536 | tf_op jit(solution)/shard_map/pack/pallas_call | solution.py:206
  11.3 1.6 collective-permute-start
  12.9 1.7 collective-permute-start.1
  14.6 8.4 %all-to-all-start = ((bf16[32,24,640]{2,1,0:T(8,128)(2,1)}), bf16[32,24,640]{2,1,0:T(8,128)(2,1)S(1)}, u32[]{:S(2)}, u32[]{:S(2)}) async-start(bf16[32,24,640]{2,1,0:T(8,128)(2,1)} %get-tuple-element.97), calls=%async_computation | async-start | bytes 1966080 | tf_op jit(solution)/shard_map/all_to_all | solution.py:106
  23.0 8.7 %collective-permute-done.refs_1_ = bf16[512,768]{1,0:T(8,128)(2,1)S(1)} collective-permute-done((bf16[512,768]{1,0:T(8,128)(2,1)S(1)}, bf16[512,768]{1,0:T(8,128)(2,1)S(1)}, u32[]{:S(2)}, u32[]{:S(2)}) %collective-permute-start) | collective-permute-done | bytes 786464 | tf_op jit(solution)/shard_map/ppermute | solution.py:88
  31.7 0.8 slice.16
  33.0 0.8 slice.17
  33.8 2.8 %collective-permute-start.3 = (bf16[256,768]{1,0:T(8,128)(2,1)}, bf16[256,768]{1,0:T(8,128)(2,1)}, u32[]{:S(2)}, u32[]{:S(2)}) collective-permute-start(bf16[256,768]{1,0:T(8,128)(2,1)} %slice.17), channel_id=1, source_target_pairs={{0,96},{32,0},{64,32},{96,64},{1,97},{33,1},{65,33},{97,65},{2,98}... | collective-permute-start | bytes 1179656 | tf_op jit(solution)/shard_map/ppermute | solution.py:88
  36.5 3.5 %plan.1 = (bf16[4,192,512]{2,1,0:T(8,128)(2,1)}, bf16[512,768]{1,0:T(8,128)(2,1)}, f32[512,128]{1,0:T(8,128)}, bf16[512,128]{1,0:T(8,128)(2,1)}, bf16[192,768]{1...) custom-call(s32[5]{0:T(128)S(1)} %stack.19.meta, ...), custom_call_target="tpu_custom_call" | custom-call | flops 1100000000 | bytes 65536 | tf_op jit(solution)/shard_map/plan/pallas_call | solution.py:73
  40.1 1.8 multiply_sine_fusion
  41.9 2.0 collective-permute-start.5
  43.9 2.9 %collective-permute-start.6 = (bf16[192,768]{1,0:T(8,128)(2,1)}, bf16[192,768]{1,0:T(8,128)(2,1)}, u32[]{:S(2)}, u32[]{:S(2)}) collective-permute-start(bf16[192,768]{1,0:T(8,128)(2,1)} %get-tuple-element.103), channel_id=1, source_target_pairs={{0,96},{32,64},{64,32},{96,0},{1,97},{33,65},{65,33},{97,1},{2,98}... | collective-permute-start | bytes 884744 | tf_op jit(solution)/shard_map/ppermute | solution.py:93
  47.0 6.3 %project.1 = (bf16[4,576,512]{2,1,0:T(8,128)(2,1)S(1)}, bf16[4,512,768]{2,1,0:T(8,128)(2,1)}) custom-call(s32[5]{0:T(128)S(1)} %stack.19.meta, bf16[512,768]{1,0:T(8,128)(2,1)S(1)} %bitcast.46, bf16[512,768]{1,0:T(8,128)(2,1)S(1)} %collective-permute-done.refs_1_, bf16[512,768]{1,0:T(8,128)(2,1)S(1)} %collective-permute-done.1.refs_2_, ...), custom_call_target="tpu_custom_call" | custom-call | flops 109999996928 | bytes 65536 | tf_op jit(solution)/shard_map/project/pallas_call | solution.py:73
  53.3 16.2 %attend.1 = (bf16[4,192,512]{2,1,0:T(8,128)(2,1)}, f32[4,8,512]{2,1,0:T(8,128)}, bf16[4,576,512]{2,1,0:T(8,128)(2,1)}) custom-call(s32[5]{0:T(128)S(1)} %stack.19.meta, bf16[4,576,512]{2,1,0:T(8,128)(2,1)S(1)} %get-tuple-element.98.qkv), custom_call_target="tpu_custom_call" | custom-call | flops 110000000 | bytes 65536 | tf_op jit(solution)/shard_map/attend/pallas_call | solution.py:350
  69.5 3.6 %all-to-all-start.1 = ((bf16[4,192,512]{2,1,0:T(8,128)(2,1)}), bf16[4,192,512]{2,1,0:T(8,128)(2,1)S(1)}, u32[]{:S(2)}, u32[]{:S(2)}) async-start(bf16[4,192,512]{2,1,0:T(8,128)(2,1)} %get-tuple-element.104.refs_1_), calls=%async_computation.1 | async-start | bytes 1572864 | tf_op jit(solution)/shard_map/all_to_all | solution.py:106
  73.2 0.7 all-gather.5.cloned.1.call-update
  73.9 0.5 reduce-scatter.4.cloned.1.call-start
  74.4 9.0 %all-to-all-done.1 = bf16[4,192,512]{2,1,0:T(8,128)(2,1)S(1)} async-done(((bf16[4,192,512]{2,1,0:T(8,128)(2,1)}), bf16[4,192,512]{2,1,0:T(8,128)(2,1)S(1)}, u32[]{:S(2)}, u32[]{:S(2)}) %all-to-all-start.1) | async-done | bytes 786464 | tf_op jit(solution)/shard_map/all_to_all | solution.py:106
  83.4 5.9 %route.1 = (bf16[192,896]{1,0:T(8,128)(2,1)}, bf16[192,896]{1,0:T(8,128)(2,1)}, bf16[192,896]{1,0:T(8,128)(2,1)}, bf16[192,896]{1,0:T(8,128)(2,1)}, f32[512,768]...) custom-call(s32[5]{0:T(128)S(1)} %stack.19.meta, bf16[768,512]{1,0:T(8,128)(2,1)S(1)} %bitcast.38, ...), custom_call_target="tpu_custom_call" | custom-call | flops 109999996928 | bytes 65536 | tf_op jit(solution)/shard_map/route/pallas_call | solution.py:73
  89.3 0.6 collective-permute-start.7
  89.8 2.1 collective-permute-start.8
  92.0 2.0 collective-permute-start.9
  94.0 4.0 %slice.19 = bf16[768,2048]{1,0:T(8,128)(2,1)} slice(bf16[768,7168]{1,0:T(8,128)(2,1)} %all-gather.3.cloned.1.call-done.out_w.small_w.refs_9_.refs_10_.refs_4_.refs_5_), slice={[0:768], [5120:7168]} | slice | bytes 6291456 | tf_op jit(solution)/shard_map/slice | solution.py:986
  98.0 4.9 %local_part.1 = (f32[512,768]{1,0:T(8,128)}, f32[512,128]{1,0:T(8,128)}, f32[768,128]{1,0:T(8,128)}) custom-call(s32[5]{0:T(128)S(1)} %stack.19.meta, f32[512,768]{1,0:T(8,128)} %get-tuple-element.108.resid.refs_7_, f32[512,128]{1,0:T(8,128)} %get-tuple-element.109.stats.refs_9_, bf16[512,768]{1,0:T(8,128)(2,1)} %get-tuple-element.110.grad.refs_10_, ...), custom_call_target="tpu_custom_call" | custom-call | flops 110000000 | bytes 65536 | tf_op jit(solution)/shard_map/local_part/pallas_call | solution.py:73
  102.9 1.3 collective-permute-done.8.refs_2_
  104.2 2.6 collective-permute-done.9.refs_3_
  106.9 0.7 copy-done.11
  107.6 30.8 %expert.1 = (bf16[192,896]{1,0:T(8,128)(2,1)}, bf16[192,896]{1,0:T(8,128)(2,1)}, bf16[192,896]{1,0:T(8,128)(2,1)}, bf16[192,896]{1,0:T(8,128)(2,1)}, bf16[4,192,...) custom-call(s32[5]{0:T(128)S(1)} %stack.19.meta, ...), custom_call_target="tpu_custom_call" | custom-call | flops 11000000512 | bytes 65536 | tf_op jit(solution)/shard_map/expert/pallas_call | solution.py:677
  139.0 3.1 %collective-permute-start.11 = (bf16[192,896]{1,0:T(8,128)(2,1)}, bf16[192,896]{1,0:T(8,128)(2,1)S(1)}, u32[]{:S(2)}, u32[]{:S(2)}) collective-permute-start(bf16[192,896]{1,0:T(8,128)(2,1)} %get-tuple-element.124), channel_id=1, source_target_pairs={{0,64},{32,96},{64,0},{96,32},{1,65},{33,97},{65,1},{97,33},{2,66}... | collective-permute-start | bytes 1032200 | tf_op jit(solution)/shard_map/ppermute | solution.py:93
  142.1 1.7 collective-permute-start.12
  143.9 2.4 collective-permute-done.14.out_b
  146.3 0.5 collective-permute-done.13.in_b
  146.8 6.1 %add_cores.1.refs_12_ = bf16[16,24,6144]{2,1,0:T(8,128)(2,1)} custom-call(bf16[4,2,16,24,512]{4,3,2,1,0:T(8,128)(2,1)} %get-tuple-element.126.in_a, bf16[4,2,16,24,512]{4,3,2,1,0:T(8,128)(2,1)} %collective-permute-done.13.in_b, bf16[16,64,768]{2,1,0:T(8,128)(2,1)} %get-tuple-element.128.out_a, bf16[16,64,768]{2,1,0:T(8,128)(2,1)S(1)} %collective-permute-done.14.out_b, ...), custom_call_target="tpu_custom_call" | custom-call | flops 110000000 | bytes 65536 | tf_op jit(solution)/shard_map/add_cores/pallas_call | solution.py:741
  152.9 5.0 %collective-permute-done.11.refs_2_ = bf16[192,896]{1,0:T(8,128)(2,1)S(1)} collective-permute-done((bf16[192,896]{1,0:T(8,128)(2,1)}, bf16[192,896]{1,0:T(8,128)(2,1)S(1)}, u32[]{:S(2)}, u32[]{:S(2)}) %collective-permute-start.11) | collective-permute-done | bytes 344096 | tf_op jit(solution)/shard_map/ppermute | solution.py:93
  157.9 2.7 collective-permute-done.12.refs_3_
  160.6 7.4 %unroute.1 = (bf16[768,512]{1,0:T(8,128)(2,1)}, f32[512,768]{1,0:T(8,128)}, bf16[512,768]{1,0:T(8,128)(2,1)}, f32[512,128]{1,0:T(8,128)}, f32[1,768]{1,0:T(1,128)}) custom-call(s32[5]{0:T(128)S(1)} %stack.19.meta, bf16[192,896]{1,0:T(8,128)(2,1)S(1)} %copy-done.7, bf16[192,896]{1,0:T(8,128)(2,1)S(1)} %collective-permute-done.10.refs_1_, ...), custom_call_target="tpu_custom_call" | custom-call | flops 109999996928 | bytes 65536 | tf_op jit(solution)/shard_map/unroute/pallas_call | solution.py:73
  168.0 3.5 %all-to-all-start.2 = ((bf16[4,192,512]{2,1,0:T(8,128)(2,1)}), bf16[4,192,512]{2,1,0:T(8,128)(2,1)S(1)}, u32[]{:S(2)}, u32[]{:S(2)}) async-start(bf16[4,192,512]{2,1,0:T(8,128)(2,1)} %bitcast.50), calls=%async_computation.2 | async-start | bytes 1572864 | tf_op jit(solution)/shard_map/all_to_all | solution.py:106
  171.5 4.0 %dense.1 = (bf16[16,24,896]{2,1,0:T(8,128)(2,1)}, bf16[16,24,896]{2,1,0:T(8,128)(2,1)}) custom-call(s32[5]{0:T(128)S(1)} %stack.19.meta, bf16[768,512]{1,0:T(8,128)(2,1)S(1)} %bitcast.39, bf16[512,768]{1,0:T(8,128)(2,1)} %get-tuple-element.134.dlow, bf16[512,768]{1,0:T(8,128)(2,1)} %get-tuple-element.135.moe, f32[512,128]{1,0:T(8,128)} %get-tuple-element.136.dlogits, ...), custom_call_target="tpu_custom_call" | custom-call | flops 110000000 | bytes 65536 | tf_op jit(solution)/shard_map/dense/pallas_call | solution.py:73
  175.5 7.3 %all-to-all-done.2.refs_0_ = bf16[4,192,512]{2,1,0:T(8,128)(2,1)S(1)} async-done(((bf16[4,192,512]{2,1,0:T(8,128)(2,1)}), bf16[4,192,512]{2,1,0:T(8,128)(2,1)S(1)}, u32[]{:S(2)}, u32[]{:S(2)}) %all-to-all-start.2) | async-done | bytes 786464 | tf_op jit(solution)/shard_map/all_to_all | solution.py:106
  182.8 3.5 %all-to-all-start.3 = ((bf16[4,192,768]{2,1,0:T(8,128)(2,1)}), bf16[4,192,768]{2,1,0:T(8,128)(2,1)S(1)}, u32[]{:S(2)}, u32[]{:S(2)}) async-start(bf16[4,192,768]{2,1,0:T(8,128)(2,1)} %get-tuple-element.133), calls=%async_computation.3 | async-start | bytes 2359296 | tf_op jit(solution)/shard_map/all_to_all | solution.py:106
  186.3 27.1 %attend_back.1 = (bf16[576,512]{1,0:T(8,128)(2,1)}, bf16[576,512]{1,0:T(8,128)(2,1)}, bf16[576,512]{1,0:T(8,128)(2,1)}, bf16[576,512]{1,0:T(8,128)(2,1)}, bf16[1...) custom-call(s32[5]{0:T(128)S(1)} %stack.19.meta, bf16[4,576,512]{2,1,0:T(8,128)(2,1)} %get-tuple-element.142.qkv, ...), custom_call_target="tpu_custom_call" | custom-call | flops 13200000000 | bytes 65536 | tf_op jit(solution)/shard_map/attend_back/pallas_call | solution.py:73
  213.5 3.6 %collective-permute-start.18 = (bf16[576,512]{1,0:T(8,128)(2,1)}, bf16[576,512]{1,0:T(8,128)(2,1)S(1)}, u32[]{:S(2)}, u32[]{:S(2)}) collective-permute-start(bf16[576,512]{1,0:T(8,128)(2,1)} %get-tuple-element.150), channel_id=1, source_target_pairs={{0,64},{32,96},{64,0},{96,32},{1,65},{33,97},{65,1},{97,33},{2,66}... | collective-permute-start | bytes 1769480 | tf_op jit(solution)/shard_map/ppermute | solution.py:93
  217.0 0.6 collective-permute-start.17
  217.6 0.6 collective-permute-start.19
  218.4 2.1 collective-permute-done.16.heads_b
  220.5 1.0 copy-done
  221.5 2.7 add_dense.1.refs_1_
  224.2 9.0 %all-to-all-start.4 = ((bf16[16,24,1536]{2,1,0:T(8,128)(2,1)}), bf16[16,24,1536]{2,1,0:T(8,128)(2,1)S(1)}, u32[]{:S(2)}, u32[]{:S(2)}) async-start(bf16[16,24,1536]{2,1,0:T(8,128)(2,1)} %add_dense.1.refs_1_), calls=%async_computation.4 | async-start | bytes 2359296 | tf_op jit(solution)/shard_map/all_to_all | solution.py:106
  233.2 3.5 %mixed.1.refs_8_ = bf16[512,768]{1,0:T(8,128)(2,1)} custom-call(s32[5]{0:T(128)S(1)} %stack.19.meta, f32[512,768]{1,0:T(8,128)} %get-tuple-element.112.partial, bf16[4,192,512]{2,1,0:T(8,128)(2,1)} %get-tuple-element.107.slots.refs_6_, bf16[4,192,768]{2,1,0:T(8,128)(2,1)S(1)} %copy-done.1, bf16[16,24,1536]{2,1,0:T(8,128)(2,1)} %add_dense.1.refs_1_), custom_call_target="tpu_custom_call" | custom-call | flops 110000000 | bytes 65536 | tf_op jit(solution)/shard_map/mixed/pallas_call | solution.py:73
  236.7 1.4 collective-permute-start.20
  238.2 2.7 collective-permute-start.21
  240.8 0.6 collective-permute-start.22
  241.4 1.2 collective-permute-done.17.refs_1_
  242.7 1.1 copy-done.9
  243.8 6.8 %finish.1.refs_0_ = bf16[512,768]{1,0:T(8,128)(2,1)} custom-call(s32[5]{0:T(128)S(1)} %stack.19.meta, bf16[576,512]{1,0:T(8,128)(2,1)S(1)} %copy-done.9, bf16[576,512]{1,0:T(8,128)(2,1)} %collective-permute-done.17.refs_1_, bf16[576,512]{1,0:T(8,128)(2,1)S(1)} %collective-permute-done.18.refs_2_, bf16[576,512]{1,0:T(8,128)(2,1)} %collective-permute-done.19.refs_3_, ...), custom_call_target="tpu_custom_call" | custom-call | flops 11000000512 | bytes 65536 | tf_op jit(solution)/shard_map/finish/pallas_call | solution.py:73
  250.6 2.2 all-to-all-done.4.pieces
  252.8 1.4 add_pieces.1.refs_0_
  254.2 2.6 collective-permute-done.22.refs_3_
  256.8 2.1 collective-permute-start.24
  258.8 2.6 collective-permute-start.25
  261.5 2.1 gather.1
  263.6 1.0 collective-permute-done.25.refs_3_
  264.6 0.9 copy-done.2
  265.5 1.9 gather_dense.1
  (57 shorter events, 1.8 us)
Async XLA Ops:
  7.2 76.2 %all-gather.3.cloned.1.call-start = ((), (), s32[]{:S(2)}) async-start(), calls=%async_computation.6 | async-start | bytes 11354112 | tf_op jit(solution)/shard_map/all_gather | solution.py:982
  8.0 3.3 %copy-start.5 = (bf16[1,512,768]{2,1,0:T(8,128)(2,1)S(1)}, bf16[1,512,768]{2,1,0:T(8,128)(2,1)}, u32[]{:S(2)}) copy-start(bf16[1,512,768]{2,1,0:T(8,128)(2,1)} %param.15) | copy-start | bytes 2359300
  11.3 20.5 %collective-permute-start = (bf16[512,768]{1,0:T(8,128)(2,1)S(1)}, bf16[512,768]{1,0:T(8,128)(2,1)S(1)}, u32[]{:S(2)}, u32[]{:S(2)}) collective-permute-start(bf16[512,768]{1,0:T(8,128)(2,1)S(1)} %bitcast.44), channel_id=1, source_target_pairs={{0,32},{32,64},{64,96},{96,0},{1,33},{33,65},{65,97},{97,1},{2,34}... | collective-permute-start | bytes 2359304 | tf_op jit(solution)/shard_map/ppermute | solution.py:88
  12.9 20.1 %collective-permute-start.1 = (bf16[512,768]{1,0:T(8,128)(2,1)S(1)}, bf16[512,768]{1,0:T(8,128)(2,1)S(1)}, u32[]{:S(2)}, u32[]{:S(2)}) collective-permute-start(bf16[512,768]{1,0:T(8,128)(2,1)S(1)} %bitcast.45), channel_id=1, source_target_pairs={{0,96},{32,0},{64,32},{96,64},{1,97},{33,1},{65,33},{97,65},{2,98}... | collective-permute-start | bytes 2359304 | tf_op jit(solution)/shard_map/ppermute | solution.py:88
  14.6 32.2 %all-to-all-start = ((bf16[32,24,640]{2,1,0:T(8,128)(2,1)}), bf16[32,24,640]{2,1,0:T(8,128)(2,1)S(1)}, u32[]{:S(2)}, u32[]{:S(2)}) async-start(bf16[32,24,640]{2,1,0:T(8,128)(2,1)} %get-tuple-element.97), calls=%async_computation | async-start | bytes 1966080 | tf_op jit(solution)/shard_map/all_to_all | solution.py:106
  32.5 14.5 %collective-permute-start.2 = (bf16[256,768]{1,0:T(8,128)(2,1)}, bf16[256,768]{1,0:T(8,128)(2,1)}, u32[]{:S(2)}, u32[]{:S(2)}) collective-permute-start(bf16[256,768]{1,0:T(8,128)(2,1)} %slice.16), channel_id=1, source_target_pairs={{0,32},{32,64},{64,96},{96,0},{1,33},{33,65},{65,97},{97,1},{2,34}... | collective-permute-start | bytes 1179656 | tf_op jit(solution)/shard_map/ppermute | solution.py:88
  33.8 13.3 %collective-permute-start.3 = (bf16[256,768]{1,0:T(8,128)(2,1)}, bf16[256,768]{1,0:T(8,128)(2,1)}, u32[]{:S(2)}, u32[]{:S(2)}) collective-permute-start(bf16[256,768]{1,0:T(8,128)(2,1)} %slice.17), channel_id=1, source_target_pairs={{0,96},{32,0},{64,32},{96,64},{1,97},{33,1},{65,33},{97,65},{2,98}... | collective-permute-start | bytes 1179656 | tf_op jit(solution)/shard_map/ppermute | solution.py:88
  41.9 27.6 %collective-permute-start.4 = (bf16[192,768]{1,0:T(8,128)(2,1)}, bf16[192,768]{1,0:T(8,128)(2,1)}, u32[]{:S(2)}, u32[]{:S(2)}) collective-permute-start(bf16[192,768]{1,0:T(8,128)(2,1)} %get-tuple-element.101), channel_id=1, source_target_pairs={{0,32},{32,0},{64,96},{96,64},{1,33},{33,1},{65,97},{97,65},{2,34}... | collective-permute-start | bytes 884744 | tf_op jit(solution)/shard_map/ppermute | solution.py:93
  41.9 27.6 %collective-permute-start.5 = (bf16[192,768]{1,0:T(8,128)(2,1)}, bf16[192,768]{1,0:T(8,128)(2,1)}, u32[]{:S(2)}, u32[]{:S(2)}) collective-permute-start(bf16[192,768]{1,0:T(8,128)(2,1)} %get-tuple-element.102), channel_id=1, source_target_pairs={{0,64},{32,96},{64,0},{96,32},{1,65},{33,97},{65,1},{97,33},{2,66}... | collective-permute-start | bytes 884744 | tf_op jit(solution)/shard_map/ppermute | solution.py:93
  43.9 25.7 %collective-permute-start.6 = (bf16[192,768]{1,0:T(8,128)(2,1)}, bf16[192,768]{1,0:T(8,128)(2,1)}, u32[]{:S(2)}, u32[]{:S(2)}) collective-permute-start(bf16[192,768]{1,0:T(8,128)(2,1)} %get-tuple-element.103), channel_id=1, source_target_pairs={{0,96},{32,64},{64,32},{96,0},{1,97},{33,65},{65,33},{97,1},{2,98}... | collective-permute-start | bytes 884744 | tf_op jit(solution)/shard_map/ppermute | solution.py:93
  47.0 6.3 %copy-start.4 = (f32[1,768]{1,0:T(1,128)}, f32[1,768]{1,0:T(1,128)S(1)}, u32[]{:S(2)}) copy-start(f32[1,768]{1,0:T(1,128)S(1)} %reshape.104.refs_6_) | copy-start | bytes 9220
  69.5 13.8 %all-to-all-start.1 = ((bf16[4,192,512]{2,1,0:T(8,128)(2,1)}), bf16[4,192,512]{2,1,0:T(8,128)(2,1)S(1)}, u32[]{:S(2)}, u32[]{:S(2)}) async-start(bf16[4,192,512]{2,1,0:T(8,128)(2,1)} %get-tuple-element.104.refs_1_), calls=%async_computation.1 | async-start | bytes 1572864 | tf_op jit(solution)/shard_map/all_to_all | solution.py:106
  73.1 70.8 %all-gather.5.cloned.1.call-start = ((), (), s32[]{:S(2)}) async-start(), calls=%async_computation.7 | async-start | bytes 3649536 | tf_op jit(solution)/shard_map/all_gather | solution.py:983
  73.9 162.9 %reduce-scatter.4.cloned.1.call-start = ((), (), s32[]{:S(2)}) async-start(), calls=%async_computation.8 | async-start | bytes 5013504
  89.3 13.6 %collective-permute-start.7 = (bf16[192,896]{1,0:T(8,128)(2,1)}, bf16[192,896]{1,0:T(8,128)(2,1)S(1)}, u32[]{:S(2)}, u32[]{:S(2)}) collective-permute-start(bf16[192,896]{1,0:T(8,128)(2,1)} %get-tuple-element.114), channel_id=1, source_target_pairs={{0,32},{32,0},{64,96},{96,64},{1,33},{33,1},{65,97},{97,65},{2,34}... | collective-permute-start | bytes 1032200 | tf_op jit(solution)/shard_map/ppermute | solution.py:93
  89.8 14.4 %collective-permute-start.8 = (bf16[192,896]{1,0:T(8,128)(2,1)}, bf16[192,896]{1,0:T(8,128)(2,1)S(1)}, u32[]{:S(2)}, u32[]{:S(2)}) collective-permute-start(bf16[192,896]{1,0:T(8,128)(2,1)} %get-tuple-element.115), channel_id=1, source_target_pairs={{0,64},{32,96},{64,0},{96,32},{1,65},{33,97},{65,1},{97,33},{2,66}... | collective-permute-start | bytes 1032200 | tf_op jit(solution)/shard_map/ppermute | solution.py:93
  92.0 14.9 %collective-permute-start.9 = (bf16[192,896]{1,0:T(8,128)(2,1)}, bf16[192,896]{1,0:T(8,128)(2,1)S(1)}, u32[]{:S(2)}, u32[]{:S(2)}) collective-permute-start(bf16[192,896]{1,0:T(8,128)(2,1)} %get-tuple-element.116), channel_id=1, source_target_pairs={{0,96},{32,64},{64,32},{96,0},{1,97},{33,65},{65,33},{97,1},{2,98}... | collective-permute-start | bytes 1032200 | tf_op jit(solution)/shard_map/ppermute | solution.py:93
  98.0 9.6 %copy-start.6 = (bf16[192,768]{1,0:T(8,128)(2,1)S(1)}, bf16[192,768]{1,0:T(8,128)(2,1)}, u32[]{:S(2)}) copy-start(bf16[192,768]{1,0:T(8,128)(2,1)} %get-tuple-element.117.refs_4_) | copy-start | bytes 884740
  98.0 9.6 %copy-start.8 = (bf16[192,896]{1,0:T(8,128)(2,1)S(1)}, bf16[192,896]{1,0:T(8,128)(2,1)}, u32[]{:S(2)}) copy-start(bf16[192,896]{1,0:T(8,128)(2,1)} %get-tuple-element.113.refs_0_) | copy-start | bytes 1032196
  104.2 2.6 copy-start.10
  106.8 0.7 copy-start.11
  138.4 8.3 %collective-permute-start.13 = (bf16[4,2,16,24,512]{4,3,2,1,0:T(8,128)(2,1)}, bf16[4,2,16,24,512]{4,3,2,1,0:T(8,128)(2,1)}, u32[]{:S(2)}, u32[]{:S(2)}) collective-permute-start(bf16[4,2,16,24,512]{4,3,2,1,0:T(8,128)(2,1)} %get-tuple-element.127), channel_id=1, source_target_pairs={{0,1},{1,0},{2,3},{3,2},{4,5},{5,4},{6,7},{7,6},{8,9},{9,8},{10,11... | collective-permute-start | bytes 9437192 | tf_op jit(solution)/shard_map/ppermute | solution.py:93
  138.5 7.7 %collective-permute-start.14 = (bf16[16,64,768]{2,1,0:T(8,128)(2,1)}, bf16[16,64,768]{2,1,0:T(8,128)(2,1)S(1)}, u32[]{:S(2)}, u32[]{:S(2)}) collective-permute-start(bf16[16,64,768]{2,1,0:T(8,128)(2,1)} %get-tuple-element.129), channel_id=1, source_target_pairs={{0,1},{1,0},{2,3},{3,2},{4,5},{5,4},{6,7},{7,6},{8,9},{9,8},{10,11... | collective-permute-start | bytes 4718600 | tf_op jit(solution)/shard_map/ppermute | solution.py:93
  139.0 13.9 %collective-permute-start.10 = (bf16[192,896]{1,0:T(8,128)(2,1)}, bf16[192,896]{1,0:T(8,128)(2,1)S(1)}, u32[]{:S(2)}, u32[]{:S(2)}) collective-permute-start(bf16[192,896]{1,0:T(8,128)(2,1)} %get-tuple-element.123), channel_id=1, source_target_pairs={{0,32},{32,0},{64,96},{96,64},{1,33},{33,1},{65,97},{97,65},{2,34}... | collective-permute-start | bytes 1032200 | tf_op jit(solution)/shard_map/ppermute | solution.py:93
  139.0 18.8 %collective-permute-start.11 = (bf16[192,896]{1,0:T(8,128)(2,1)}, bf16[192,896]{1,0:T(8,128)(2,1)S(1)}, u32[]{:S(2)}, u32[]{:S(2)}) collective-permute-start(bf16[192,896]{1,0:T(8,128)(2,1)} %get-tuple-element.124), channel_id=1, source_target_pairs={{0,64},{32,96},{64,0},{96,32},{1,65},{33,97},{65,1},{97,33},{2,66}... | collective-permute-start | bytes 1032200 | tf_op jit(solution)/shard_map/ppermute | solution.py:93
  142.1 18.4 %collective-permute-start.12 = (bf16[192,896]{1,0:T(8,128)(2,1)}, bf16[192,896]{1,0:T(8,128)(2,1)S(1)}, u32[]{:S(2)}, u32[]{:S(2)}) collective-permute-start(bf16[192,896]{1,0:T(8,128)(2,1)} %get-tuple-element.125), channel_id=1, source_target_pairs={{0,96},{32,64},{64,32},{96,0},{1,97},{33,65},{65,33},{97,1},{2,98}... | collective-permute-start | bytes 1032200 | tf_op jit(solution)/shard_map/ppermute | solution.py:93
  152.9 7.7 %copy-start.7 = (bf16[192,896]{1,0:T(8,128)(2,1)S(1)}, bf16[192,896]{1,0:T(8,128)(2,1)}, u32[]{:S(2)}) copy-start(bf16[192,896]{1,0:T(8,128)(2,1)} %get-tuple-element.122.refs_0_) | copy-start | bytes 1032196
  168.0 14.8 %all-to-all-start.2 = ((bf16[4,192,512]{2,1,0:T(8,128)(2,1)}), bf16[4,192,512]{2,1,0:T(8,128)(2,1)S(1)}, u32[]{:S(2)}, u32[]{:S(2)}) async-start(bf16[4,192,512]{2,1,0:T(8,128)(2,1)} %bitcast.50), calls=%async_computation.2 | async-start | bytes 1572864 | tf_op jit(solution)/shard_map/all_to_all | solution.py:106
  175.5 42.9 %collective-permute-start.15 = (bf16[16,24,896]{2,1,0:T(8,128)(2,1)}, bf16[16,24,896]{2,1,0:T(8,128)(2,1)S(1)}, u32[]{:S(2)}, u32[]{:S(2)}) collective-permute-start(bf16[16,24,896]{2,1,0:T(8,128)(2,1)} %get-tuple-element.141), channel_id=1, source_target_pairs={{0,1},{1,0},{2,3},{3,2},{4,5},{5,4},{6,7},{7,6},{8,9},{9,8},{10,11... | collective-permute-start | bytes 2064392 | tf_op jit(solution)/shard_map/ppermute | solution.py:93
  182.8 37.7 %all-to-all-start.3 = ((bf16[4,192,768]{2,1,0:T(8,128)(2,1)}), bf16[4,192,768]{2,1,0:T(8,128)(2,1)S(1)}, u32[]{:S(2)}, u32[]{:S(2)}) async-start(bf16[4,192,768]{2,1,0:T(8,128)(2,1)} %get-tuple-element.133), calls=%async_computation.3 | async-start | bytes 2359296 | tf_op jit(solution)/shard_map/all_to_all | solution.py:106
  213.5 23.3 %collective-permute-start.18 = (bf16[576,512]{1,0:T(8,128)(2,1)}, bf16[576,512]{1,0:T(8,128)(2,1)S(1)}, u32[]{:S(2)}, u32[]{:S(2)}) collective-permute-start(bf16[576,512]{1,0:T(8,128)(2,1)} %get-tuple-element.150), channel_id=1, source_target_pairs={{0,64},{32,96},{64,0},{96,32},{1,65},{33,97},{65,1},{97,33},{2,66}... | collective-permute-start | bytes 1769480 | tf_op jit(solution)/shard_map/ppermute | solution.py:93
  217.0 25.7 %collective-permute-start.17 = (bf16[576,512]{1,0:T(8,128)(2,1)}, bf16[576,512]{1,0:T(8,128)(2,1)}, u32[]{:S(2)}, u32[]{:S(2)}) collective-permute-start(bf16[576,512]{1,0:T(8,128)(2,1)} %get-tuple-element.149), channel_id=1, source_target_pairs={{0,32},{32,0},{64,96},{96,64},{1,33},{33,1},{65,97},{97,65},{2,34}... | collective-permute-start | bytes 1769480 | tf_op jit(solution)/shard_map/ppermute | solution.py:93
  217.6 25.1 %collective-permute-start.19 = (bf16[576,512]{1,0:T(8,128)(2,1)}, bf16[576,512]{1,0:T(8,128)(2,1)}, u32[]{:S(2)}, u32[]{:S(2)}) collective-permute-start(bf16[576,512]{1,0:T(8,128)(2,1)} %get-tuple-element.152), channel_id=1, source_target_pairs={{0,96},{32,64},{64,32},{96,0},{1,97},{33,65},{65,33},{97,1},{2,98}... | collective-permute-start | bytes 1769480 | tf_op jit(solution)/shard_map/ppermute | solution.py:93
  218.2 2.3 collective-permute-start.16
  220.5 1.0 copy-start
  224.2 9.0 %copy-start.1 = (bf16[4,192,768]{2,1,0:T(8,128)(2,1)S(1)}, bf16[4,192,768]{2,1,0:T(8,128)(2,1)}, u32[]{:S(2)}) copy-start(bf16[4,192,768]{2,1,0:T(8,128)(2,1)} %copy-done) | copy-start | bytes 3538948
  224.2 28.6 %all-to-all-start.4 = ((bf16[16,24,1536]{2,1,0:T(8,128)(2,1)}), bf16[16,24,1536]{2,1,0:T(8,128)(2,1)S(1)}, u32[]{:S(2)}, u32[]{:S(2)}) async-start(bf16[16,24,1536]{2,1,0:T(8,128)(2,1)} %add_dense.1.refs_1_), calls=%async_computation.4 | async-start | bytes 2359296 | tf_op jit(solution)/shard_map/all_to_all | solution.py:106
  236.7 17.4 %collective-permute-start.20 = (bf16[24,6144]{1,0:T(8,128)(2,1)}, bf16[24,6144]{1,0:T(8,128)(2,1)S(1)}, u32[]{:S(2)}, u32[]{:S(2)}) collective-permute-start(bf16[24,6144]{1,0:T(8,128)(2,1)} %reduce-scatter.4.cloned.1.call-done.refs_0_), channel_id=1, source_target_pairs={{0,32},{32,0},{64,96},{96,64},{1,33},{33,1},{65,97},{97,65},{2,34}... | collective-permute-start | bytes 884744 | tf_op jit(solution)/shard_map/ppermute | solution.py:93
  238.2 16.0 %collective-permute-start.21 = (bf16[24,6144]{1,0:T(8,128)(2,1)}, bf16[24,6144]{1,0:T(8,128)(2,1)S(1)}, u32[]{:S(2)}, u32[]{:S(2)}) collective-permute-start(bf16[24,6144]{1,0:T(8,128)(2,1)} %reduce-scatter.4.cloned.1.call-done.refs_0_), channel_id=1, source_target_pairs={{0,64},{32,96},{64,0},{96,32},{1,65},{33,97},{65,1},{97,33},{2,66}... | collective-permute-start | bytes 884744 | tf_op jit(solution)/shard_map/ppermute | solution.py:93
  240.8 15.9 %collective-permute-start.22 = (bf16[24,6144]{1,0:T(8,128)(2,1)}, bf16[24,6144]{1,0:T(8,128)(2,1)S(1)}, u32[]{:S(2)}, u32[]{:S(2)}) collective-permute-start(bf16[24,6144]{1,0:T(8,128)(2,1)} %reduce-scatter.4.cloned.1.call-done.refs_0_), channel_id=1, source_target_pairs={{0,96},{32,64},{64,32},{96,0},{1,97},{33,65},{65,33},{97,1},{2,98}... | collective-permute-start | bytes 884744 | tf_op jit(solution)/shard_map/ppermute | solution.py:93
  242.7 1.1 copy-start.9
  250.6 10.9 %copy-start.3 = (bf16[24,6144]{1,0:T(8,128)(2,1)S(1)}, bf16[24,6144]{1,0:T(8,128)(2,1)}, u32[]{:S(2)}) copy-start(bf16[24,6144]{1,0:T(8,128)(2,1)} %reduce-scatter.4.cloned.1.call-done.refs_0_) | copy-start | bytes 884740
  256.8 6.8 %collective-permute-start.23 = (bf16[24,1536]{1,0:T(8,128)(2,1)}, bf16[24,1536]{1,0:T(8,128)(2,1)S(1)}, u32[]{:S(2)}, u32[]{:S(2)}) collective-permute-start(bf16[24,1536]{1,0:T(8,128)(2,1)} %add_pieces.1.refs_0_), channel_id=1, source_target_pairs={{0,32},{32,0},{64,96},{96,64},{1,33},{33,1},{65,97},{97,65},{2,34}... | collective-permute-start | bytes 221192 | tf_op jit(solution)/shard_map/ppermute | solution.py:93
  256.8 6.8 %collective-permute-start.24 = (bf16[24,1536]{1,0:T(8,128)(2,1)}, bf16[24,1536]{1,0:T(8,128)(2,1)S(1)}, u32[]{:S(2)}, u32[]{:S(2)}) collective-permute-start(bf16[24,1536]{1,0:T(8,128)(2,1)} %add_pieces.1.refs_0_), channel_id=1, source_target_pairs={{0,64},{32,96},{64,0},{96,32},{1,65},{33,97},{65,1},{97,33},{2,66}... | collective-permute-start | bytes 221192 | tf_op jit(solution)/shard_map/ppermute | solution.py:93
  258.8 5.8 %collective-permute-start.25 = (bf16[24,1536]{1,0:T(8,128)(2,1)}, bf16[24,1536]{1,0:T(8,128)(2,1)S(1)}, u32[]{:S(2)}, u32[]{:S(2)}) collective-permute-start(bf16[24,1536]{1,0:T(8,128)(2,1)} %add_pieces.1.refs_0_), channel_id=1, source_target_pairs={{0,96},{32,64},{64,32},{96,0},{1,97},{33,65},{65,33},{97,1},{2,98}... | collective-permute-start | bytes 221192 | tf_op jit(solution)/shard_map/ppermute | solution.py:93
  264.6 0.9 copy-start.2
Sparse Core Ops, SparseCore 0:
  11.4 66.9 all-gather.2
  80.7 45.3 all-gather.4
  153.0 80.2 reduce-scatter.3
